TPU v7x, 32 devices: a whole 2x2x4 slice. The times are simulated.
32 devices in a mesh: group: 2 (over x), member: 8 (over z, y), role: 2 (over core).
Axes of the slice: x: 2, y: 2, z: 4, core: 2. Of those that a mesh axis runs over, the one named last changes fastest.
Arguments:
- frames: bfloat16 [16, 2, 256, 1024], P(('group', 'member'), 'role'), may hold values from -6 to 6
- cotangent: bfloat16 [16, 2, 256, 1024], P(('group', 'member'), 'role'), may hold values from -6 to 6
- w_qkv: bfloat16 [1024, 3072], replicated, may hold values from -0.1875 to 0.1875
- w_out: bfloat16 [1024, 1024], replicated, may hold values from -1 to 1
- w_up: bfloat16 [1024, 4096], replicated, may hold values from -0.1875 to 0.1875
- w_down: bfloat16 [4096, 1024], replicated, may hold values from -0.09375 to 0.09375
- gains: bfloat16 [7, 2, 1024], replicated, may hold values from 0.25 to 1.75
- shifts: bfloat16 [7, 2, 1024], replicated, may hold values from -3 to 3
- prompt_len: int32 [16], P(('group', 'member')), may hold values from 64 to 256, as said below
- section: int32 [16], P(('group', 'member')), may hold values from 0 to 6
Outputs:
- output: bfloat16 [16, 2, 256, 1024], P(('group', 'member'), 'role')
- input_grad: float32 [16, 2, 256, 1024], P(('group', 'member'), 'role')
- grad_params: float32 [12611584], P(('member', 'role'))
Inputs may be any that keep to these rules, and one draw needn't show every extreme that they name: `prompt_len`: some utterance has a prompt of 256 frames.
All inputs are finite; a program needn't handle non-finite values.
Results may differ from a plain program's by a relative error of at most 0.01.
Values may be sent and summed in bfloat16 or wider, within the bound.
No kernel may reach another device: no remote copies, remote signals or barrier semaphores. Data moves between devices by JAX's collectives and lax.ppermute only.
A program may use at most 256 MiB of HBM per device.

v0:
```python
import jax
import jax.numpy as jnp
from jax import lax
from jax.sharding import PartitionSpec as P

HEADS = 16


def from_behind(value, axis, steps):
    count = lax.axis_size(axis)
    leading, last = (max(0, -steps), min(count, count - steps))
    return lax.ppermute(value, axis, [(source, source + steps) for source in range(leading, last)])


def normalize(values):
    center = values - jnp.mean(values, axis=-1, keepdims=True)
    spread = jnp.mean(center * center, axis=-1, keepdims=True)
    return center * lax.rsqrt(spread + 1e-05)


def affine_norm(values, gain_row, shift_row):
    return normalize(values) * gain_row + shift_row


def erf_gelu(values):
    return jax.nn.gelu(values, approximate=False)


def masked_scores(query_heads, key_heads, allowed, score_scale):
    raw_scores = (
        jnp.einsum("ihd,jhd->hij", query_heads, key_heads, preferred_element_type=jnp.float32)
        * score_scale
    )
    return jnp.where(allowed[None, None, :], raw_scores, -1e30)


def local(frames, cotangent, w_qkv, w_out, w_up, w_down, gains, shifts, prompt_len, section):
    frame_rows = frames[0, 0].astype(jnp.float32)
    frame_count = frame_rows.shape[0]
    model_width = frame_rows.shape[1]
    head_size = model_width // HEADS
    score_scale = head_size ** (-0.5)
    on_target = lax.axis_index("role") == 1
    select = (jnp.arange(gains.shape[0], dtype=jnp.int32) == section[0]).astype(jnp.float32)
    gain_rows = jnp.einsum("s,sjd->jd", select, gains.astype(jnp.float32))
    shift_rows = jnp.einsum("s,sjd->jd", select, shifts.astype(jnp.float32))
    hidden_one, norm_one = jax.vjp(affine_norm, frame_rows, gain_rows[0], shift_rows[0])
    hidden_one = hidden_one.astype(jnp.bfloat16)
    qkv_all = jnp.dot(hidden_one, w_qkv, preferred_element_type=jnp.float32).astype(jnp.bfloat16)
    far_pairs = from_behind(qkv_all[:, model_width:], "role", 1)
    key_pairs = jnp.concatenate([far_pairs, qkv_all[:, model_width:]], axis=0)
    key_slots = jnp.arange(frame_count, dtype=jnp.int32)
    live_keys = key_slots < prompt_len[0]
    allowed = jnp.concatenate([live_keys & on_target, live_keys | on_target])
    query_heads = qkv_all[:, :model_width].reshape(frame_count, HEADS, head_size)
    key_heads = key_pairs[:, :model_width].reshape(2 * frame_count, HEADS, head_size)
    value_heads = key_pairs[:, model_width:].reshape(2 * frame_count, HEADS, head_size)
    scores = masked_scores(query_heads, key_heads, allowed, score_scale)
    row_max = jnp.max(scores, axis=-1, keepdims=True)
    exponent = jnp.exp(scores - row_max)
    row_sum = jnp.sum(exponent, axis=-1, keepdims=True)
    log_total = row_max + jnp.log(row_sum)
    prob_low = (exponent / row_sum).astype(jnp.bfloat16)
    attended = jnp.einsum("hij,jhd->ihd", prob_low, value_heads, preferred_element_type=jnp.float32)
    attended = attended.reshape(frame_count, model_width).astype(jnp.bfloat16)
    residual = frame_rows + jnp.dot(attended, w_out, preferred_element_type=jnp.float32)
    hidden_two, norm_two = jax.vjp(affine_norm, residual, gain_rows[1], shift_rows[1])
    hidden_two = hidden_two.astype(jnp.bfloat16)
    upward = jnp.dot(hidden_two, w_up, preferred_element_type=jnp.float32)
    active, gelu_back = jax.vjp(erf_gelu, upward)
    active = active.astype(jnp.bfloat16)
    output = (residual + jnp.dot(active, w_down, preferred_element_type=jnp.float32)).astype(
        jnp.bfloat16
    )
    grad_y = cotangent[0, 0]
    grad_down = jnp.einsum("rf,rd->fd", active, grad_y, preferred_element_type=jnp.float32)
    grad_active = jnp.einsum("rd,fd->rf", grad_y, w_down, preferred_element_type=jnp.float32)
    grad_upward = gelu_back(grad_active)[0].astype(jnp.bfloat16)
    grad_up = jnp.einsum("rd,rf->df", hidden_two, grad_upward, preferred_element_type=jnp.float32)
    grad_hidden_two = jnp.einsum("rf,df->rd", grad_upward, w_up, preferred_element_type=jnp.float32)
    grad_resid_norm, grad_gain_two, grad_shift_two = norm_two(grad_hidden_two)
    grad_residual = grad_y.astype(jnp.float32) + grad_resid_norm
    grad_branch = grad_residual.astype(jnp.bfloat16)
    grad_out = jnp.einsum("ri,ro->io", attended, grad_branch, preferred_element_type=jnp.float32)
    grad_attended = jnp.einsum("ro,io->ri", grad_branch, w_out, preferred_element_type=jnp.float32)
    grad_attended = grad_attended.astype(jnp.bfloat16).reshape(frame_count, HEADS, head_size)
    scores = masked_scores(query_heads, key_heads, allowed, score_scale)
    prob_full = jnp.exp(scores - log_total)
    prob_again = prob_full.astype(jnp.bfloat16)
    grad_values = jnp.einsum(
        "hij,ihd->jhd", prob_again, grad_attended, preferred_element_type=jnp.float32
    )
    grad_probs = jnp.einsum(
        "ihd,jhd->hij", grad_attended, value_heads, preferred_element_type=jnp.float32
    )
    row_delta = jnp.sum(prob_full * grad_probs, axis=-1, keepdims=True)
    grad_scores = (prob_full * (grad_probs - row_delta)).astype(jnp.bfloat16)
    grad_queries = (
        jnp.einsum("hij,jhd->ihd", grad_scores, key_heads, preferred_element_type=jnp.float32)
        * score_scale
    )
    grad_keys = (
        jnp.einsum("hij,ihd->jhd", grad_scores, query_heads, preferred_element_type=jnp.float32)
        * score_scale
    )
    grad_pairs = jnp.concatenate(
        [
            grad_keys.reshape(2 * frame_count, model_width),
            grad_values.reshape(2 * frame_count, model_width),
        ],
        axis=1,
    )
    returned = from_behind(grad_pairs[:frame_count].astype(jnp.bfloat16), "role", -1).astype(
        jnp.float32
    )
    grad_qkv = jnp.concatenate(
        [grad_queries.reshape(frame_count, model_width), grad_pairs[frame_count:] + returned],
        axis=1,
    ).astype(jnp.bfloat16)
    grad_qkv_w = jnp.einsum("rd,re->de", hidden_one, grad_qkv, preferred_element_type=jnp.float32)
    grad_hidden_one = jnp.einsum("re,de->rd", grad_qkv, w_qkv, preferred_element_type=jnp.float32)
    grad_frame_norm, grad_gain_one, grad_shift_one = norm_one(grad_hidden_one)
    input_grad = grad_residual + grad_frame_norm
    grad_gains = select[:, None, None] * jnp.stack([grad_gain_one, grad_gain_two])[None]
    grad_shifts = select[:, None, None] * jnp.stack([grad_shift_one, grad_shift_two])[None]
    flat_grads = jnp.concatenate(
        [
            grad_qkv_w.reshape(-1),
            grad_out.reshape(-1),
            grad_up.reshape(-1),
            grad_down.reshape(-1),
            grad_gains.reshape(-1),
            grad_shifts.reshape(-1),
        ]
    )
    inner_count = lax.axis_size("member") * lax.axis_size("role")
    blocks = flat_grads.reshape(inner_count, -1)
    blocks = lax.all_to_all(blocks, ("member", "role"), split_axis=0, concat_axis=0, tiled=True)
    shard_sum = jnp.sum(blocks, axis=0)
    shard_sum = lax.psum(shard_sum, "group")
    return (output[None, None], input_grad[None, None], shard_sum)


def solution(mesh):
    placed = (
        P(("group", "member"), "role", None, None),
        P(("group", "member"), "role", None, None),
        P(),
        P(),
        P(),
        P(),
        P(),
        P(),
        P(("group", "member")),
        P(("group", "member")),
    )
    return jax.shard_map(
        local,
        mesh=mesh,
        in_specs=placed,
        out_specs=(
            P(("group", "member"), "role", None, None),
            P(("group", "member"), "role", None, None),
            P(("member", "role")),
        ),
        check_vma=False,
    )
```

profile of v0, /device:TPU:1, one launch (start us, length us, event | category | flops | bytes accessed | tf_op | source)
XLA Modules:
  0.0 1610.3 jit_solution(3040594344153046077)
XLA Ops:
  12.4 4.9 convolution_convert_fusion
  20.3 2.1 copy.30
  22.4 2.7 pad_maximum_fusion.2
  25.1 2.3 copy.29
  28.9 3.0 fusion.12
  31.9 2.1 fusion
  34.0 2.1 copy-done.2
  36.1 2.8 fusion.23
  40.1 16.1 %multiply_convert_fusion.1 = (bf16[256,4096]{1,0:T(8,128)(2,1)}, f32[256,4096]{1,0:T(8,128)}, f32[256,4096]{1,0:T(8,128)}) fusion(bf16[1024,4096]{1,0:T(8,128)(2,1)S(1)} %bitcast.185, f32[256,1024]{1,0:T(8,128)S(1)} %get-tuple-element.25, f32[1024]{0:T(1024)S(1)} %bitcast.169, f32[1024]{0:T(1024)S(1)} %bitcast.163, f32[256]{0:T(256)S(1)} %fusion.50, ...), kind=kOutput, calls=%fused_computation.18 | convolution fusion | flops 2216951808 | bytes 19933184 | tf_op jit(solution)/shard_map/dot_general | solution.py:69
  56.3 11.7 add_convert_fusion
  68.0 2.7 multiply_reduce_fusion.1
  76.0 6.0 multiply_reduce_fusion
  82.0 4.6 fusion.3
  86.5 2.7 convolution_bitcast_fusion.3
  89.2 2.5 multiply_convert_fusion
  92.8 5.3 collective-permute-start.1
  98.1 3.0 copy.40
  101.1 2.6 convolution_bitcast_fusion.1
  103.6 7.1 copy.41
  110.8 2.4 convolution_bitcast_fusion
  113.2 8.1 copy.42
  126.4 6.6 convolution_bitcast_fusion.2
  133.0 12.1 copy.39
  145.0 11.2 constant_dynamic-update-slice_fusion.5
  157.0 2.4 constant_dynamic-update-slice_fusion.4
  161.8 8.4 constant_dynamic-update-slice_fusion.3
  172.3 6.0 constant_dynamic-update-slice_fusion.2
  179.6 1094.5 %all_to_all.9 = f32[16,1,788224]{2,1,0:T(1,128)} all-to-all(f32[16,1,788224]{2,1,0:T(1,128)} %bitcast.138), channel_id=1, replica_groups=mesh['group'=2,'member'=8,'role'=2] {'member','role'}, dimensions={0} | all-to-all | bytes 100892672 | tf_op jit(solution)/shard_map/all_to_all | solution.py:138
  1274.1 238.7 %reduce_sum.155 = f32[788224]{0:T(1024)} reduce(f32[16,1,788224]{2,1,0:T(1,128)} %all_to_all.9, f32[]{:T(128)} %constant.39.clone.1), dimensions={0,1}, to_apply=%region_15.16 | reduce | flops 11823360 | bytes 53599236 | tf_op jit(solution)/shard_map/reduce_sum | solution.py:139
  1512.8 7.3 fusion.25
  1521.6 77.9 %all-reduce.2.cloned.1.call-done = f32[788224]{0:T(1024)} async-done(((f32[788224]{0:T(1024)}), f32[788224]{0:T(1024)}) %all-reduce.2.cloned.1.call-update) | async-done | bytes 3152912 | tf_op jit(solution)/shard_map/psum | solution.py:140
  1599.5 3.8 copy.61
  (134 shorter events, 28.6 us)
Async XLA Ops:
  7.2 31.8 %copy-start = (bf16[1024,1024]{1,0:T(8,128)(2,1)S(1)}, bf16[1024,1024]{1,0:T(8,128)(2,1)}, u32[]{:S(2)}) copy-start(bf16[1024,1024]{1,0:T(8,128)(2,1)} %param.13) | copy-start | bytes 6291460
  7.2 1592.3 %all-reduce.2.cloned.1.call-start = ((), (), s32[]{:S(2)}) async-start(), calls=%async_computation.1 | async-start | bytes 6307840 | tf_op jit(solution)/shard_map/psum | solution.py:140
  17.3 5.1 collective-permute-start
  31.9 8.2 slice-start.10
  39.0 17.3 %copy-start.18 = (bf16[16,64,256]{2,1,0:T(8,128)(2,1)}, bf16[16,64,256]{2,1,0:T(8,128)(2,1)S(1)}, u32[]{:S(2)}) copy-start(bf16[16,64,256]{2,1,0:T(8,128)(2,1)S(1)} %fusion.23) | copy-start | bytes 1572868
  39.8 30.9 %copy-start.4 = (f32[256,1024]{1,0:T(8,128)}, f32[256,1024]{1,0:T(8,128)S(1)}, u32[]{:S(2)}) copy-start(f32[256,1024]{1,0:T(8,128)S(1)} %get-tuple-element.25) | copy-start | bytes 3145732
  40.1 16.2 %copy-start.13 = (bf16[1,1,256,1024]{3,2,1,0:T(8,128)(2,1)S(1)}, bf16[1,1,256,1024]{3,2,1,0:T(8,128)(2,1)}, u32[]{:S(2)}) copy-start(bf16[1,1,256,1024]{3,2,1,0:T(8,128)(2,1)} %param.11) | copy-start | bytes 1572868
  75.9 13.3 slice-start
  76.0 13.3 slice-start.1
  92.6 5.5 copy-start.8
  92.8 8.3 copy-start.5
  92.8 8.3 copy-start.22
  92.8 29.9 %collective-permute-start.1 = (bf16[256,2048]{0,1:T(8,128)(2,1)S(1)}, bf16[256,2048]{0,1:T(8,128)(2,1)}, u32[]{:S(2)}, u32[]{:S(2)}) collective-permute-start(bf16[256,2048]{0,1:T(8,128)(2,1)S(1)} %fusion.16), channel_id=1, source_target_pairs={{1,0},{3,2},{5,4},{7,6},{9,8},{11,10},{13,12},{15,14},{17,16},{19,... | collective-permute-start | bytes 3145736 | tf_op jit(solution)/shard_map/ppermute | solution.py:12
  103.6 7.1 copy-start.20
  110.8 13.5 slice-start.12
  113.2 8.1 copy-start.12
  113.2 11.1 slice-start.13
  126.3 29.9 %copy-start.15 = (f32[256,1024]{1,0:T(8,128)}, f32[256,1024]{1,0:T(8,128)S(1)}, u32[]{:S(2)}) copy-start(f32[256,1024]{1,0:T(8,128)S(1)} %get-tuple-element.30) | copy-start | bytes 3145732
  145.0 11.9 copy-start.7
  145.0 14.3 slice-start.2
  145.0 14.3 slice-start.3
  145.0 15.4 slice-start.4
  156.2 5.6 slice-start.5
  156.9 13.3 slice-start.6
  161.8 8.4 slice-start.7
  161.8 8.7 slice-start.8
  161.8 10.5 slice-start.9
  1274.1 238.7 %copy-start.6 = (f32[256,1024]{1,0:T(8,128)S(1)}, f32[256,1024]{1,0:T(8,128)}, u32[]{:S(2)}) copy-start(f32[256,1024]{1,0:T(8,128)} %copy-done.4) | copy-start | bytes 3145732
  1512.8 7.3 copy-start.10
  1512.8 7.3 copy-start.16
  1512.8 7.3 copy-start.26
  1520.1 83.1 %copy-start.1 = (bf16[1024,1024]{1,0:T(8,128)(2,1)S(1)}, bf16[1024,1024]{1,0:T(8,128)(2,1)}, u32[]{:S(2)}) copy-start(bf16[1024,1024]{1,0:T(8,128)(2,1)} %param.13) | copy-start | bytes 6291460
  (12 other events, 35.7 us)
Sparse Core Ops, SparseCore 0:
  1512.9 86.5 all-reduce.1
where the time goes:
time: 1610 us
  blocking collectives  1090 us (68%)
  other arithmetic  253 us (16%)
  matrix products  81.6 us (5%)
  local copies, waits for them, and re-layouts  79.9 us (5%)
  waiting for transfers between devices  77.9 us (5%)
  between operations  16.3 us (1%)
    all_to_all x1, blocking collectives, local(): lax.all_to_all(blocks, ('member', 'role'), split_axis=0, concat_axis=0, t...  1090 us
    reduce_sum x1, other arithmetic, local(): shard_sum = jnp.sum(blocks, axis=0)  239 us
    psum x1, waiting for transfers between devices, local(): shard_sum = lax.psum(shard_sum, 'group')  77.9 us
    unnamed x94, local copies, waits for them, and re-layouts  71.3 us
  transfers between devices with their start and end apart: 3, of which 1 were waited for; matrix products, arithmetic and copies ran while one was open for 2% of the time, Pallas kernels for 0%

commit v1 on v0

v1 whole, which is shorter than its diff:
```python
import functools

import jax
import jax.numpy as jnp
import numpy as np
from jax import lax
from jax.experimental import pallas as pl
from jax.experimental.pallas import tpu as pltpu
from jax.sharding import PartitionSpec as P

HEADS = 16
LANE = 128
HEAD = 64
F32 = jnp.float32
BF16 = jnp.bfloat16


def dot(left, right, dims):
    return lax.dot_general(left, right, (dims, ((), ())), preferred_element_type=F32)


def mm(left, right):
    return dot(left, right, ((1,), (0,)))


def mm_nt(left, right):
    return dot(left, right, ((1,), (1,)))


def mm_tn(left, right):
    return dot(left, right, ((0,), (0,)))


def swap(value, axis, distance=1):
    count = lax.axis_size(axis)
    return lax.ppermute(value, axis, [(i, i ^ distance) for i in range(count)])


def norm_stats(values):
    center = values - jnp.mean(values, axis=-1, keepdims=True)
    rstd = lax.rsqrt(jnp.mean(center * center, axis=-1, keepdims=True) + 1e-05)
    return center * rstd, rstd


def norm_back(unit, rstd, gain, grad):
    grad_unit = grad * gain
    inner = grad_unit - jnp.mean(grad_unit, axis=-1, keepdims=True)
    return rstd * (inner - unit * jnp.mean(grad_unit * unit, axis=-1, keepdims=True))


def full(shape, dtype):
    return jax.ShapeDtypeStruct(shape, dtype)


def params(mib):
    return pltpu.CompilerParams(vmem_limit_bytes=mib * 2**20)


def cost(flops, moved):
    return pl.CostEstimate(flops=int(flops), bytes_accessed=int(moved), transcendentals=0)


HBM = pl.BlockSpec(memory_space=pl.ANY)
SMEM = pl.BlockSpec(memory_space=pltpu.SMEM)
VMEM = pl.BlockSpec(memory_space=pltpu.VMEM)


def copy_all(pairs, sems):
    copies = [pltpu.make_async_copy(source, target, sems.at[i]) for i, (source, target) in enumerate(pairs)]
    for each in copies:
        each.start()
    return copies


def head_masks(dtype, scale):
    lane = lax.broadcasted_iota(jnp.int32, (1, LANE), 1)
    return [jnp.where(lane // HEAD == h, scale, 0.0).astype(dtype) for h in range(2)]


def live_scores(key, query, length):
    scores = mm_nt(key, query)
    return jnp.where(lax.broadcasted_iota(jnp.int32, scores.shape, 0) < length, scores, -1e30)


def attend_kernel(scalars, x_ref, gs_ref, w_qkv, w_out, ht_ref, qkv_ref, att_ref, part_ref, lse_ref, w_buf, o_buf, h_buf, sems):
    role, length = scalars[0], scalars[1]
    width, half = w_out.shape[1], w_out.shape[0] // 2
    rows = x_ref.shape[0] // 2
    col = pl.multiple_of(role * half, LANE)
    copies = copy_all(
        [(w_qkv.at[:, pl.ds(i * width + col, half)], w_buf.at[:, pl.ds(i * half, half)]) for i in range(3)]
        + [(w_out.at[pl.ds(col, half), :], o_buf)],
        sems,
    )
    for at in range(0, 2 * rows, LANE):
        unit, _ = norm_stats(x_ref[at : at + LANE, :].astype(F32))
        hidden = (unit * gs_ref[0:1, :] + gs_ref[1:2, :]).astype(BF16)
        h_buf[at : at + LANE, :] = hidden
        ht_ref[:, at : at + LANE] = hidden.T
    for i in range(3):
        copies[i].wait()
        qkv_ref[:, i * half : (i + 1) * half] = mm(h_buf[...], w_buf[:, i * half : (i + 1) * half]).astype(BF16)

    def pair(at, carry):
        c = pl.multiple_of(at * LANE, LANE)
        q, k, v = (qkv_ref[:, pl.ds(i * half + c, LANE)] for i in range(3))
        q_masks, v_masks = head_masks(BF16, 0.125), head_masks(BF16, 1.0)
        for group in range(2):
            total = 0.0
            for h in range(2):
                query = q[group * rows : (group + 1) * rows] * q_masks[h]
                scores = [live_scores(k[:rows], query, length)]
                if group:
                    scores.append(mm_nt(k[rows:], query))
                top = jnp.max(scores[0], axis=0, keepdims=True)
                if group:
                    top = jnp.maximum(top, jnp.max(scores[1], axis=0, keepdims=True))
                powers = [jnp.exp(s - top) for s in scores]
                below = sum(jnp.sum(p, axis=0, keepdims=True) for p in powers)
                lse_ref[pl.ds(2 * at + h, 1), group * rows : (group + 1) * rows] = top + jnp.log(below)
                inverse = 1.0 / below
                for which, p in enumerate(powers):
                    prob = (p * inverse).astype(BF16)
                    total = total + mm_tn(prob, v[which * rows : (which + 1) * rows] * v_masks[h])
            att_ref[group * rows : (group + 1) * rows, pl.ds(c, LANE)] = total.astype(BF16)
        return carry

    lax.fori_loop(0, half // LANE, pair, 0)
    copies[3].wait()
    part_ref[...] = mm(att_ref[...], o_buf[...]).astype(BF16)


def attend(scalars, values, gs, w_qkv, w_out):
    rows, width = values.shape
    half = width // 2
    return pl.pallas_call(
        attend_kernel,
        in_specs=[SMEM, VMEM, VMEM, HBM, HBM],
        out_specs=[VMEM] * 5,
        out_shape=[full((width, rows), BF16), full((rows, 3 * half), BF16), full((rows, half), BF16), full((rows, width), BF16), full((half // HEAD, rows), F32)],
        scratch_shapes=[pltpu.VMEM((width, 3 * half), BF16), pltpu.VMEM((half, width), BF16), pltpu.VMEM((rows, width), BF16), pltpu.SemaphoreType.DMA((4,))],
        compiler_params=params(48),
        cost_estimate=cost(2 * rows * width * 4 * half * 2, 12e6),
        name="attend",
    )(scalars, values, gs, w_qkv, w_out)


def unit_copies(w_up, w_down, up_buf, down_buf, first):
    blocks = w_up.shape[1] // (4 * LANE)
    pairs = []
    for b in range(blocks):
        at = pl.multiple_of((4 * b + first) * LANE, LANE)
        pairs.append((w_up.at[:, pl.ds(at, LANE)], up_buf.at[:, pl.ds(b * LANE, LANE)]))
    for b in range(blocks):
        at = pl.multiple_of((4 * b + first) * LANE, LANE)
        pairs.append((w_down.at[pl.ds(at, LANE), :], down_buf.at[pl.ds(b * LANE, LANE), :]))
    return pairs


def gelu_parts(up):
    cdf = 0.5 + 0.5 * lax.erf(up * np.float32(0.5**0.5))
    slope = cdf + up * (jnp.exp(-0.5 * up * up) * np.float32(1 / np.sqrt(2 * np.pi)))
    return up * cdf, slope


def own_kernel(scalars, xa, xb, pa, ra, pb, rb, dya, dyb, gs_ref, w_up, w_down,
               h_ref, gd_ref, gu_ref, act_ref, dup_ref, res_ref,
               x_buf, p_buf, r_buf, dy_buf, up_buf, down_buf, ht_buf, sems):
    role, x = scalars[0], scalars[2]
    rows = xa.shape[0]
    quarter = up_buf.shape[1]
    copies = copy_all(
        [(s, t.at[pl.ds(u * rows, rows), :]) for u, trio in enumerate(((xa, pa, ra), (xb, pb, rb))) for s, t in zip(trio, (x_buf, p_buf, r_buf))]
        + unit_copies(w_up, w_down, up_buf, down_buf, role + 2 * x)
        + [(dya, dy_buf.at[pl.ds(0, rows), :]), (dyb, dy_buf.at[pl.ds(rows, rows), :])],
        sems,
    )
    for u in range(2):
        for i in range(3):
            copies[3 * u + i].wait()

        def norm(i, carry):
            at = pl.multiple_of(u * rows + i * LANE, LANE)
            here = pl.ds(at, LANE)
            residual = x_buf[here, :].astype(F32) + (p_buf[here, :].astype(F32) + r_buf[here, :].astype(F32))
            unit, _ = norm_stats(residual)
            hidden = (unit * gs_ref[u, 2:3, :] + gs_ref[u, 3:4, :]).astype(BF16)
            h_ref[here, :] = hidden
            ht_buf[:, here] = hidden.T
            if u == 0:
                @pl.when(i // (rows // LANE // 2) == role)
                def _():
                    res_ref[pl.ds(pl.multiple_of((i % (rows // LANE // 2)) * LANE, LANE), LANE), :] = residual
            return carry

        lax.fori_loop(0, rows // LANE, norm, 0)
    for each in copies[6:]:
        each.wait()

    def block(i, carry):
        cols = pl.ds(pl.multiple_of(i * 256, 256), 256)
        act, slope = gelu_parts(mm(h_ref[...], up_buf[:, cols]))
        act = act.astype(BF16)
        act_ref[:, cols] = act[:rows]
        dup = (mm_nt(dy_buf[...], down_buf[cols, :]) * slope).astype(BF16)
        dup_ref[:, cols] = dup
        gd_ref[cols, :] = mm_tn(act, dy_buf[...]).astype(BF16)
        gu_ref[:, cols] = mm(ht_buf[...], dup).astype(BF16)
        return carry

    lax.fori_loop(0, quarter // 256, block, 0)


def own_units(scalars, values, parts, came, dys, gs, w_up, w_down):
    rows, width = values[0].shape
    quarter = w_up.shape[1] // 4
    count = 6 + 2 * (quarter // LANE) + 2
    big = lambda *s: pltpu.VMEM(s, BF16)
    return pl.pallas_call(
        own_kernel,
        in_specs=[SMEM] + [HBM] * 8 + [VMEM] + [HBM] * 2,
        out_specs=[VMEM] * 6,
        out_shape=[full((2 * rows, width), BF16), full((quarter, width), BF16), full((width, quarter), BF16), full((rows, quarter), BF16), full((2 * rows, quarter), BF16), full((rows // 2, width), F32)],
        scratch_shapes=[big(2 * rows, width)] * 4 + [big(width, quarter), big(quarter, width), big(width, 2 * rows), pltpu.SemaphoreType.DMA((count,))],
        compiler_params=params(56),
        cost_estimate=cost(2 * 2 * rows * width * quarter * 4, 20e6),
        name="own_units",
    )(scalars, values[0], values[1], parts[0], came[0], parts[1], came[1], dys[0], dys[1], gs, w_up, w_down)


def rest_kernel(scalars, h_any, dya, dyb, act_any, dup_any, res_ref, w_up, w_down, dh_ref, keep_ref, send_ref,
                h_buf, dy_buf, act_own, act_buf, dup_own, dup_buf, up_own, down_own, up_buf, down_buf, sems):
    role, x = scalars[0], scalars[2]
    rows = dya.shape[0]
    quarter = up_buf.shape[1]
    blocks = quarter // LANE
    copies = copy_all(
        [(h_any, h_buf)]
        + unit_copies(w_up, w_down, up_buf, down_buf, role + 2 * (1 - x))
        + [(dya, dy_buf.at[pl.ds(0, rows), :]), (dyb, dy_buf.at[pl.ds(rows, rows), :]), (act_any, act_own), (dup_any, dup_own)]
        + unit_copies(w_up, w_down, up_own, down_own, role + 2 * x),
        sems,
    )
    first = 1 + 2 * blocks + 2
    for each in copies[:first]:
        each.wait()

    def block(i, carry):
        cols = pl.ds(pl.multiple_of(i * 256, 256), 256)
        act, slope = gelu_parts(mm(h_buf[...], up_buf[:, cols]))
        act_buf[:, cols] = act[:rows].astype(BF16)
        dup_buf[:, cols] = (mm_nt(dy_buf[...], down_buf[cols, :]) * slope).astype(BF16)
        return carry

    lax.fori_loop(0, quarter // 256, block, 0)
    for each in copies[first:]:
        each.wait()

    def back(i, carry):
        here = pl.ds(pl.multiple_of(i * 256, 256), 256)
        dh_ref[here, :] = (mm_nt(dup_own[here, :], up_own[...]) + mm_nt(dup_buf[here, :], up_buf[...])).astype(BF16)
        return carry

    lax.fori_loop(0, 2 * rows // 256, back, 0)
    keep = pl.ds(pl.multiple_of(role * (rows // 2), rows // 2), rows // 2)
    send = pl.ds(pl.multiple_of((1 - role) * (rows // 2), rows // 2), rows // 2)
    keep_ref[...] = res_ref[...] + (mm(act_own[keep, :], down_own[...]) + mm(act_buf[keep, :], down_buf[...]))
    send_ref[...] = (mm(act_own[send, :], down_own[...]) + mm(act_buf[send, :], down_buf[...])).astype(BF16)


def rest_units(scalars, hidden, dys, act, dup, residual, w_up, w_down):
    rows, width = dys[0].shape
    quarter = w_up.shape[1] // 4
    count = 5 + 4 * (quarter // LANE)
    big = lambda *s: pltpu.VMEM(s, BF16)
    return pl.pallas_call(
        rest_kernel,
        in_specs=[SMEM] + [HBM] * 5 + [VMEM] + [HBM] * 2,
        out_specs=[VMEM] * 3,
        out_shape=[full((2 * rows, width), BF16), full((rows // 2, width), F32), full((rows // 2, width), BF16)],
        scratch_shapes=[big(2 * rows, width)] * 2 + [big(rows, quarter)] * 2 + [big(2 * rows, quarter)] * 2 + [big(width, quarter), big(quarter, width)] * 2 + [pltpu.SemaphoreType.DMA((count,))],
        compiler_params=params(56),
        cost_estimate=cost(2 * 2 * rows * width * quarter * 5, 24e6),
        name="rest_units",
    )(scalars, hidden, dys[0], dys[1], act, dup, residual, w_up, w_down)


def pair_back(qkv, lse, datt, c, c_d, rows, half, length):
    q, k, v = (qkv[:, pl.ds(i * half + c, LANE)] for i in range(3))
    grad = datt[:, pl.ds(c_d, LANE)]
    scaled, plain = head_masks(BF16, 0.125), head_masks(BF16, 1.0)
    dq = []
    dk, dv = [0.0, 0.0], [0.0, 0.0]
    for group in range(2):
        here = slice(group * rows, (group + 1) * rows)
        dq_here = 0.0
        for h in range(2):
            query, above = q[here] * scaled[h], grad[here] * plain[h]
            log_total = lse(h, here)
            probs, dprobs = [], []
            delta = 0.0
            for which in range(group + 1):
                there = slice(which * rows, (which + 1) * rows)
                scores = live_scores(k[there], query, length) if which == 0 else mm_nt(k[there], query)
                prob = jnp.exp(scores - log_total)
                dprob = mm_nt(v[there], above)
                delta = delta + jnp.sum(prob * dprob, axis=0, keepdims=True)
                dv[which] = dv[which] + mm(prob.astype(BF16), above)
                probs.append(prob)
                dprobs.append(dprob)
            for which in range(group + 1):
                there = slice(which * rows, (which + 1) * rows)
                dscore = (probs[which] * (dprobs[which] - delta)).astype(BF16)
                dk[which] = dk[which] + mm(dscore, query)
                dq_here = dq_here + mm_tn(dscore, k[there] * scaled[h])
        dq.append(dq_here)
    return dq, dk, dv


def back_kernel(scalars, xa, xb, pa, ra, pb, rb, dh_any, dhr_any, dya, dyb, gs_ref, w_out, att_a, att_b, qkv_a, qkv_b, lse_a, lse_b, ht_a, ht_b,
                gq_ref, go_ref, dr_ref, vec_ref, datt_ref, dqa_ref,
                x_buf, p_buf, r_buf, dh_buf, dhr_buf, dy_buf, da_buf, o_buf, datt_buf, att_buf, qkv_buf, ht_buf, dq_buf, sems):
    role, x = scalars[0], scalars[2]
    rows2, width = xa.shape
    rows, half = rows2 // 2, width // 2
    quarter = half // 2
    own = pl.multiple_of(x * quarter, LANE)
    col = pl.multiple_of(role * half, LANE)
    lse = (lse_a, lse_b)
    pairs = []
    for u, (xs, ps, rs, dys) in enumerate(((xa, pa, ra, dya), (xb, pb, rb, dyb))):
        here = pl.ds(u * rows2, rows2)
        pairs += [(xs, x_buf.at[here, :]), (ps, p_buf.at[here, :]), (rs, r_buf.at[here, :]), (dys, dy_buf.at[here, :]),
                  (dh_any.at[here, :], dh_buf.at[here, :]), (dhr_any.at[here, :], dhr_buf.at[here, :])]
    pairs.append((w_out.at[pl.ds(col, half), :], o_buf))
    for u, (a, q, h) in enumerate(((att_a, qkv_a, ht_a), (att_b, qkv_b, ht_b))):
        here = pl.ds(u * rows2, rows2)
        pairs += [(q, qkv_buf.at[here, :]), (a.at[:, pl.ds(own, quarter)], att_buf.at[here, :]), (h, ht_buf.at[:, here])]
    copies = copy_all(pairs, sems)
    vec_ref[...] = jnp.zeros_like(vec_ref)
    for u in range(2):
        for i in range(6):
            copies[6 * u + i].wait()

        def norm(i, carry):
            here = pl.ds(pl.multiple_of(u * rows2 + i * LANE, LANE), LANE)
            residual = x_buf[here, :].astype(F32) + (p_buf[here, :].astype(F32) + r_buf[here, :].astype(F32))
            unit, rstd = norm_stats(residual)
            dh2 = dh_buf[here, :].astype(F32) + dhr_buf[here, :].astype(F32)
            grad = dy_buf[here, :].astype(F32) + norm_back(unit, rstd, gs_ref[u, 2:3, :], dh2)
            da_buf[here, :] = grad.astype(BF16)
            if u == 0:
                per = rows // LANE
                @pl.when(i // per == role)
                def _():
                    dr_ref[pl.ds(pl.multiple_of((i % per) * LANE, LANE), LANE), :] = grad
                    vec_ref[0:1, :] += jnp.sum(dh2 * unit, axis=0, keepdims=True)
                    vec_ref[1:2, :] += jnp.sum(dh2, axis=0, keepdims=True)
            return carry

        lax.fori_loop(0, rows2 // LANE, norm, 0)
        if u == 0:
            copies[12].wait()
            datt_buf[:rows2, :] = mm_nt(da_buf[:rows2, :], o_buf[...]).astype(BF16)
            datt_ref[...] = datt_buf[:rows2, :]
        else:
            mine = o_buf[pl.ds(pl.multiple_of(x * quarter, quarter), quarter), :]
            datt_buf[rows2:, pl.ds(own, quarter)] = mm_nt(da_buf[rows2:, :], mine).astype(BF16)
    for each in copies[13:]:
        each.wait()
    go_ref[...] = mm_tn(att_buf[...], da_buf[...]).astype(BF16)
    for u in range(2):
        base = u * rows2
        length = scalars[1] if u == 0 else scalars[3]

        def one(at, carry):
            c = pl.multiple_of(own + at * LANE, LANE)
            to = pl.multiple_of(at * LANE, LANE)
            first = (own + at * LANE) // HEAD
            look = lambda h, here: lse[u][pl.ds(first + h, 1), here]
            dq, dk, dv = pair_back(qkv_buf.at[pl.ds(base, rows2), :], look, datt_buf.at[pl.ds(base, rows2), :], c, c, rows, half, length)
            for i, halves in enumerate((dq, dk, dv)):
                for g in range(2):
                    dq_buf[base + g * rows : base + (g + 1) * rows, pl.ds(i * quarter + to, LANE)] = halves[g].astype(BF16)
            return carry

        lax.fori_loop(0, quarter // LANE, one, 0)
    dqa_ref[...] = dq_buf[:rows2, :]
    for i in range(3):
        cols = slice(i * quarter, (i + 1) * quarter)
        gq_ref[:, cols] = mm(ht_buf[...], dq_buf[:, cols]).astype(BF16)


def back(scalars, values, parts, came, dh, dh_came, dys, gs, w_out, atts, qkvs, lses, hts):
    rows2, width = values[0].shape
    half = width // 2
    big = lambda *s: pltpu.VMEM(s, BF16)
    tokens = 2 * rows2
    return pl.pallas_call(
        back_kernel,
        in_specs=[SMEM] + [HBM] * 10 + [VMEM] + [HBM] * 5 + [VMEM] * 2 + [HBM] * 2,
        out_specs=[VMEM] * 6,
        out_shape=[full((width, 3 * half // 2), BF16), full((half // 2, width), BF16), full((rows2 // 2, width), F32), full((8, width), F32), full((rows2, half), BF16), full((rows2, 3 * half // 2), BF16)],
        scratch_shapes=[big(tokens, width)] * 7 + [big(half, width), big(tokens, half), big(tokens, half // 2), big(tokens, 3 * half), big(width, tokens), big(tokens, 3 * half // 2), pltpu.SemaphoreType.DMA((19,))],
        compiler_params=params(56),
        cost_estimate=cost(15e9, 24e6),
        name="back",
    )(scalars, values[0], values[1], parts[0], came[0], parts[1], came[1], dh, dh_came, dys[0], dys[1], gs, w_out, atts[0], atts[1], qkvs[0], qkvs[1], lses[0], lses[1], hts[0], hts[1])


def last_kernel(scalars, qkv_ref, lse_ref, datt_ref, dqa_ref, w_qkv, keep_ref, send_ref, w_own, w_buf, dq_buf, sems):
    role, x, length = scalars[0], scalars[2], scalars[1]
    rows2, half = datt_ref.shape
    rows, quarter, width = rows2 // 2, half // 2, 2 * half
    mine = pl.multiple_of(x * quarter, LANE)
    other = pl.multiple_of((1 - x) * quarter, LANE)
    col = pl.multiple_of(role * half, LANE)
    copies = copy_all(
        [(w_qkv.at[:, pl.ds(i * width + col + from_, quarter)], to.at[:, pl.ds(i * quarter, quarter)]) for from_, to in ((mine, w_own), (other, w_buf)) for i in range(3)],
        sems,
    )

    def one(at, carry):
        c = pl.multiple_of(other + at * LANE, LANE)
        to = pl.multiple_of(at * LANE, LANE)
        first = (other + at * LANE) // HEAD
        look = lambda h, here: lse_ref[pl.ds(first + h, 1), here]
        dq, dk, dv = pair_back(qkv_ref, look, datt_ref, c, c, rows, half, length)
        for i, halves in enumerate((dq, dk, dv)):
            for g in range(2):
                dq_buf[g * rows : (g + 1) * rows, pl.ds(i * quarter + to, LANE)] = halves[g].astype(BF16)
        return carry

    lax.fori_loop(0, quarter // LANE, one, 0)
    for each in copies:
        each.wait()
    keep = pl.ds(pl.multiple_of(role * rows, rows), rows)
    send = pl.ds(pl.multiple_of((1 - role) * rows, rows), rows)
    keep_ref[...] = mm_nt(dqa_ref[keep, :], w_own[...]) + mm_nt(dq_buf[keep, :], w_buf[...])
    send_ref[...] = (mm_nt(dqa_ref[send, :], w_own[...]) + mm_nt(dq_buf[send, :], w_buf[...])).astype(BF16)


def last(scalars, qkv, lse, datt, dqa, w_qkv):
    rows2, half = datt.shape
    width = 2 * half
    big = lambda *s: pltpu.VMEM(s, BF16)
    return pl.pallas_call(
        last_kernel,
        in_specs=[SMEM] + [VMEM] * 4 + [HBM],
        out_specs=[VMEM] * 2,
        out_shape=[full((rows2 // 2, width), F32), full((rows2 // 2, width), BF16)],
        scratch_shapes=[big(width, 3 * half // 2)] * 2 + [big(rows2, 3 * half // 2), pltpu.SemaphoreType.DMA((6,))],
        compiler_params=params(48),
        cost_estimate=cost(5e9, 10e6),
        name="last",
    )(scalars, qkv, lse, datt, dqa, w_qkv)


class Layout:
    def __init__(self, width, ff, sections, members):
        self.width, self.ff, self.members = width, ff, members
        shapes = {"q": (width, 3 * width), "o": (width, width), "u": (width, ff), "d": (ff, width), "s": (4 * sections, width)}
        start, self.spans = 0, {}
        for name, (rows, columns) in shapes.items():
            self.spans[name] = (start, rows, columns)
            start += rows * columns
        self.total = start
        self.share = start // members
        self.segments = [self.parts_of(m) for m in range(members)]
        self.rows = max(s[-1]["at"] + s[-1]["wire"] for s in self.segments)

    def span(self, member, name):
        start, rows, columns = self.spans[name]
        low = max(member * self.share, start) - start
        high = min((member + 1) * self.share, start + rows * columns) - start
        return (low, high) if low < high else None

    def parts_of(self, member):
        parts, at = [], 0
        for name in ("q", "o", "u", "d"):
            found = self.span(member, name)
            if found is None:
                continue
            columns = self.spans[name][2]
            low, high = found[0] // columns, -(-found[1] // columns)
            if name == "o":
                held = [r % (self.width // 4) for r in range(low, high)]
                low, high = min(held), max(held) + 1
            if name == "d":
                held = [r // (4 * LANE) * LANE + r % LANE for r in range(low, high)]
                low, high = min(held), max(held) + 1
            low, high = low // 16 * 16, -(-high // 16) * 16
            count = high - low
            wire = -(-(3 * count // 4) // 16) * 16 if name == "q" else count
            parts.append({"name": name, "low": low, "high": high, "at": at, "wire": wire})
            at += wire
        return parts

    def table(self):
        rows = []
        for share in range(2 * self.members):
            entry = [share * (self.share // 2) // LANE]
            held = {p["name"]: p for p in self.segments[share // 2]}
            for name in ("q", "o", "u", "d"):
                p = held.get(name)
                entry += [p["low"], p["high"], p["at"], p["wire"]] if p else [0, 0, 0, 0]
            rows.append(entry + [0] * (24 - len(entry)))
        return np.asarray(rows, np.int32)

    def wire(self, member, pieces):
        out = []
        for p in self.segments[member]:
            piece = pieces[p["name"]][p["low"] : p["high"]]
            if p["name"] == "q":
                n1 = p["wire"]
                n2 = p["high"] - p["low"] - n1
                quarter = piece.shape[1] // 3
                side = [piece[n1:, i * quarter : (i + 1) * quarter] for i in range(3)]
                if n1 > 3 * n2:
                    side.append(jnp.zeros((n1 - 3 * n2, quarter), BF16))
                piece = jnp.concatenate([piece[:n1], jnp.concatenate(side, 0)], 1)
            out.append(piece)
        short = self.rows - sum(o.shape[0] for o in out)
        if short:
            out.append(jnp.zeros((short, self.width), BF16))
        return jnp.concatenate(out, 0) if len(out) > 1 else out[0]


def after(value, *first):
    return lax.optimization_barrier((value, *first))[0]


def add(left, right):
    return (left.astype(F32) + right.astype(F32)).astype(BF16)


def tree_pairs(block, level, count):
    size = 2 << level
    pairs = []
    for low in range(0, count, size):
        middle, high = low + size // 2, low + size
        left, right = min(max(block, low), middle - 1), min(max(block, middle), high - 1)
        source, target = (right, left) if block < middle else (left, right)
        pairs += [(2 * source + y, 2 * target + y) for y in range(2)]
    return pairs


def place_kernel(spans, table, own, mate, across, diagonal, small_ref, out_ref, wire, flat, sems):
    me, unit0 = table[24], table[0]
    units = out_ref.shape[0]
    width = wire.shape[2]
    chunks = width // LANE
    front = 512
    x, role = me // 2, me % 2
    where = (me, role + 2 * (1 - x), (1 - role) + 2 * x, (1 - role) + 2 * (1 - x))
    copies = copy_all([(source, wire.at[at]) for source, at in zip((own, mate, across, diagonal), where)], sems.at[pl.ds(0, 4)])
    for each in copies:
        each.wait()

    def rows_of(name, per_row):
        at = 1 + 4 * "qoud".index(name)
        low, high = table[at], table[at + 1]
        base = unit0 - spans[name][0] // LANE
        first = jnp.maximum(low // 16, jnp.maximum(base, 0) // per_row // 16)
        last = jnp.minimum(high // 16, (jnp.maximum(base + units, 0) + per_row * 16 - 1) // (per_row * 16))
        return low, first, last, table[at + 2], table[at + 3], base

    low, first, last, at, n1, base = rows_of("q", 3 * chunks)
    n2 = table[2] - table[1] - n1

    def qkv(g, carry):
        row = g * 16 - low
        to = front + g * 16 * 3 * chunks - base
        beside = row >= n1
        half = chunks // 4
        for section in range(3):
            source = jnp.where(beside, at + section * n2 + row - n1, at + row)
            for h in range(half):
                column = pl.multiple_of(jnp.where(beside, 3 * width // 4 + h * LANE, section * (width // 4) + h * LANE), LANE)
                for piece in range(4):
                    unit = section * chunks + (piece % 2) * (chunks // 2) + (piece // 2) * half + h
                    flat[pl.ds(to + unit, 16, stride=3 * chunks), :] = wire[piece, pl.ds(pl.multiple_of(source, 16), 16), pl.ds(column, LANE)].astype(F32)
        return carry

    lax.fori_loop(first, jnp.maximum(first, last), qkv, 0)
    per = spans["u"][2] // LANE
    low, first, last, at, _, base = rows_of("u", per)

    def up(g, carry):
        source = pl.multiple_of(at + g * 16 - low, 16)
        to = front + g * 16 * per - base
        for h in range(chunks):
            for piece in range(4):
                flat[pl.ds(to + 4 * h + piece, 16, stride=per), :] = wire[piece, pl.ds(source, 16), h * LANE : (h + 1) * LANE].astype(F32)
        return carry

    lax.fori_loop(first, jnp.maximum(first, last), up, 0)

    for name in ("o", "d"):
        slot = 1 + 4 * "qoud".index(name)
        low, high, at = table[slot], table[slot + 1], table[slot + 2]
        base = unit0 - spans[name][0] // LANE

        def rows(g, carry):
            row = g * 16
            source = pl.multiple_of(at + row - low, 16)
            for piece in range(4):
                if name == "o":
                    line = (piece % 2) * (width // 2) + (piece // 2) * (width // 4) + row
                else:
                    line = (row // LANE) * (4 * LANE) + piece * LANE + row % LANE
                to = line * chunks - base

                @pl.when((to + 16 * chunks > 0) & (to < units))
                def _():
                    for h in range(chunks):
                        flat[pl.ds(front + to + h, 16, stride=chunks), :] = wire[piece, pl.ds(source, 16), h * LANE : (h + 1) * LANE].astype(F32)

            return carry

        lax.fori_loop(low // 16, high // 16, rows, 0)

    tail = spans["s"][0] // LANE - unit0

    @pl.when(tail < units)
    def _():
        for g in range(small_ref.shape[0] // 8):
            for h in range(chunks):
                flat[pl.ds(front + tail + g * 8 * chunks + h, 8, stride=chunks), :] = small_ref[g * 8 : (g + 1) * 8, h * LANE : (h + 1) * LANE]

    done = pltpu.make_async_copy(flat.at[pl.ds(front, units), :], out_ref, sems.at[4])
    done.start()
    done.wait()


def place(layout, table, quad, small):
    rows, width = quad[0].shape
    units = layout.share // 2 // LANE
    return pl.pallas_call(
        functools.partial(place_kernel, layout.spans),
        in_specs=[SMEM] + [HBM] * 4 + [VMEM],
        out_specs=HBM,
        out_shape=full((units, LANE), F32),
        scratch_shapes=[pltpu.VMEM((4, rows, width), BF16), pltpu.VMEM((-(-units // 8) * 8 + 1024, LANE), F32), pltpu.SemaphoreType.DMA((5,))],
        compiler_params=params(32),
        cost_estimate=cost(0, 12e6),
        name="place",
    )(table, *quad, small)


def local(frames, cotangent, w_qkv, w_out, w_up, w_down, gains, shifts, prompt_len, section):
    rows, width = frames.shape[2], frames.shape[3]
    ff, sections = w_up.shape[1], gains.shape[0]
    role, group, member = lax.axis_index("role"), lax.axis_index("group"), lax.axis_index("member")
    x = group % 2
    members, groups = lax.axis_size("member"), lax.axis_size("group")
    layout = Layout(width, ff, sections, members)
    outer, inner = member // 2, member % 2
    count = members // 2

    def whole(own):
        other = swap(own, "role")
        return jnp.concatenate([jnp.where(role == 0, own, other), jnp.where(role == 0, other, own)], 0)

    own_frames, own_cot = frames[0, 0], cotangent[0, 0]
    values = [whole(own_frames), whole(swap(own_frames, "group"))]
    dys = [whole(own_cot), whole(swap(own_cot, "group"))]
    lengths = [prompt_len[0], swap(prompt_len, "group")[0]]
    section_ids = [section[0], swap(section, "group")[0]]

    def rows_of(table, at):
        return lax.dynamic_slice(table, (at, 0, 0), (1, 2, width))[0].astype(F32)

    gs = []
    for at in section_ids:
        gain, shift = rows_of(gains, at), rows_of(shifts, at)
        gs.append(jnp.stack([gain[0], shift[0], gain[1], shift[1]]))
    both_gs = jnp.stack(gs)
    scalars = jnp.stack([role, lengths[0], x, lengths[1]]).astype(jnp.int32)
    scalars_b = jnp.stack([role, lengths[1], x, lengths[0]]).astype(jnp.int32)

    totals, pieces = {}, {}
    early, late = [], []
    for block in reversed(range(count)):
        names = {p["name"] for m in (2 * block, 2 * block + 1) for p in layout.segments[m]}
        (early if names <= {"u", "d"} else late).append(block)
    halves = lambda value: [value[: layout.rows // 32 * 16], value[layout.rows // 32 * 16 :]]
    sent = []

    def exchange(block, cut):
        even, odd = layout.wire(2 * block, pieces), layout.wire(2 * block + 1, pieces)
        keep = jnp.where(inner == 0, even, odd)
        send = jnp.where(inner == 0, odd, even)
        totals[block] = []
        for k, s in zip(cut(keep), cut(send)):
            if sent:
                s = after(s, sent[-1])
            sent.append(swap(s, "member"))
            totals[block].append(add(k, sent[-1]))

    levels = count.bit_length() - 1

    def climb(block, level):
        totals[block] = [add(t, lax.ppermute(t, "member", tree_pairs(block, level, count))) for t in totals[block]]

    hts, qkvs, atts, parts, lses = zip(*(attend(s, v, g, w_qkv, w_out) for s, v, g in zip((scalars, scalars_b), values, gs)))
    came = [swap(part, "role") for part in parts]
    hidden, pieces["d"], pieces["u"], act, dup, residual = own_units(scalars, values, parts, came, dys, both_gs, w_up, w_down)
    for block in early:
        exchange(block, lambda value: [value])
    dh, out_keep, out_send = rest_units(scalars, hidden, dys, act, dup, residual, w_up, w_down)
    output = (out_keep + swap(out_send, "role").astype(F32)).astype(BF16)
    dh_came = swap(dh, "role")
    if early:
        dh_came = after(dh_came, *totals[early[0]])
    pieces["q"], pieces["o"], dr1, vec_two, datt, dqa = back(scalars, values, parts, came, dh, dh_came, dys, both_gs, w_out, atts, qkvs, lses, hts)
    for block in late:
        exchange(block, halves)
    if early:
        climb(early[0], 0)
        datt = after(datt, *totals[early[0]], *totals[early[1 % len(early)]])
    dh1_keep, dh1_send = last(scalars, qkvs[0], lses[0], datt, dqa, w_qkv)
    dh1 = dh1_keep + swap(dh1_send, "role").astype(F32)
    unit, rstd = norm_stats(own_frames.astype(F32))
    input_grad = dr1 + norm_back(unit, rstd, gs[0][0:1], dh1)

    vectors = jnp.stack([jnp.stack([jnp.sum(dh1 * unit, 0), vec_two[0]]), jnp.stack([jnp.sum(dh1, 0), vec_two[1]])])
    select = (jnp.arange(sections, dtype=jnp.int32) == section_ids[0]).astype(F32)
    small = select[None, :, None, None] * vectors[:, None]
    small = jnp.pad(small.reshape(4 * sections, width), ((0, -4 * sections % 8), (0, 0)))
    for axis in ("role", "group", "member"):
        distance = 1
        while distance < lax.axis_size(axis):
            small = small + swap(small, axis, distance)
            distance *= 2

    for block in early + late:
        for level in range(1 if early and block == early[0] else 0, levels):
            climb(block, level)
    finals = None
    for block in early + late:
        here = totals[block] if len(totals[block]) == 2 else halves(totals[block][0])
        finals = here if finals is None else [jnp.where(outer == block, h, f) for h, f in zip(here, finals)]
    distance = 2
    while distance < groups:
        finals = [add(f, swap(f, "group", distance)) for f in finals]
        distance *= 2
    mates = [swap(f, "group") for f in finals]
    own, mate = jnp.concatenate(finals, 0), jnp.concatenate(mates, 0)
    quad = [own, mate, swap(own, "role"), swap(mate, "role")]
    table = lax.dynamic_slice(jnp.asarray(layout.table()), (2 * member + role, 0), (1, 24))[0]
    table = jnp.concatenate([table, (role + 2 * x)[None].astype(jnp.int32), jnp.zeros((7,), jnp.int32)])
    shard = place(layout, table, quad, small).reshape(-1)
    return output[None, None], input_grad[None, None], shard


def solution(mesh):
    rows = P(("group", "member"), "role", None, None)
    per_seq = P(("group", "member"))
    return jax.shard_map(
        local,
        mesh=mesh,
        in_specs=(rows, rows, P(), P(), P(), P(), P(), P(), per_seq, per_seq),
        out_specs=(rows, rows, P(("member", "role"))),
        check_vma=False,
    )
```

time: 1610 us -> 315 us (0.20)
  blocking collectives: 1090 us -> 0 us
  other arithmetic: 253 us -> 39 us
  Pallas kernels: 0 us -> 93.6 us
  matrix products: 81.6 us -> 0 us
  local copies, waits for them, and re-layouts: 79.9 us -> 15.4 us
  starting transfers between devices: 6.79 us -> 55.9 us
  waiting for transfers between devices: 77.9 us -> 102 us
    all_to_all x1 -> x0, blocking collectives: 1090 us -> none  [local(): lax.all_to_all(blocks, ('member', 'role'), split_axis=0, concat_axis=0, t...]
    reduce_sum x7 -> x3, other arithmetic: 244 us -> 1.06 us  [the longest x1 0.63 us: local(): jnp.sum(dh1 * unit, 0)]
    ppermute x2 -> x40, waiting for transfers between devices: 0.01 us -> 102 us  [the longest x28 68.1 us: swap(): return lax.ppermute(value, axis, [(i, i ^ distance) for i in range(count)])]
    pallas_call x0 -> x7, Pallas kernels: none -> 93.6 us  [the longest x2 22.6 us: attend(): pl.pallas_call(attend_kernel, in_specs=[SMEM, VMEM, VMEM, HBM, HBM], out_...]
    dot_general x20 -> x0, matrix products: 81.6 us -> none  [the longest x1 16.1 us: local(): upward = jnp.dot(hidden_two, w_up, preferred_element_type=jnp.float32)]
    psum x1 -> x0, waiting for transfers between devices: 77.9 us -> none  [local(): shard_sum = lax.psum(shard_sum, 'group')]
    unnamed x94 -> x65, local copies, waits for them, and re-layouts: 71.3 us -> 7.03 us
    ppermute x2 -> x40, starting transfers between devices: 6.75 us -> 55.9 us  [the longest x28 29.6 us: swap(): return lax.ppermute(value, axis, [(i, i ^ distance) for i in range(count)])]
  transfers between devices with their start and end apart: 3 -> 40, of which waited for: 1 -> 16; matrix products, arithmetic and copies ran while one was open for 2% -> 14% of each run, Pallas kernels for 0% -> 23%
where the time goes in v1:
time: 315 us; the launch traced here: 310 us
  waiting for transfers between devices  102 us (32%)
  Pallas kernels  93.6 us (30%)
  starting transfers between devices  55.9 us (18%)
  other arithmetic  39 us (12%)
  local copies, waits for them, and re-layouts  15.4 us (5%)
  between operations  4.75 us (2%)
    ppermute x28, waiting for transfers between devices, swap(): return lax.ppermute(value, axis, [(i, i ^ distance) for i in range(count)])  68.1 us
    ppermute x12, waiting for transfers between devices, climb(): lax.ppermute(t, 'member', tree_pairs(block, level, count))  33.4 us
    ppermute x28, starting transfers between devices, swap(): return lax.ppermute(value, axis, [(i, i ^ distance) for i in range(count)])  29.6 us
    ppermute x12, starting transfers between devices, climb(): lax.ppermute(t, 'member', tree_pairs(block, level, count))  26.3 us
    pallas_call x2, Pallas kernels, attend(): pl.pallas_call(attend_kernel, in_specs=[SMEM, VMEM, VMEM, HBM, HBM], out_...  22.6 us
    pallas_call x1, Pallas kernels, back(): pl.pallas_call(back_kernel, in_specs=[SMEM] + [HBM] * 10 + [VMEM] + [HBM]...  20.9 us
    pallas_call x1, Pallas kernels, rest_units(): pl.pallas_call(rest_kernel, in_specs=[SMEM] + [HBM] * 5 + [VMEM] + [HBM]...  20.2 us
    pallas_call x1, Pallas kernels, own_units(): pl.pallas_call(own_kernel, in_specs=[SMEM] + [HBM] * 8 + [VMEM] + [HBM] *...  19.7 us
  transfers between devices with their start and end apart: 40, of which 16 were waited for; matrix products, arithmetic and copies ran while one was open for 14% of the time, Pallas kernels for 23%

profile of v1, /device:TPU:1, one launch (start us, length us, event | category | flops | bytes accessed | tf_op | source)
XLA Modules:
  0.0 310.1 jit_solution(6678502870727313149)
XLA Ops:
  6.5 8.1 %collective-permute-done.5 = s32[1]{0:T(128)} collective-permute-done((s32[1]{0:T(128)}, s32[1]{0:T(128)}, u32[]{:S(2)}, u32[]{:S(2)}) %collective-permute-start.5) | collective-permute-done | bytes 36 | tf_op jit(solution)/shard_map/ppermute | solution.py:36
  14.6 2.2 collective-permute-start.1
  21.0 4.9 %collective-permute-done.2 = bf16[256,1024]{1,0:T(8,128)(2,1)S(1)} collective-permute-done((bf16[256,1024]{1,0:T(8,128)(2,1)}, bf16[256,1024]{1,0:T(8,128)(2,1)S(1)}, u32[]{:S(2)}, u32[]{:S(2)}) %collective-permute-start.2) | collective-permute-done | bytes 524320 | tf_op jit(solution)/shard_map/ppermute | solution.py:36
  28.3 11.4 %attend.2 = (bf16[1024,512]{1,0:T(8,128)(2,1)S(1)}, bf16[512,1536]{1,0:T(8,128)(2,1)S(1)}, bf16[512,512]{1,0:T(8,128)(2,1)S(1)}, bf16[512,1024]{1,0:T(8,128)(2,1)S(1)}, f32[8,512]{1,0:T(8,128)S(1)}) custom-call(s32[4]{0:T(128)S(1)} %pad_add_fusion.scalars, bf16[512,1024]{1,0:T(8,128)(2,1)S(1)} %pad_maximum_fusion.x_ref.xa, ...), custom_call_target="tpu_custom_call" | custom-call | flops 4294967296 | bytes 12000000 | tf_op jit(solution)/shard_map/attend/pallas_call | solution.py:136
  42.3 11.2 %attend.3 = (bf16[1024,512]{1,0:T(8,128)(2,1)S(1)}, bf16[512,1536]{1,0:T(8,128)(2,1)S(1)}, bf16[512,512]{1,0:T(8,128)(2,1)S(1)}, bf16[512,1024]{1,0:T(8,128)(2,1)S(1)}, f32[8,512]{1,0:T(8,128)S(1)}) custom-call(s32[4]{0:T(128)S(1)} %pad_add_fusion.1.scalars, bf16[512,1024]{1,0:T(8,128)(2,1)S(1)} %pad_maximum_fusion.1.x_ref.xb, ...), custom_call_target="tpu_custom_call" | custom-call | flops 4294967296 | bytes 12000000 | tf_op jit(solution)/shard_map/attend/pallas_call | solution.py:136
  63.3 19.7 %own_units.1 = (bf16[1024,1024]{1,0:T(8,128)(2,1)}, bf16[1024,1024]{1,0:T(8,128)(2,1)}, bf16[1024,1024]{1,0:T(8,128)(2,1)}, bf16[512,1024]{1,0:T(8,128)(2,1)}, b...) custom-call(s32[4]{0:T(128)} %copy-done.2, bf16[512,1024]{1,0:T(8,128)(2,1)} %copy-done, bf16[512,1024]{1,0:T(8,128)(2,1)} %copy-done.1, ...), custom_call_target="tpu_custom_call" | custom-call | flops 8589934592 | bytes 20000000 | tf_op jit(solution)/shard_map/own_units/pallas_call | solution.py:219
  84.3 2.4 broadcast_select_fusion.5
  88.2 20.2 %rest_units.1 = (bf16[1024,1024]{1,0:T(8,128)(2,1)}, f32[256,1024]{1,0:T(8,128)}, bf16[256,1024]{1,0:T(8,128)(2,1)}) custom-call(s32[4]{0:T(128)} %copy-done.2, bf16[1024,1024]{1,0:T(8,128)(2,1)} %get-tuple-element.39.h_any, bf16[512,1024]{1,0:T(8,128)(2,1)} %get-tuple-element.125.dya, bf16[512,1024]{1,0:T(8,128)(2,1)} %get-tuple-element.126.dyb, ...), custom_call_target="tpu_custom_call" | custom-call | flops 10737418240 | bytes 24000000 | tf_op jit(solution)/shard_map/rest_units/pallas_call | solution.py:276
  112.0 3.5 %collective-permute-start.13 = (bf16[416,1024]{1,0:T(8,128)(2,1)S(1)}, bf16[416,1024]{1,0:T(8,128)(2,1)S(1)}, u32[]{:S(2)}, u32[]{:S(2)}) collective-permute-start(bf16[416,1024]{1,0:T(8,128)(2,1)S(1)} %add_convert_fusion.5), channel_id=1, source_target_pairs={{0,4},{2,6},{8,12},{10,14},{1,5},{3,7},{9,13},{11,15},{16,20},{18,... | collective-permute-start | bytes 2555912 | tf_op jit(solution)/shard_map/ppermute | solution.py:704
  116.5 14.4 %collective-permute-done.14 = bf16[416,1024]{1,0:T(8,128)(2,1)S(1)} collective-permute-done((bf16[416,1024]{1,0:T(8,128)(2,1)S(1)}, bf16[416,1024]{1,0:T(8,128)(2,1)S(1)}, u32[]{:S(2)}, u32[]{:S(2)}) %collective-permute-start.14) | collective-permute-done | bytes 852000 | tf_op jit(solution)/shard_map/ppermute | solution.py:36
  131.4 4.1 %collective-permute-start.23 = (bf16[416,1024]{1,0:T(8,128)(2,1)S(1)}, bf16[416,1024]{1,0:T(8,128)(2,1)}, u32[]{:S(2)}, u32[]{:S(2)}) collective-permute-start(bf16[416,1024]{1,0:T(8,128)(2,1)S(1)} %add_convert_fusion.3), channel_id=1, source_target_pairs={{0,4},{2,6},{12,8},{14,10},{1,5},{3,7},{13,9},{15,11},{16,20},{18,... | collective-permute-start | bytes 2555912 | tf_op jit(solution)/shard_map/ppermute | solution.py:704
  137.4 20.9 %back.1 = (bf16[1024,768]{1,0:T(8,128)(2,1)}, bf16[256,1024]{1,0:T(8,128)(2,1)}, f32[256,1024]{1,0:T(8,128)}, f32[8,1024]{1,0:T(8,128)}, bf16[512,512]{1,0:T(8,128)(2,1)}, /*index=5*/bf16[512,768]{1,0:T(8,128)(2,1)}) custom-call(s32[4]{0:T(128)} %copy-done.2, bf16[512,1024]{1,0:T(8,128)(2,1)} %copy-done, bf16[512,1024]{1,0:T(8,128)(2,1)} %copy-done.1, ...), custom_call_target="tpu_custom_call" | custom-call | flops 15000000512 | bytes 24000000 | tf_op jit(solution)/shard_map/back/pallas_call | solution.py:399
  161.7 6.1 %broadcast_select_fusion = (bf16[416,1024]{1,0:T(8,128)(2,1)S(1)}, bf16[416,1024]{1,0:T(8,128)(2,1)S(1)}, bf16[416,1024]{1,0:T(8,128)(2,1)S(1)}) fusion(pred[]{:T(512)S(6)} %eq.22, bf16[400,1024]{1,0:T(8,128)(2,1)S(1)} %get-tuple-element.75, bf16[144,1024]{1,0:T(8,128)(2,1)S(1)} %copy-done.25, bf16[256,1024]{1,0:T(8,128)(2,1)S(1)} %copy-done.28, ...), kind=kLoop, calls=%fused_computation.53 | loop fusion | flops 15335424 | bytes 5833537 | tf_op jit(solution)/shard_map/jit(_where)/select_n | solution.py:692
  169.3 6.4 %last.1 = (f32[256,1024]{1,0:T(8,128)S(1)}, bf16[256,1024]{1,0:T(8,128)(2,1)S(1)}) custom-call(s32[4]{0:T(128)S(1)} %copy-done.3, bf16[512,1536]{1,0:T(8,128)(2,1)S(1)} %copy-done.7, f32[8,512]{1,0:T(8,128)S(1)} %copy-done.16, bf16[512,512]{1,0:T(8,128)(2,1)S(1)} %copy-done.14, bf16[512,768]{1,0:T(8,128)(2,1)S(1)} %copy-done.13, bf16[1024,3072]{1,0:T(8,128)(2,1)} %w_qkv.5), custom_call_target="tpu_custom_call" | custom-call | flops 5000000000 | bytes 10000000 | tf_op jit(solution)/shard_map/last/pallas_call | solution.py:447
  175.7 5.3 %broadcast_select_fusion.2 = bf16[416,1024]{1,0:T(8,128)(2,1)S(1)} fusion(pred[]{:T(512)S(6)} %eq.22, bf16[416]{0:T(512)(128)(2,1)S(1)} %pad.25.clone, bf16[16,1024]{1,0:T(8,128)(2,1)S(1)} %slice.177, bf16[128,256]{1,0:T(8,128)(2,1)S(1)} %get-tuple-element.82, bf16[128,256]{1,0:T(8,128)(2,1)S(1)} %get-tuple-element.83, ...), kind=kLoop, calls=%fused_computation.55 | loop fusion | flops 12353536 | bytes 2491201 | tf_op jit(solution)/shard_map/jit(_where)/select_n | solution.py:693
  187.4 7.1 %collective-permute-done.17 = bf16[208,1024]{1,0:T(8,128)(2,1)S(1)} collective-permute-done((bf16[208,1024]{1,0:T(8,128)(2,1)S(1)}, bf16[208,1024]{1,0:T(8,128)(2,1)S(1)}, u32[]{:S(2)}, u32[]{:S(2)}) %collective-permute-start.17) | collective-permute-done | bytes 426016 | tf_op jit(solution)/shard_map/ppermute | solution.py:36
  195.0 2.3 add_convert_fusion
  197.9 7.1 %collective-permute-done.18 = bf16[208,1024]{1,0:T(8,128)(2,1)S(1)} collective-permute-done((bf16[208,1024]{1,0:T(8,128)(2,1)S(1)}, bf16[208,1024]{1,0:T(8,128)(2,1)S(1)}, u32[]{:S(2)}, u32[]{:S(2)}) %collective-permute-start.18) | collective-permute-done | bytes 426016 | tf_op jit(solution)/shard_map/ppermute | solution.py:36
  206.7 7.3 %collective-permute-start.21 = (bf16[208,1024]{1,0:T(8,128)(2,1)}, bf16[208,1024]{1,0:T(8,128)(2,1)}, u32[]{:S(2)}, u32[]{:S(2)}) collective-permute-start(bf16[208,1024]{1,0:T(8,128)(2,1)} %get-tuple-element.95), channel_id=1, source_target_pairs={{0,4},{2,6},{12,8},{14,10},{1,5},{3,7},{13,9},{15,11},{16,20},{18,... | collective-permute-start | bytes 1277960 | tf_op jit(solution)/shard_map/ppermute | solution.py:704
  218.3 2.5 collective-permute-done.21
  224.0 5.8 %collective-permute-done.29 = bf16[208,1024]{1,0:T(8,128)(2,1)S(1)} collective-permute-done((bf16[208,1024]{1,0:T(8,128)(2,1)}, bf16[208,1024]{1,0:T(8,128)(2,1)S(1)}, u32[]{:S(2)}, u32[]{:S(2)}) %collective-permute-start.29) | collective-permute-done | bytes 426016 | tf_op jit(solution)/shard_map/ppermute | solution.py:704
  232.2 6.3 %collective-permute-done.27 = bf16[208,1024]{1,0:T(8,128)(2,1)S(1)} collective-permute-done((bf16[208,1024]{1,0:T(8,128)(2,1)S(1)}, bf16[208,1024]{1,0:T(8,128)(2,1)S(1)}, u32[]{:S(2)}, u32[]{:S(2)}) %collective-permute-start.27) | collective-permute-done | bytes 426016 | tf_op jit(solution)/shard_map/ppermute | solution.py:704
  240.4 3.3 %collective-permute-start.35 = (f32[32,1024]{1,0:T(8,128)S(1)}, f32[32,1024]{1,0:T(8,128)S(1)}, u32[]{:S(2)}, u32[]{:S(2)}) collective-permute-start(f32[32,1024]{1,0:T(8,128)S(1)} %pad.8), channel_id=1, source_target_pairs={{0,1},{1,0},{2,3},{3,2},{4,5},{5,4},{6,7},{7,6},{8,9},{9,8},{10,11... | collective-permute-start | bytes 393224 | tf_op jit(solution)/shard_map/ppermute | solution.py:36
  245.1 9.6 %collective-permute-done.20 = bf16[208,1024]{1,0:T(8,128)(2,1)S(1)} collective-permute-done((bf16[208,1024]{1,0:T(8,128)(2,1)S(1)}, bf16[208,1024]{1,0:T(8,128)(2,1)S(1)}, u32[]{:S(2)}, u32[]{:S(2)}) %collective-permute-start.20) | collective-permute-done | bytes 426016 | tf_op jit(solution)/shard_map/ppermute | solution.py:704
  254.8 9.1 %collective-permute-done.28 = bf16[208,1024]{1,0:T(8,128)(2,1)S(1)} collective-permute-done((bf16[208,1024]{1,0:T(8,128)(2,1)S(1)}, bf16[208,1024]{1,0:T(8,128)(2,1)S(1)}, u32[]{:S(2)}, u32[]{:S(2)}) %collective-permute-start.28) | collective-permute-done | bytes 426016 | tf_op jit(solution)/shard_map/ppermute | solution.py:704
  266.4 3.1 %collective-permute-start.10 = (bf16[256,1024]{1,0:T(8,128)(2,1)S(1)}, bf16[256,1024]{1,0:T(8,128)(2,1)S(1)}, u32[]{:S(2)}, u32[]{:S(2)}) collective-permute-start(bf16[256,1024]{1,0:T(8,128)(2,1)S(1)} %copy-done.31), channel_id=1, source_target_pairs={{0,1},{1,0},{2,3},{3,2},{4,5},{5,4},{6,7},{7,6},{8,9},{9,8},{10,11... | collective-permute-start | bytes 1572872 | tf_op jit(solution)/shard_map/ppermute | solution.py:36
  273.6 9.1 %collective-permute-done.32 = bf16[208,1024]{1,0:T(8,128)(2,1)S(1)} collective-permute-done((bf16[208,1024]{1,0:T(8,128)(2,1)S(1)}, bf16[208,1024]{1,0:T(8,128)(2,1)S(1)}, u32[]{:S(2)}, u32[]{:S(2)}) %collective-permute-start.32) | collective-permute-done | bytes 426016 | tf_op jit(solution)/shard_map/ppermute | solution.py:36
  282.8 5.2 %collective-permute-start.34 = (bf16[416,1024]{1,0:T(8,128)(2,1)S(1)}, bf16[416,1024]{1,0:T(8,128)(2,1)S(1)}, u32[]{:S(2)}, u32[]{:S(2)}) collective-permute-start(bf16[416,1024]{1,0:T(8,128)(2,1)S(1)} %constant_dynamic-update-slice_fusion.mate), channel_id=1, source_target_pairs={{0,1},{1,0},{2,3},{3,2},{4,5},{5,4},{6,7},{7,6},{8,9},{9,8},{10,11... | collective-permute-start | bytes 2555912 | tf_op jit(solution)/shard_map/ppermute | solution.py:36
  289.6 4.3 %collective-permute-done.37 = f32[32,1024]{1,0:T(8,128)S(1)} collective-permute-done((f32[32,1024]{1,0:T(8,128)S(1)}, f32[32,1024]{1,0:T(8,128)S(1)}, u32[]{:S(2)}, u32[]{:S(2)}) %collective-permute-start.37) | collective-permute-done | bytes 131104 | tf_op jit(solution)/shard_map/ppermute | solution.py:36
  294.0 3.8 %collective-permute-done.38 = f32[32,1024]{1,0:T(8,128)S(1)} collective-permute-done((f32[32,1024]{1,0:T(8,128)S(1)}, f32[32,1024]{1,0:T(8,128)S(1)}, u32[]{:S(2)}, u32[]{:S(2)}) %collective-permute-start.38) | collective-permute-done | bytes 131104 | tf_op jit(solution)/shard_map/ppermute | solution.py:36
  299.3 6.7 %collective-permute-done.39 = f32[32,1024]{1,0:T(8,128)S(1)} collective-permute-done((f32[32,1024]{1,0:T(8,128)S(1)}, f32[32,1024]{1,0:T(8,128)S(1)}, u32[]{:S(2)}, u32[]{:S(2)}) %collective-permute-start.39) | collective-permute-done | bytes 131104 | tf_op jit(solution)/shard_map/ppermute | solution.py:36
  306.1 3.8 %place.1 = f32[6158,128]{1,0:T(8,128)} custom-call(s32[32]{0:T(128)S(1)} %pad_add_fusion.2.table, bf16[416,1024]{1,0:T(8,128)(2,1)S(1)} %pad_maximum_fusion.5.own, bf16[416,1024]{1,0:T(8,128)(2,1)S(1)} %constant_dynamic-update-slice_fusion.mate, bf16[416,1024]{1,0:T(8,128)(2,1)S(1)} %collective-permute-done.33.across, ...), custom_call_target="tpu_custom_call" | custom-call | bytes 12000000 | tf_op jit(solution)/shard_map/place/pallas_call | solution.py:639
  (198 shorter events, 68.2 us)
Async XLA Ops:
  0.6 56.5 %collective-permute-start.8 = (bf16[256,1024]{1,0:T(8,128)(2,1)}, bf16[256,1024]{1,0:T(8,128)(2,1)S(1)}, u32[]{:S(2)}, u32[]{:S(2)}) collective-permute-start(bf16[256,1024]{1,0:T(8,128)(2,1)} %bitcast.57), channel_id=1, source_target_pairs={{0,16},{16,0},{1,17},{17,1},{2,18},{18,2},{3,19},{19,3},{4,20},{20... | collective-permute-start | bytes 1572872 | tf_op jit(solution)/shard_map/ppermute | solution.py:36
  2.7 55.8 %collective-permute-start.7 = (bf16[256,1024]{1,0:T(8,128)(2,1)}, bf16[256,1024]{1,0:T(8,128)(2,1)}, u32[]{:S(2)}, u32[]{:S(2)}) collective-permute-start(bf16[256,1024]{1,0:T(8,128)(2,1)} %bitcast.58), channel_id=1, source_target_pairs={{0,1},{1,0},{2,3},{3,2},{4,5},{5,4},{6,7},{7,6},{8,9},{9,8},{10,11... | collective-permute-start | bytes 1572872 | tf_op jit(solution)/shard_map/ppermute | solution.py:36
  3.7 15.7 %collective-permute-start = (s32[1]{0:T(128)}, s32[1]{0:T(128)}, u32[]{:S(2)}, u32[]{:S(2)}) collective-permute-start(s32[1]{0:T(128)} %param.19), channel_id=1, source_target_pairs={{0,16},{16,0},{1,17},{17,1},{2,18},{18,2},{3,19},{19,3},{4,20},{20... | collective-permute-start | bytes 20 | tf_op jit(solution)/shard_map/ppermute | solution.py:36
  3.7 10.9 %collective-permute-start.5 = (s32[1]{0:T(128)}, s32[1]{0:T(128)}, u32[]{:S(2)}, u32[]{:S(2)}) collective-permute-start(s32[1]{0:T(128)} %param.20), channel_id=1, source_target_pairs={{0,16},{16,0},{1,17},{17,1},{2,18},{18,2},{3,19},{19,3},{4,20},{20... | collective-permute-start | bytes 20 | tf_op jit(solution)/shard_map/ppermute | solution.py:36
  5.2 20.7 %collective-permute-start.2 = (bf16[256,1024]{1,0:T(8,128)(2,1)}, bf16[256,1024]{1,0:T(8,128)(2,1)S(1)}, u32[]{:S(2)}, u32[]{:S(2)}) collective-permute-start(bf16[256,1024]{1,0:T(8,128)(2,1)} %bitcast.54), channel_id=1, source_target_pairs={{0,16},{16,0},{1,17},{17,1},{2,18},{18,2},{3,19},{19,3},{4,20},{20... | collective-permute-start | bytes 1572872 | tf_op jit(solution)/shard_map/ppermute | solution.py:36
  14.6 12.5 %collective-permute-start.1 = (bf16[256,1024]{1,0:T(8,128)(2,1)}, bf16[256,1024]{1,0:T(8,128)(2,1)S(1)}, u32[]{:S(2)}, u32[]{:S(2)}) collective-permute-start(bf16[256,1024]{1,0:T(8,128)(2,1)} %bitcast.55), channel_id=1, source_target_pairs={{0,1},{1,0},{2,3},{3,2},{4,5},{5,4},{6,7},{7,6},{8,9},{9,8},{10,11... | collective-permute-start | bytes 1572872 | tf_op jit(solution)/shard_map/ppermute | solution.py:36
  25.9 14.5 %collective-permute-start.3 = (bf16[256,1024]{1,0:T(8,128)(2,1)S(1)}, bf16[256,1024]{1,0:T(8,128)(2,1)S(1)}, u32[]{:S(2)}, u32[]{:S(2)}) collective-permute-start(bf16[256,1024]{1,0:T(8,128)(2,1)S(1)} %collective-permute-done.2), channel_id=1, source_target_pairs={{0,1},{1,0},{2,3},{3,2},{4,5},{5,4},{6,7},{7,6},{8,9},{9,8},{10,11... | collective-permute-start | bytes 1572872 | tf_op jit(solution)/shard_map/ppermute | solution.py:36
  40.3 23.0 %collective-permute-start.4 = (bf16[512,1024]{1,0:T(8,128)(2,1)S(1)}, bf16[512,1024]{1,0:T(8,128)(2,1)}, u32[]{:S(2)}, u32[]{:S(2)}) collective-permute-start(bf16[512,1024]{1,0:T(8,128)(2,1)S(1)} %get-tuple-element.37.pa), channel_id=1, source_target_pairs={{0,1},{1,0},{2,3},{3,2},{4,5},{5,4},{6,7},{7,6},{8,9},{9,8},{10,11... | collective-permute-start | bytes 3145736 | tf_op jit(solution)/shard_map/ppermute | solution.py:36
  86.7 23.7 %collective-permute-start.12 = (bf16[416,1024]{1,0:T(8,128)(2,1)}, bf16[416,1024]{1,0:T(8,128)(2,1)}, u32[]{:S(2)}, u32[]{:S(2)}) collective-permute-start(bf16[416,1024]{1,0:T(8,128)(2,1)} %broadcast_select_fusion.5), channel_id=1, source_target_pairs={{0,2},{2,0},{4,6},{6,4},{8,10},{10,8},{12,14},{14,12},{1,3},{3,1},... | collective-permute-start | bytes 2555912 | tf_op jit(solution)/shard_map/ppermute | solution.py:36
  108.4 29.0 %collective-permute-start.11 = (bf16[1024,1024]{1,0:T(8,128)(2,1)}, bf16[1024,1024]{1,0:T(8,128)(2,1)}, u32[]{:S(2)}, u32[]{:S(2)}) collective-permute-start(bf16[1024,1024]{1,0:T(8,128)(2,1)} %get-tuple-element.45.dh_any), channel_id=1, source_target_pairs={{0,1},{1,0},{2,3},{3,2},{4,5},{5,4},{6,7},{7,6},{8,9},{9,8},{10,11... | collective-permute-start | bytes 6291464 | tf_op jit(solution)/shard_map/ppermute | solution.py:36
  110.3 20.6 %collective-permute-start.14 = (bf16[416,1024]{1,0:T(8,128)(2,1)S(1)}, bf16[416,1024]{1,0:T(8,128)(2,1)S(1)}, u32[]{:S(2)}, u32[]{:S(2)}) collective-permute-start(bf16[416,1024]{1,0:T(8,128)(2,1)S(1)} %broadcast_select_fusion.4), channel_id=1, source_target_pairs={{0,2},{2,0},{4,6},{6,4},{8,10},{10,8},{12,14},{14,12},{1,3},{3,1},... | collective-permute-start | bytes 2555912 | tf_op jit(solution)/shard_map/ppermute | solution.py:36
  112.0 23.5 %collective-permute-start.13 = (bf16[416,1024]{1,0:T(8,128)(2,1)S(1)}, bf16[416,1024]{1,0:T(8,128)(2,1)S(1)}, u32[]{:S(2)}, u32[]{:S(2)}) collective-permute-start(bf16[416,1024]{1,0:T(8,128)(2,1)S(1)} %add_convert_fusion.5), channel_id=1, source_target_pairs={{0,4},{2,6},{8,12},{10,14},{1,5},{3,7},{9,13},{11,15},{16,20},{18,... | collective-permute-start | bytes 2555912 | tf_op jit(solution)/shard_map/ppermute | solution.py:704
  131.4 53.0 %collective-permute-start.23 = (bf16[416,1024]{1,0:T(8,128)(2,1)S(1)}, bf16[416,1024]{1,0:T(8,128)(2,1)}, u32[]{:S(2)}, u32[]{:S(2)}) collective-permute-start(bf16[416,1024]{1,0:T(8,128)(2,1)S(1)} %add_convert_fusion.3), channel_id=1, source_target_pairs={{0,4},{2,6},{12,8},{14,10},{1,5},{3,7},{13,9},{15,11},{16,20},{18,... | collective-permute-start | bytes 2555912 | tf_op jit(solution)/shard_map/ppermute | solution.py:704
  135.8 59.1 %collective-permute-start.25 = (bf16[416,1024]{1,0:T(8,128)(2,1)S(1)}, bf16[416,1024]{1,0:T(8,128)(2,1)}, u32[]{:S(2)}, u32[]{:S(2)}) collective-permute-start(bf16[416,1024]{1,0:T(8,128)(2,1)S(1)} %add_convert_fusion.4), channel_id=1, source_target_pairs={{4,12},{6,14},{5,13},{7,15},{20,28},{22,30},{21,29},{23,31}} | collective-permute-start | bytes 2555912 | tf_op jit(solution)/shard_map/ppermute | solution.py:704
  168.0 15.0 %collective-permute-start.16 = (bf16[208,1024]{1,0:T(8,128)(2,1)S(1)}, bf16[208,1024]{1,0:T(8,128)(2,1)S(1)}, u32[]{:S(2)}, u32[]{:S(2)}) collective-permute-start(bf16[208,1024]{1,0:T(8,128)(2,1)S(1)} %get-tuple-element.66), channel_id=1, source_target_pairs={{0,2},{2,0},{4,6},{6,4},{8,10},{10,8},{12,14},{14,12},{1,3},{3,1},... | collective-permute-start | bytes 1277960 | tf_op jit(solution)/shard_map/ppermute | solution.py:36
  181.0 16.3 %collective-permute-start.15 = (bf16[256,1024]{1,0:T(8,128)(2,1)S(1)}, bf16[256,1024]{1,0:T(8,128)(2,1)S(1)}, u32[]{:S(2)}, u32[]{:S(2)}) collective-permute-start(bf16[256,1024]{1,0:T(8,128)(2,1)S(1)} %get-tuple-element.63), channel_id=1, source_target_pairs={{0,1},{1,0},{2,3},{3,2},{4,5},{5,4},{6,7},{7,6},{8,9},{9,8},{10,11... | collective-permute-start | bytes 1572872 | tf_op jit(solution)/shard_map/ppermute | solution.py:36
  183.0 11.4 %collective-permute-start.17 = (bf16[208,1024]{1,0:T(8,128)(2,1)S(1)}, bf16[208,1024]{1,0:T(8,128)(2,1)S(1)}, u32[]{:S(2)}, u32[]{:S(2)}) collective-permute-start(bf16[208,1024]{1,0:T(8,128)(2,1)S(1)} %get-tuple-element.67), channel_id=1, source_target_pairs={{0,2},{2,0},{4,6},{6,4},{8,10},{10,8},{12,14},{14,12},{1,3},{3,1},... | collective-permute-start | bytes 1277960 | tf_op jit(solution)/shard_map/ppermute | solution.py:36
  185.8 54.6 %collective-permute-start.24 = (bf16[416,1024]{1,0:T(8,128)(2,1)S(1)}, bf16[416,1024]{1,0:T(8,128)(2,1)}, u32[]{:S(2)}, u32[]{:S(2)}) collective-permute-start(bf16[416,1024]{1,0:T(8,128)(2,1)S(1)} %add_convert_fusion.2), channel_id=1, source_target_pairs={{4,8},{6,10},{5,9},{7,11},{20,24},{22,26},{21,25},{23,27}} | collective-permute-start | bytes 2555912 | tf_op jit(solution)/shard_map/ppermute | solution.py:704
  206.7 14.0 %collective-permute-start.21 = (bf16[208,1024]{1,0:T(8,128)(2,1)}, bf16[208,1024]{1,0:T(8,128)(2,1)}, u32[]{:S(2)}, u32[]{:S(2)}) collective-permute-start(bf16[208,1024]{1,0:T(8,128)(2,1)} %get-tuple-element.95), channel_id=1, source_target_pairs={{0,4},{2,6},{12,8},{14,10},{1,5},{3,7},{13,9},{15,11},{16,20},{18,... | collective-permute-start | bytes 1277960 | tf_op jit(solution)/shard_map/ppermute | solution.py:704
  214.2 15.6 %collective-permute-start.29 = (bf16[208,1024]{1,0:T(8,128)(2,1)}, bf16[208,1024]{1,0:T(8,128)(2,1)S(1)}, u32[]{:S(2)}, u32[]{:S(2)}) collective-permute-start(bf16[208,1024]{1,0:T(8,128)(2,1)} %get-tuple-element.96), channel_id=1, source_target_pairs={{0,4},{2,6},{12,8},{14,10},{1,5},{3,7},{13,9},{15,11},{16,20},{18,... | collective-permute-start | bytes 1277960 | tf_op jit(solution)/shard_map/ppermute | solution.py:704
  217.0 13.8 %collective-permute-start.19 = (bf16[208,1024]{1,0:T(8,128)(2,1)S(1)}, bf16[208,1024]{1,0:T(8,128)(2,1)S(1)}, u32[]{:S(2)}, u32[]{:S(2)}) collective-permute-start(bf16[208,1024]{1,0:T(8,128)(2,1)S(1)} %get-tuple-element.97), channel_id=1, source_target_pairs={{4,0},{6,2},{12,8},{14,10},{5,1},{7,3},{13,9},{15,11},{20,16},{22,... | collective-permute-start | bytes 1277960 | tf_op jit(solution)/shard_map/ppermute | solution.py:704
  222.0 23.1 %collective-permute-start.22 = (bf16[208,1024]{1,0:T(8,128)(2,1)S(1)}, bf16[208,1024]{1,0:T(8,128)(2,1)S(1)}, u32[]{:S(2)}, u32[]{:S(2)}) collective-permute-start(bf16[208,1024]{1,0:T(8,128)(2,1)S(1)} %add_convert_fusion.14), channel_id=1, source_target_pairs={{8,4},{10,6},{9,5},{11,7},{24,20},{26,22},{25,21},{27,23}} | collective-permute-start | bytes 1277960 | tf_op jit(solution)/shard_map/ppermute | solution.py:704
  222.7 15.7 %collective-permute-start.27 = (bf16[208,1024]{1,0:T(8,128)(2,1)S(1)}, bf16[208,1024]{1,0:T(8,128)(2,1)S(1)}, u32[]{:S(2)}, u32[]{:S(2)}) collective-permute-start(bf16[208,1024]{1,0:T(8,128)(2,1)S(1)} %get-tuple-element.98), channel_id=1, source_target_pairs={{4,0},{6,2},{12,8},{14,10},{5,1},{7,3},{13,9},{15,11},{20,16},{22,... | collective-permute-start | bytes 1277960 | tf_op jit(solution)/shard_map/ppermute | solution.py:704
  230.0 15.1 %collective-permute-start.30 = (bf16[208,1024]{1,0:T(8,128)(2,1)S(1)}, bf16[208,1024]{1,0:T(8,128)(2,1)S(1)}, u32[]{:S(2)}, u32[]{:S(2)}) collective-permute-start(bf16[208,1024]{1,0:T(8,128)(2,1)S(1)} %add_convert_fusion.8), channel_id=1, source_target_pairs={{8,4},{10,6},{9,5},{11,7},{24,20},{26,22},{25,21},{27,23}} | collective-permute-start | bytes 1277960 | tf_op jit(solution)/shard_map/ppermute | solution.py:704
  230.9 23.9 %collective-permute-start.20 = (bf16[208,1024]{1,0:T(8,128)(2,1)S(1)}, bf16[208,1024]{1,0:T(8,128)(2,1)S(1)}, u32[]{:S(2)}, u32[]{:S(2)}) collective-permute-start(bf16[208,1024]{1,0:T(8,128)(2,1)S(1)} %add_convert_fusion.17), channel_id=1, source_target_pairs={{8,0},{10,2},{9,1},{11,3},{24,16},{26,18},{25,17},{27,19}} | collective-permute-start | bytes 1277960 | tf_op jit(solution)/shard_map/ppermute | solution.py:704
  238.6 25.3 %collective-permute-start.28 = (bf16[208,1024]{1,0:T(8,128)(2,1)S(1)}, bf16[208,1024]{1,0:T(8,128)(2,1)S(1)}, u32[]{:S(2)}, u32[]{:S(2)}) collective-permute-start(bf16[208,1024]{1,0:T(8,128)(2,1)S(1)} %add_convert_fusion.11), channel_id=1, source_target_pairs={{8,0},{10,2},{9,1},{11,3},{24,16},{26,18},{25,17},{27,19}} | collective-permute-start | bytes 1277960 | tf_op jit(solution)/shard_map/ppermute | solution.py:704
  240.4 29.4 %collective-permute-start.35 = (f32[32,1024]{1,0:T(8,128)S(1)}, f32[32,1024]{1,0:T(8,128)S(1)}, u32[]{:S(2)}, u32[]{:S(2)}) collective-permute-start(f32[32,1024]{1,0:T(8,128)S(1)} %pad.8), channel_id=1, source_target_pairs={{0,1},{1,0},{2,3},{3,2},{4,5},{5,4},{6,7},{7,6},{8,9},{9,8},{10,11... | collective-permute-start | bytes 393224 | tf_op jit(solution)/shard_map/ppermute | solution.py:36
  266.4 21.6 %collective-permute-start.10 = (bf16[256,1024]{1,0:T(8,128)(2,1)S(1)}, bf16[256,1024]{1,0:T(8,128)(2,1)S(1)}, u32[]{:S(2)}, u32[]{:S(2)}) collective-permute-start(bf16[256,1024]{1,0:T(8,128)(2,1)S(1)} %copy-done.31), channel_id=1, source_target_pairs={{0,1},{1,0},{2,3},{3,2},{4,5},{5,4},{6,7},{7,6},{8,9},{9,8},{10,11... | collective-permute-start | bytes 1572872 | tf_op jit(solution)/shard_map/ppermute | solution.py:36
  269.5 13.2 %collective-permute-start.32 = (bf16[208,1024]{1,0:T(8,128)(2,1)S(1)}, bf16[208,1024]{1,0:T(8,128)(2,1)S(1)}, u32[]{:S(2)}, u32[]{:S(2)}) collective-permute-start(bf16[208,1024]{1,0:T(8,128)(2,1)S(1)} %get-tuple-element.78), channel_id=1, source_target_pairs={{0,16},{16,0},{1,17},{17,1},{2,18},{18,2},{3,19},{19,3},{4,20},{20... | collective-permute-start | bytes 1277960 | tf_op jit(solution)/shard_map/ppermute | solution.py:36
  269.8 19.1 %collective-permute-start.36 = (f32[32,1024]{1,0:T(8,128)S(1)}, f32[32,1024]{1,0:T(8,128)S(1)}, u32[]{:S(2)}, u32[]{:S(2)}) collective-permute-start(f32[32,1024]{1,0:T(8,128)S(1)} %pad_add_fusion.3), channel_id=1, source_target_pairs={{0,16},{16,0},{1,17},{17,1},{2,18},{18,2},{3,19},{19,3},{4,20},{20... | collective-permute-start | bytes 393224 | tf_op jit(solution)/shard_map/ppermute | solution.py:36
  271.2 34.9 %collective-permute-start.33 = (bf16[416,1024]{1,0:T(8,128)(2,1)S(1)}, bf16[416,1024]{1,0:T(8,128)(2,1)S(1)}, u32[]{:S(2)}, u32[]{:S(2)}) collective-permute-start(bf16[416,1024]{1,0:T(8,128)(2,1)S(1)} %pad_maximum_fusion.5.own), channel_id=1, source_target_pairs={{0,1},{1,0},{2,3},{3,2},{4,5},{5,4},{6,7},{7,6},{8,9},{9,8},{10,11... | collective-permute-start | bytes 2555912 | tf_op jit(solution)/shard_map/ppermute | solution.py:36
  282.8 23.3 %collective-permute-start.34 = (bf16[416,1024]{1,0:T(8,128)(2,1)S(1)}, bf16[416,1024]{1,0:T(8,128)(2,1)S(1)}, u32[]{:S(2)}, u32[]{:S(2)}) collective-permute-start(bf16[416,1024]{1,0:T(8,128)(2,1)S(1)} %constant_dynamic-update-slice_fusion.mate), channel_id=1, source_target_pairs={{0,1},{1,0},{2,3},{3,2},{4,5},{5,4},{6,7},{7,6},{8,9},{9,8},{10,11... | collective-permute-start | bytes 2555912 | tf_op jit(solution)/shard_map/ppermute | solution.py:36
  (40 other events, 334.2 us)

commit v2 on v1

--- a/solution.py
+++ b/solution.py
@@ -60,7 +60,7 @@
     return pl.CostEstimate(flops=int(flops), bytes_accessed=int(moved), transcendentals=0)
 
 
-HBM = pl.BlockSpec(memory_space=pl.ANY)
+HBM = pl.BlockSpec(memory_space=pltpu.HBM)
 SMEM = pl.BlockSpec(memory_space=pltpu.SMEM)
 VMEM = pl.BlockSpec(memory_space=pltpu.VMEM)
 
@@ -82,24 +82,70 @@
     return jnp.where(lax.broadcasted_iota(jnp.int32, scores.shape, 0) < length, scores, -1e30)
 
 
-def attend_kernel(scalars, x_ref, gs_ref, w_qkv, w_out, ht_ref, qkv_ref, att_ref, part_ref, lse_ref, w_buf, o_buf, h_buf, sems):
-    role, length = scalars[0], scalars[1]
+def emit(regions, pieces, target, sems, first):
+    return [
+        pltpu.make_async_copy(
+            pieces[name].at[pl.ds(row, rows), pl.ds(column, columns)],
+            target.at[pl.ds(to_row, rows), pl.ds(to_column, columns)],
+            sems.at[first + i],
+        )
+        for i, (name, row, column, rows, columns, to_row, to_column) in enumerate(regions)
+    ]
+
+
+def wire_copies(plan, inner, pieces, targets, sems, act):
+    for parity in range(2):
+
+        @pl.when(inner == parity)
+        def _():
+            at = to = 0
+            for chunk in plan:
+                for regions in (chunk["regions"][parity], chunk["regions"][1 - parity]):
+                    for each in emit(regions, pieces, targets[to], sems, at):
+                        getattr(each, act)()
+                    at += chunk["most"]
+                    to += 1
+
+
+def plan_shapes(plan, width):
+    return [full((chunk["high"] - chunk["low"], width), BF16) for chunk in plan for _ in range(2)]
+
+
+def plan_sems(plan):
+    return sum(2 * chunk["most"] for chunk in plan)
+
+
+def table_rows(gains_ref, shifts_ref, section, which):
+    return gains_ref[section, which : which + 1, :].astype(F32), shifts_ref[section, which : which + 1, :].astype(F32)
+
+
+def attend_kernel(scalars, facts, own_any, other_any, gains_ref, shifts_ref, w_qkv, w_out, ht_any, qkv_any, att_any, part_any, lse_ref,
+                  x_buf, w_buf, o_buf, h_buf, ht_ref, qkv_ref, att_ref, part_ref, sems):
+    role, length = scalars[0], facts[0]
+    gain, shift = table_rows(gains_ref, shifts_ref, facts[1], 0)
     width, half = w_out.shape[1], w_out.shape[0] // 2
-    rows = x_ref.shape[0] // 2
+    rows = own_any.shape[0]
     col = pl.multiple_of(role * half, LANE)
+    mine, theirs = (pl.ds(pl.multiple_of(r * rows, rows), rows) for r in (role, 1 - role))
     copies = copy_all(
-        [(w_qkv.at[:, pl.ds(i * width + col, half)], w_buf.at[:, pl.ds(i * half, half)]) for i in range(3)]
+        [(own_any, x_buf.at[mine, :]), (other_any, x_buf.at[theirs, :])]
+        + [(w_qkv.at[:, pl.ds(i * width + col, half)], w_buf.at[:, pl.ds(i * half, half)]) for i in range(3)]
         + [(w_out.at[pl.ds(col, half), :], o_buf)],
         sems,
     )
+    copies[0].wait()
+    copies[1].wait()
     for at in range(0, 2 * rows, LANE):
-        unit, _ = norm_stats(x_ref[at : at + LANE, :].astype(F32))
-        hidden = (unit * gs_ref[0:1, :] + gs_ref[1:2, :]).astype(BF16)
+        unit, _ = norm_stats(x_buf[at : at + LANE, :].astype(F32))
+        hidden = (unit * gain + shift).astype(BF16)
         h_buf[at : at + LANE, :] = hidden
         ht_ref[:, at : at + LANE] = hidden.T
+    writes = [pltpu.make_async_copy(s, t, sems.at[6 + i]) for i, (s, t) in enumerate(((ht_ref, ht_any), (qkv_ref, qkv_any), (att_ref, att_any), (part_ref, part_any)))]
+    writes[0].start()
     for i in range(3):
-        copies[i].wait()
+        copies[2 + i].wait()
         qkv_ref[:, i * half : (i + 1) * half] = mm(h_buf[...], w_buf[:, i * half : (i + 1) * half]).astype(BF16)
+    writes[1].start()
 
     def pair(at, carry):
         c = pl.multiple_of(at * LANE, LANE)
@@ -126,23 +172,29 @@
         return carry
 
     lax.fori_loop(0, half // LANE, pair, 0)
-    copies[3].wait()
+    writes[2].start()
+    copies[5].wait()
     part_ref[...] = mm(att_ref[...], o_buf[...]).astype(BF16)
-
-
-def attend(scalars, values, gs, w_qkv, w_out):
-    rows, width = values.shape
+    writes[3].start()
+    for each in writes:
+        each.wait()
+
+
+def attend(scalars, facts, halves, gains, shifts, w_qkv, w_out):
+    rows, width = 2 * halves[0].shape[0], halves[0].shape[1]
     half = width // 2
+    outs = [(width, rows), (rows, 3 * half), (rows, half), (rows, width)]
     return pl.pallas_call(
         attend_kernel,
-        in_specs=[SMEM, VMEM, VMEM, HBM, HBM],
-        out_specs=[VMEM] * 5,
-        out_shape=[full((width, rows), BF16), full((rows, 3 * half), BF16), full((rows, half), BF16), full((rows, width), BF16), full((half // HEAD, rows), F32)],
-        scratch_shapes=[pltpu.VMEM((width, 3 * half), BF16), pltpu.VMEM((half, width), BF16), pltpu.VMEM((rows, width), BF16), pltpu.SemaphoreType.DMA((4,))],
-        compiler_params=params(48),
-        cost_estimate=cost(2 * rows * width * 4 * half * 2, 12e6),
+        in_specs=[SMEM, SMEM, HBM, HBM, VMEM, VMEM, HBM, HBM],
+        out_specs=[HBM] * 4 + [VMEM],
+        out_shape=[full(s, BF16) for s in outs] + [full((half // HEAD, rows), F32)],
+        scratch_shapes=[pltpu.VMEM((rows, width), BF16), pltpu.VMEM((width, 3 * half), BF16), pltpu.VMEM((half, width), BF16), pltpu.VMEM((rows, width), BF16)]
+        + [pltpu.VMEM(s, BF16) for s in outs] + [pltpu.SemaphoreType.DMA((10,))],
+        compiler_params=params(60),
+        cost_estimate=cost(12e9, 8e6),
         name="attend",
-    )(scalars, values, gs, w_qkv, w_out)
+    )(scalars, facts, *halves, gains, shifts, w_qkv, w_out)
 
 
 def unit_copies(w_up, w_down, up_buf, down_buf, first):
@@ -163,38 +215,55 @@
     return up * cdf, slope
 
 
-def own_kernel(scalars, xa, xb, pa, ra, pb, rb, dya, dyb, gs_ref, w_up, w_down,
-               h_ref, gd_ref, gu_ref, act_ref, dup_ref, res_ref,
-               x_buf, p_buf, r_buf, dy_buf, up_buf, down_buf, ht_buf, sems):
-    role, x = scalars[0], scalars[2]
-    rows = xa.shape[0]
+def both_halves(role, rows, pairs):
+    out = []
+    for own, other, buffer, first in pairs:
+        for source, r in ((own, role), (other, 1 - role)):
+            out.append((source, buffer.at[pl.ds(pl.multiple_of(first + r * rows, rows), rows), :]))
+    return out
+
+
+def own_kernel(plan, scalars, facts_a, facts_b, xa, xao, xb, xbo, pa, ra, pb, rb, dya, dyao, dyb, dybo, gains_ref, shifts_ref, w_up, w_down, *refs):
+    h_any, act_any, dup_any, res_any, gu_any = refs[:5]
+    targets = refs[5:-14]
+    x_buf, p_buf, r_buf, dy_buf, up_buf, down_buf, ht_buf, h_ref, gd_ref, gu_ref, act_ref, dup_ref, res_ref, sems = refs[-14:]
+    role, x, inner = scalars[0], scalars[1], scalars[2]
+    half_rows = xa.shape[0]
+    rows = 2 * half_rows
     quarter = up_buf.shape[1]
-    copies = copy_all(
-        [(s, t.at[pl.ds(u * rows, rows), :]) for u, trio in enumerate(((xa, pa, ra), (xb, pb, rb))) for s, t in zip(trio, (x_buf, p_buf, r_buf))]
-        + unit_copies(w_up, w_down, up_buf, down_buf, role + 2 * x)
-        + [(dya, dy_buf.at[pl.ds(0, rows), :]), (dyb, dy_buf.at[pl.ds(rows, rows), :])],
-        sems,
-    )
+    sources = both_halves(role, half_rows, [(xa, xao, x_buf, 0)]) + [(pa, p_buf.at[pl.ds(0, rows), :]), (ra, r_buf.at[pl.ds(0, rows), :])]
+    sources += both_halves(role, half_rows, [(xb, xbo, x_buf, rows)]) + [(pb, p_buf.at[pl.ds(rows, rows), :]), (rb, r_buf.at[pl.ds(rows, rows), :])]
+    sources += unit_copies(w_up, w_down, up_buf, down_buf, role + 2 * x)
+    sources += both_halves(role, half_rows, [(dya, dyao, dy_buf, 0), (dyb, dybo, dy_buf, rows)])
+    copies = copy_all(sources, sems)
+    count = len(sources)
     for u in range(2):
-        for i in range(3):
-            copies[3 * u + i].wait()
+        gain, shift = table_rows(gains_ref, shifts_ref, (facts_a, facts_b)[u][1], 1)
+        for i in range(4):
+            copies[4 * u + i].wait()
 
         def norm(i, carry):
             at = pl.multiple_of(u * rows + i * LANE, LANE)
             here = pl.ds(at, LANE)
             residual = x_buf[here, :].astype(F32) + (p_buf[here, :].astype(F32) + r_buf[here, :].astype(F32))
             unit, _ = norm_stats(residual)
-            hidden = (unit * gs_ref[u, 2:3, :] + gs_ref[u, 3:4, :]).astype(BF16)
+            hidden = (unit * gain + shift).astype(BF16)
             h_ref[here, :] = hidden
             ht_buf[:, here] = hidden.T
             if u == 0:
-                @pl.when(i // (rows // LANE // 2) == role)
+                per = half_rows // LANE
+
+                @pl.when(i // per == role)
                 def _():
-                    res_ref[pl.ds(pl.multiple_of((i % (rows // LANE // 2)) * LANE, LANE), LANE), :] = residual
+                    res_ref[pl.ds(pl.multiple_of((i % per) * LANE, LANE), LANE), :] = residual
+
             return carry
 
         lax.fori_loop(0, rows // LANE, norm, 0)
-    for each in copies[6:]:
+    writes = [pltpu.make_async_copy(s, t, sems.at[count + i]) for i, (s, t) in enumerate(((h_ref, h_any), (res_ref, res_any), (act_ref, act_any), (dup_ref, dup_any), (gu_ref, gu_any)))]
+    writes[0].start()
+    writes[1].start()
+    for each in copies[8:]:
         each.wait()
 
     def block(i, carry):
@@ -209,39 +278,50 @@
         return carry
 
     lax.fori_loop(0, quarter // 256, block, 0)
-
-
-def own_units(scalars, values, parts, came, dys, gs, w_up, w_down):
-    rows, width = values[0].shape
+    pieces = {"d": gd_ref, "u": gu_ref}
+    wire_sems = sems.at[pl.ds(count + 5, plan_sems(plan))]
+    wire_copies(plan, inner, pieces, targets, wire_sems, "start")
+    for each in writes[2:]:
+        each.start()
+    wire_copies(plan, inner, pieces, targets, wire_sems, "wait")
+    for each in writes:
+        each.wait()
+
+
+def own_units(plan, scalars, facts, values, parts, came, dys, gains, shifts, w_up, w_down):
+    rows, width = 2 * values[0].shape[0], values[0].shape[1]
     quarter = w_up.shape[1] // 4
-    count = 6 + 2 * (quarter // LANE) + 2
+    count = 8 + 2 * (quarter // LANE) + 4 + 5 + plan_sems(plan)
     big = lambda *s: pltpu.VMEM(s, BF16)
+    shapes = plan_shapes(plan, width)
     return pl.pallas_call(
-        own_kernel,
-        in_specs=[SMEM] + [HBM] * 8 + [VMEM] + [HBM] * 2,
-        out_specs=[VMEM] * 6,
-        out_shape=[full((2 * rows, width), BF16), full((quarter, width), BF16), full((width, quarter), BF16), full((rows, quarter), BF16), full((2 * rows, quarter), BF16), full((rows // 2, width), F32)],
-        scratch_shapes=[big(2 * rows, width)] * 4 + [big(width, quarter), big(quarter, width), big(width, 2 * rows), pltpu.SemaphoreType.DMA((count,))],
-        compiler_params=params(56),
-        cost_estimate=cost(2 * 2 * rows * width * quarter * 4, 20e6),
+        functools.partial(own_kernel, plan),
+        in_specs=[SMEM] * 3 + [HBM] * 12 + [VMEM] * 2 + [HBM] * 2,
+        out_specs=[HBM] * (5 + len(shapes)),
+        out_shape=[full((2 * rows, width), BF16), full((rows, quarter), BF16), full((2 * rows, quarter), BF16), full((rows // 2, width), F32), full((width, quarter), BF16)] + shapes,
+        scratch_shapes=[big(2 * rows, width)] * 4
+        + [big(width, quarter), big(quarter, width), big(width, 2 * rows), big(2 * rows, width), big(quarter, width), big(width, quarter), big(rows, quarter), big(2 * rows, quarter), pltpu.VMEM((rows // 2, width), F32), pltpu.SemaphoreType.DMA((count,))],
+        compiler_params=params(60),
+        cost_estimate=cost(20e9, 8e6),
         name="own_units",
-    )(scalars, values[0], values[1], parts[0], came[0], parts[1], came[1], dys[0], dys[1], gs, w_up, w_down)
-
-
-def rest_kernel(scalars, h_any, dya, dyb, act_any, dup_any, res_ref, w_up, w_down, dh_ref, keep_ref, send_ref,
+    )(scalars, *facts, *values, parts[0], came[0], parts[1], came[1], *dys, gains, shifts, w_up, w_down)
+
+
+def rest_kernel(scalars, h_any, dya, dyao, dyb, dybo, act_any, dup_any, res_ref, w_up, w_down, dh_ref, keep_ref, send_ref,
                 h_buf, dy_buf, act_own, act_buf, dup_own, dup_buf, up_own, down_own, up_buf, down_buf, sems):
-    role, x = scalars[0], scalars[2]
-    rows = dya.shape[0]
+    role, x = scalars[0], scalars[1]
+    rows = 2 * dya.shape[0]
     quarter = up_buf.shape[1]
     blocks = quarter // LANE
     copies = copy_all(
         [(h_any, h_buf)]
         + unit_copies(w_up, w_down, up_buf, down_buf, role + 2 * (1 - x))
-        + [(dya, dy_buf.at[pl.ds(0, rows), :]), (dyb, dy_buf.at[pl.ds(rows, rows), :]), (act_any, act_own), (dup_any, dup_own)]
+        + both_halves(role, rows // 2, [(dya, dyao, dy_buf, 0), (dyb, dybo, dy_buf, rows)])
+        + [(act_any, act_own), (dup_any, dup_own)]
         + unit_copies(w_up, w_down, up_own, down_own, role + 2 * x),
         sems,
     )
-    first = 1 + 2 * blocks + 2
+    first = 1 + 2 * blocks + 4
     for each in copies[:first]:
         each.wait()
 
@@ -269,20 +349,20 @@
 
 
 def rest_units(scalars, hidden, dys, act, dup, residual, w_up, w_down):
-    rows, width = dys[0].shape
+    rows, width = 2 * dys[0].shape[0], dys[0].shape[1]
     quarter = w_up.shape[1] // 4
-    count = 5 + 4 * (quarter // LANE)
+    count = 7 + 4 * (quarter // LANE)
     big = lambda *s: pltpu.VMEM(s, BF16)
     return pl.pallas_call(
         rest_kernel,
-        in_specs=[SMEM] + [HBM] * 5 + [VMEM] + [HBM] * 2,
+        in_specs=[SMEM] + [HBM] * 7 + [VMEM] + [HBM] * 2,
         out_specs=[VMEM] * 3,
         out_shape=[full((2 * rows, width), BF16), full((rows // 2, width), F32), full((rows // 2, width), BF16)],
         scratch_shapes=[big(2 * rows, width)] * 2 + [big(rows, quarter)] * 2 + [big(2 * rows, quarter)] * 2 + [big(width, quarter), big(quarter, width)] * 2 + [pltpu.SemaphoreType.DMA((count,))],
-        compiler_params=params(56),
-        cost_estimate=cost(2 * 2 * rows * width * quarter * 5, 24e6),
+        compiler_params=params(60),
+        cost_estimate=cost(20e9, 8e6),
         name="rest_units",
-    )(scalars, hidden, dys[0], dys[1], act, dup, residual, w_up, w_down)
+    )(scalars, hidden, *dys, act, dup, residual, w_up, w_down)
 
 
 def pair_back(qkv, lse, datt, c, c_d, rows, half, length):
@@ -317,61 +397,108 @@
     return dq, dk, dv
 
 
-def back_kernel(scalars, xa, xb, pa, ra, pb, rb, dh_any, dhr_any, dya, dyb, gs_ref, w_out, att_a, att_b, qkv_a, qkv_b, lse_a, lse_b, ht_a, ht_b,
-                gq_ref, go_ref, dr_ref, vec_ref, datt_ref, dqa_ref,
-                x_buf, p_buf, r_buf, dh_buf, dhr_buf, dy_buf, da_buf, o_buf, datt_buf, att_buf, qkv_buf, ht_buf, dq_buf, sems):
-    role, x = scalars[0], scalars[2]
-    rows2, width = xa.shape
-    rows, half = rows2 // 2, width // 2
+def turn_kernel(plan, scalars, facts_a, facts_b, xa, xao, xb, xbo, pa, ra, pb, rb, dh_any, dhr_any, dya, dyao, dyb, dybo, gains_ref, shifts_ref, w_out, att_a, att_b, gu_any, *refs):
+    dr_any, vec_ref, datt_any, go_any = refs[:4]
+    targets = refs[4:-14]
+    x_buf, p_buf, r_buf, dh_buf, dhr_buf, dy_buf, da_buf, o_buf, datt_buf, att_buf, gu_buf, dr_ref, go_ref, sems = refs[-14:]
+    role, x, inner = scalars[0], scalars[1], scalars[2]
+    rows, width = xa.shape
+    rows2, half = 2 * rows, width // 2
     quarter = half // 2
     own = pl.multiple_of(x * quarter, LANE)
     col = pl.multiple_of(role * half, LANE)
-    lse = (lse_a, lse_b)
     pairs = []
-    for u, (xs, ps, rs, dys) in enumerate(((xa, pa, ra, dya), (xb, pb, rb, dyb))):
+    for u, (xs, xo, ps, rs, dys, dyo) in enumerate(((xa, xao, pa, ra, dya, dyao), (xb, xbo, pb, rb, dyb, dybo))):
         here = pl.ds(u * rows2, rows2)
-        pairs += [(xs, x_buf.at[here, :]), (ps, p_buf.at[here, :]), (rs, r_buf.at[here, :]), (dys, dy_buf.at[here, :]),
-                  (dh_any.at[here, :], dh_buf.at[here, :]), (dhr_any.at[here, :], dhr_buf.at[here, :])]
+        pairs += both_halves(role, rows, [(xs, xo, x_buf, u * rows2), (dys, dyo, dy_buf, u * rows2)])
+        pairs += [(ps, p_buf.at[here, :]), (rs, r_buf.at[here, :]), (dh_any.at[here, :], dh_buf.at[here, :]), (dhr_any.at[here, :], dhr_buf.at[here, :])]
     pairs.append((w_out.at[pl.ds(col, half), :], o_buf))
-    for u, (a, q, h) in enumerate(((att_a, qkv_a, ht_a), (att_b, qkv_b, ht_b))):
-        here = pl.ds(u * rows2, rows2)
-        pairs += [(q, qkv_buf.at[here, :]), (a.at[:, pl.ds(own, quarter)], att_buf.at[here, :]), (h, ht_buf.at[:, here])]
+    for u, a in enumerate((att_a, att_b)):
+        pairs.append((a.at[:, pl.ds(own, quarter)], att_buf.at[pl.ds(u * rows2, rows2), :]))
+    pairs.append((gu_any, gu_buf))
     copies = copy_all(pairs, sems)
+    count = len(pairs)
     vec_ref[...] = jnp.zeros_like(vec_ref)
     for u in range(2):
-        for i in range(6):
-            copies[6 * u + i].wait()
+        gain, _ = table_rows(gains_ref, shifts_ref, (facts_a, facts_b)[u][1], 1)
+        for i in range(8):
+            copies[8 * u + i].wait()
 
         def norm(i, carry):
             here = pl.ds(pl.multiple_of(u * rows2 + i * LANE, LANE), LANE)
             residual = x_buf[here, :].astype(F32) + (p_buf[here, :].astype(F32) + r_buf[here, :].astype(F32))
             unit, rstd = norm_stats(residual)
             dh2 = dh_buf[here, :].astype(F32) + dhr_buf[here, :].astype(F32)
-            grad = dy_buf[here, :].astype(F32) + norm_back(unit, rstd, gs_ref[u, 2:3, :], dh2)
+            grad = dy_buf[here, :].astype(F32) + norm_back(unit, rstd, gain, dh2)
             da_buf[here, :] = grad.astype(BF16)
             if u == 0:
                 per = rows // LANE
+
                 @pl.when(i // per == role)
                 def _():
                     dr_ref[pl.ds(pl.multiple_of((i % per) * LANE, LANE), LANE), :] = grad
                     vec_ref[0:1, :] += jnp.sum(dh2 * unit, axis=0, keepdims=True)
                     vec_ref[1:2, :] += jnp.sum(dh2, axis=0, keepdims=True)
+
             return carry
 
         lax.fori_loop(0, rows2 // LANE, norm, 0)
-        if u == 0:
-            copies[12].wait()
-            datt_buf[:rows2, :] = mm_nt(da_buf[:rows2, :], o_buf[...]).astype(BF16)
-            datt_ref[...] = datt_buf[:rows2, :]
-        else:
-            mine = o_buf[pl.ds(pl.multiple_of(x * quarter, quarter), quarter), :]
-            datt_buf[rows2:, pl.ds(own, quarter)] = mm_nt(da_buf[rows2:, :], mine).astype(BF16)
-    for each in copies[13:]:
+    writes = [pltpu.make_async_copy(s, t, sems.at[count + i]) for i, (s, t) in enumerate(((dr_ref, dr_any), (go_ref, go_any), (datt_buf, datt_any)))]
+    writes[0].start()
+    for each in copies[16:]:
         each.wait()
     go_ref[...] = mm_tn(att_buf[...], da_buf[...]).astype(BF16)
+    writes[1].start()
+    wire_sems = sems.at[pl.ds(count + 3, max(1, plan_sems(plan)))]
+    wire_copies(plan, inner, {"o": go_ref, "u": gu_buf}, targets, wire_sems, "start")
+    datt_buf[...] = mm_nt(da_buf[...], o_buf[...]).astype(BF16)
+    writes[2].start()
+    wire_copies(plan, inner, {"o": go_ref, "u": gu_buf}, targets, wire_sems, "wait")
+    for each in writes:
+        each.wait()
+
+
+def turn(plan, scalars, facts, values, parts, came, dh, dh_came, dys, gains, shifts, w_out, atts, grad_up):
+    rows2, width = 2 * values[0].shape[0], values[0].shape[1]
+    half = width // 2
+    big = lambda *s: pltpu.VMEM(s, BF16)
+    tokens = 2 * rows2
+    shapes = plan_shapes(plan, width)
+    return pl.pallas_call(
+        functools.partial(turn_kernel, plan),
+        in_specs=[SMEM] * 3 + [HBM] * 14 + [VMEM] * 2 + [HBM] * 4,
+        out_specs=[HBM, VMEM, HBM, HBM] + [HBM] * len(shapes),
+        out_shape=[full((rows2 // 2, width), F32), full((8, width), F32), full((tokens, half), BF16), full((half // 2, width), BF16)] + shapes,
+        scratch_shapes=[big(tokens, width)] * 7
+        + [big(half, width), big(tokens, half), big(tokens, half // 2), big(*grad_up.shape), pltpu.VMEM((rows2 // 2, width), F32), big(half // 2, width), pltpu.SemaphoreType.DMA((23 + max(1, plan_sems(plan)),))],
+        compiler_params=params(60),
+        cost_estimate=cost(12e9, 8e6),
+        name="turn",
+    )(scalars, *facts, *values, parts[0], came[0], parts[1], came[1], dh, dh_came, *dys, gains, shifts, w_out, *atts, grad_up)
+
+
+def back_kernel(plan, scalars, facts_a, facts_b, datt_any, qkv_a, qkv_b, ht_a, ht_b, go_any, lse_a, lse_b, *refs):
+    dqa_any = refs[0]
+    targets = refs[1:-7]
+    datt_buf, qkv_buf, ht_buf, dq_buf, gq_ref, go_buf, sems = refs[-7:]
+    x, inner = scalars[1], scalars[2]
+    tokens, half = datt_any.shape
+    rows2 = tokens // 2
+    rows, quarter = rows2 // 2, half // 2
+    own = pl.multiple_of(x * quarter, LANE)
+    lse = (lse_a, lse_b)
+    first_half, second_half = pl.ds(0, rows2), pl.ds(rows2, rows2)
+    pairs = []
+    for here, q in ((first_half, qkv_a), (second_half, qkv_b)):
+        pairs += [(q, qkv_buf.at[here, :]), (datt_any.at[here, :], datt_buf.at[here, :])]
+    pairs += [(ht_a, ht_buf.at[:, first_half]), (ht_b, ht_buf.at[:, second_half]), (go_any, go_buf)]
+    copies = copy_all(pairs, sems)
+    count = len(pairs)
     for u in range(2):
+        copies[2 * u].wait()
+        copies[2 * u + 1].wait()
         base = u * rows2
-        length = scalars[1] if u == 0 else scalars[3]
+        length = (facts_a, facts_b)[u][0]
 
         def one(at, carry):
             c = pl.multiple_of(own + at * LANE, LANE)
@@ -385,32 +512,40 @@
             return carry
 
         lax.fori_loop(0, quarter // LANE, one, 0)
-    dqa_ref[...] = dq_buf[:rows2, :]
+    write = pltpu.make_async_copy(dq_buf.at[first_half, :], dqa_any, sems.at[count])
+    write.start()
+    for each in copies[4:]:
+        each.wait()
     for i in range(3):
         cols = slice(i * quarter, (i + 1) * quarter)
         gq_ref[:, cols] = mm(ht_buf[...], dq_buf[:, cols]).astype(BF16)
-
-
-def back(scalars, values, parts, came, dh, dh_came, dys, gs, w_out, atts, qkvs, lses, hts):
-    rows2, width = values[0].shape
-    half = width // 2
+    pieces = {"q": gq_ref, "o": go_buf}
+    wire_sems = sems.at[pl.ds(count + 1, plan_sems(plan))]
+    wire_copies(plan, inner, pieces, targets, wire_sems, "start")
+    wire_copies(plan, inner, pieces, targets, wire_sems, "wait")
+    write.wait()
+
+
+def back(plan, scalars, facts, datt, qkvs, hts, grad_out, lses):
+    tokens, half = datt.shape
+    width = 2 * half
     big = lambda *s: pltpu.VMEM(s, BF16)
-    tokens = 2 * rows2
+    shapes = plan_shapes(plan, width)
     return pl.pallas_call(
-        back_kernel,
-        in_specs=[SMEM] + [HBM] * 10 + [VMEM] + [HBM] * 5 + [VMEM] * 2 + [HBM] * 2,
-        out_specs=[VMEM] * 6,
-        out_shape=[full((width, 3 * half // 2), BF16), full((half // 2, width), BF16), full((rows2 // 2, width), F32), full((8, width), F32), full((rows2, half), BF16), full((rows2, 3 * half // 2), BF16)],
-        scratch_shapes=[big(tokens, width)] * 7 + [big(half, width), big(tokens, half), big(tokens, half // 2), big(tokens, 3 * half), big(width, tokens), big(tokens, 3 * half // 2), pltpu.SemaphoreType.DMA((19,))],
-        compiler_params=params(56),
-        cost_estimate=cost(15e9, 24e6),
+        functools.partial(back_kernel, plan),
+        in_specs=[SMEM] * 3 + [HBM] * 6 + [VMEM] * 2,
+        out_specs=[HBM] * (1 + len(shapes)),
+        out_shape=[full((tokens // 2, 3 * half // 2), BF16)] + shapes,
+        scratch_shapes=[big(tokens, half), big(tokens, 3 * half), big(width, tokens), big(tokens, 3 * half // 2), big(width, 3 * half // 2), big(*grad_out.shape), pltpu.SemaphoreType.DMA((8 + plan_sems(plan),))],
+        compiler_params=params(60),
+        cost_estimate=cost(14e9, 8e6),
         name="back",
-    )(scalars, values[0], values[1], parts[0], came[0], parts[1], came[1], dh, dh_came, dys[0], dys[1], gs, w_out, atts[0], atts[1], qkvs[0], qkvs[1], lses[0], lses[1], hts[0], hts[1])
-
-
-def last_kernel(scalars, qkv_ref, lse_ref, datt_ref, dqa_ref, w_qkv, keep_ref, send_ref, w_own, w_buf, dq_buf, sems):
-    role, x, length = scalars[0], scalars[2], scalars[1]
-    rows2, half = datt_ref.shape
+    )(scalars, *facts, datt, *qkvs, *hts, grad_out, *lses)
+
+
+def last_kernel(scalars, facts, qkv_ref, lse_ref, datt_ref, dqa_ref, w_qkv, keep_ref, send_ref, w_own, w_buf, dq_buf, sems):
+    role, x, length = scalars[0], scalars[1], facts[0]
+    rows2, half = qkv_ref.shape[0], datt_ref.shape[1]
     rows, quarter, width = rows2 // 2, half // 2, 2 * half
     mine = pl.multiple_of(x * quarter, LANE)
     other = pl.multiple_of((1 - x) * quarter, LANE)
@@ -440,20 +575,20 @@
     send_ref[...] = (mm_nt(dqa_ref[send, :], w_own[...]) + mm_nt(dq_buf[send, :], w_buf[...])).astype(BF16)
 
 
-def last(scalars, qkv, lse, datt, dqa, w_qkv):
-    rows2, half = datt.shape
+def last(scalars, facts, qkv, lse, datt, dqa, w_qkv):
+    rows2, half = qkv.shape[0], datt.shape[1]
     width = 2 * half
     big = lambda *s: pltpu.VMEM(s, BF16)
     return pl.pallas_call(
         last_kernel,
-        in_specs=[SMEM] + [VMEM] * 4 + [HBM],
+        in_specs=[SMEM] * 2 + [VMEM] * 4 + [HBM],
         out_specs=[VMEM] * 2,
         out_shape=[full((rows2 // 2, width), F32), full((rows2 // 2, width), BF16)],
         scratch_shapes=[big(width, 3 * half // 2)] * 2 + [big(rows2, 3 * half // 2), pltpu.SemaphoreType.DMA((6,))],
-        compiler_params=params(48),
-        cost_estimate=cost(5e9, 10e6),
+        compiler_params=params(60),
+        cost_estimate=cost(7e9, 8e6),
         name="last",
-    )(scalars, qkv, lse, datt, dqa, w_qkv)
+    )(scalars, facts, qkv, lse, datt, dqa, w_qkv)
 
 
 class Layout:
@@ -507,23 +642,48 @@
             rows.append(entry + [0] * (24 - len(entry)))
         return np.asarray(rows, np.int32)
 
-    def wire(self, member, pieces):
-        out = []
+    def regions(self, member, low, high):
+        found = []
+
+        def cut(name, row, column, rows, columns, to_row, to_column):
+            first, last = max(to_row, low), min(to_row + rows, high)
+            if first < last:
+                found.append((name, row + first - to_row, column, last - first, columns, first - low, to_column))
+
         for p in self.segments[member]:
-            piece = pieces[p["name"]][p["low"] : p["high"]]
             if p["name"] == "q":
-                n1 = p["wire"]
-                n2 = p["high"] - p["low"] - n1
-                quarter = piece.shape[1] // 3
-                side = [piece[n1:, i * quarter : (i + 1) * quarter] for i in range(3)]
-                if n1 > 3 * n2:
-                    side.append(jnp.zeros((n1 - 3 * n2, quarter), BF16))
-                piece = jnp.concatenate([piece[:n1], jnp.concatenate(side, 0)], 1)
-            out.append(piece)
-        short = self.rows - sum(o.shape[0] for o in out)
-        if short:
-            out.append(jnp.zeros((short, self.width), BF16))
-        return jnp.concatenate(out, 0) if len(out) > 1 else out[0]
+                quarter = self.width // 4
+                side = p["high"] - p["low"] - p["wire"]
+                cut("q", p["low"], 0, p["wire"], 3 * quarter, p["at"], 0)
+                for i in range(3):
+                    cut("q", p["low"] + p["wire"], i * quarter, side, quarter, p["at"] + i * side, 3 * quarter)
+            else:
+                cut(p["name"], p["low"], 0, p["wire"], self.width, p["at"], 0)
+        return found
+
+    def plans(self):
+        stage_of = {"u": 0, "d": 0, "o": 1, "q": 2}
+        stages = ([], [], [])
+        for block in reversed(range(self.members // 2)):
+            edges = {0, self.rows}
+            for member in (2 * block, 2 * block + 1):
+                for p in self.segments[member]:
+                    edges |= {p["at"], p["at"] + p["wire"]}
+            edges = sorted(edges)
+            runs = []
+            for low, high in zip(edges, edges[1:]):
+                found = [stage_of[f[0]] for member in (2 * block, 2 * block + 1) for f in self.regions(member, low, high)]
+                stage = max(found) if found else runs[-1][2]
+                if runs and (runs[-1][2] == stage or 2 in (stage, runs[-1][2])):
+                    runs[-1][1], runs[-1][2] = high, max(stage, runs[-1][2])
+                else:
+                    runs.append([low, high, stage])
+            for low, high, stage in runs:
+                middle = low + (high - low) // 32 * 16
+                for first, last in [(low, middle), (middle, high)] if stage == 2 else [(low, high)]:
+                    regions = [self.regions(2 * block + i, first, last) for i in range(2)]
+                    stages[stage].append({"block": block, "low": first, "high": last, "regions": regions, "most": max(map(len, regions))})
+        return stages
 
 
 def after(value, *first):
@@ -545,7 +705,8 @@
     return pairs
 
 
-def place_kernel(spans, table, own, mate, across, diagonal, small_ref, out_ref, wire, flat, sems):
+def place_kernel(spans, table, *refs):
+    quad, (small_ref, out_ref, wire, flat, sems) = refs[:-5], refs[-5:]
     me, unit0 = table[24], table[0]
     units = out_ref.shape[0]
     width = wire.shape[2]
@@ -553,7 +714,13 @@
     front = 512
     x, role = me // 2, me % 2
     where = (me, role + 2 * (1 - x), (1 - role) + 2 * x, (1 - role) + 2 * (1 - x))
-    copies = copy_all([(source, wire.at[at]) for source, at in zip((own, mate, across, diagonal), where)], sems.at[pl.ds(0, 4)])
+    per_piece = len(quad) // 4
+    pairs = []
+    for i, source in enumerate(quad):
+        rows = source.shape[0]
+        first = sum(s.shape[0] for s in quad[i // per_piece * per_piece : i])
+        pairs.append((source, wire.at[where[i // per_piece], pl.ds(first, rows), :]))
+    copies = copy_all(pairs, sems.at[pl.ds(1, len(pairs))])
     for each in copies:
         each.wait()
 
@@ -628,129 +795,154 @@
             for h in range(chunks):
                 flat[pl.ds(front + tail + g * 8 * chunks + h, 8, stride=chunks), :] = small_ref[g * 8 : (g + 1) * 8, h * LANE : (h + 1) * LANE]
 
-    done = pltpu.make_async_copy(flat.at[pl.ds(front, units), :], out_ref, sems.at[4])
+    done = pltpu.make_async_copy(flat.at[pl.ds(front, units), :], out_ref, sems.at[0])
     done.start()
     done.wait()
 
 
 def place(layout, table, quad, small):
-    rows, width = quad[0].shape
+    rows, width = layout.rows, layout.width
     units = layout.share // 2 // LANE
+    quad = [part for piece in quad for part in piece]
     return pl.pallas_call(
         functools.partial(place_kernel, layout.spans),
-        in_specs=[SMEM] + [HBM] * 4 + [VMEM],
+        in_specs=[SMEM] + [HBM] * len(quad) + [VMEM],
         out_specs=HBM,
         out_shape=full((units, LANE), F32),
-        scratch_shapes=[pltpu.VMEM((4, rows, width), BF16), pltpu.VMEM((-(-units // 8) * 8 + 1024, LANE), F32), pltpu.SemaphoreType.DMA((5,))],
-        compiler_params=params(32),
-        cost_estimate=cost(0, 12e6),
+        scratch_shapes=[pltpu.VMEM((4, rows, width), BF16), pltpu.VMEM((-(-units // 8) * 8 + 1024, LANE), F32), pltpu.SemaphoreType.DMA((1 + len(quad),))],
+        compiler_params=params(60),
+        cost_estimate=cost(4e9, 8e6),
         name="place",
     )(table, *quad, small)
 
 
 def local(frames, cotangent, w_qkv, w_out, w_up, w_down, gains, shifts, prompt_len, section):
-    rows, width = frames.shape[2], frames.shape[3]
-    ff, sections = w_up.shape[1], gains.shape[0]
+    width, ff, sections = frames.shape[3], w_up.shape[1], gains.shape[0]
     role, group, member = lax.axis_index("role"), lax.axis_index("group"), lax.axis_index("member")
     x = group % 2
     members, groups = lax.axis_size("member"), lax.axis_size("group")
     layout = Layout(width, ff, sections, members)
+    early, middle, late = layout.plans()
     outer, inner = member // 2, member % 2
     count = members // 2
 
-    def whole(own):
-        other = swap(own, "role")
-        return jnp.concatenate([jnp.where(role == 0, own, other), jnp.where(role == 0, other, own)], 0)
-
     own_frames, own_cot = frames[0, 0], cotangent[0, 0]
-    values = [whole(own_frames), whole(swap(own_frames, "group"))]
-    dys = [whole(own_cot), whole(swap(own_cot, "group"))]
-    lengths = [prompt_len[0], swap(prompt_len, "group")[0]]
-    section_ids = [section[0], swap(section, "group")[0]]
-
-    def rows_of(table, at):
-        return lax.dynamic_slice(table, (at, 0, 0), (1, 2, width))[0].astype(F32)
-
-    gs = []
-    for at in section_ids:
-        gain, shift = rows_of(gains, at), rows_of(shifts, at)
-        gs.append(jnp.stack([gain[0], shift[0], gain[1], shift[1]]))
-    both_gs = jnp.stack(gs)
-    scalars = jnp.stack([role, lengths[0], x, lengths[1]]).astype(jnp.int32)
-    scalars_b = jnp.stack([role, lengths[1], x, lengths[0]]).astype(jnp.int32)
-
-    totals, pieces = {}, {}
-    early, late = [], []
-    for block in reversed(range(count)):
-        names = {p["name"] for m in (2 * block, 2 * block + 1) for p in layout.segments[m]}
-        (early if names <= {"u", "d"} else late).append(block)
-    halves = lambda value: [value[: layout.rows // 32 * 16], value[layout.rows // 32 * 16 :]]
-    sent = []
-
-    def exchange(block, cut):
-        even, odd = layout.wire(2 * block, pieces), layout.wire(2 * block + 1, pieces)
-        keep = jnp.where(inner == 0, even, odd)
-        send = jnp.where(inner == 0, odd, even)
-        totals[block] = []
-        for k, s in zip(cut(keep), cut(send)):
-            if sent:
-                s = after(s, sent[-1])
-            sent.append(swap(s, "member"))
-            totals[block].append(add(k, sent[-1]))
+    values = [own_frames, swap(own_frames, "role")]
+    mate_frames = swap(own_frames, "group")
+    facts = jnp.concatenate([prompt_len, section])
+    mate_facts = swap(facts, "group")
+    scalars = jnp.stack([role, x, inner]).astype(jnp.int32)
 
     levels = count.bit_length() - 1
-
-    def climb(block, level):
-        totals[block] = [add(t, lax.ppermute(t, "member", tree_pairs(block, level, count))) for t in totals[block]]
-
-    hts, qkvs, atts, parts, lses = zip(*(attend(s, v, g, w_qkv, w_out) for s, v, g in zip((scalars, scalars_b), values, gs)))
-    came = [swap(part, "role") for part in parts]
-    hidden, pieces["d"], pieces["u"], act, dup, residual = own_units(scalars, values, parts, came, dys, both_gs, w_up, w_down)
-    for block in early:
-        exchange(block, lambda value: [value])
+    chunks = []
+
+    def exchange(plan, arrays, *first):
+        for i, chunk in enumerate(plan):
+            keep, send = arrays[2 * i], arrays[2 * i + 1]
+            chunks.append(dict(chunk, total=keep, came=swap(after(send, *first) if first else send, "member"), level=0))
+
+    def climb(chunk):
+        chunk["came"] = lax.ppermute(chunk["total"], "member", tree_pairs(chunk["block"], chunk["level"], count))
+        chunk["level"] += 1
+
+    def settle(chunk, *first):
+        total = after(chunk["total"], *first) if first else chunk["total"]
+        chunk["total"] = add(total, chunk["came"])
+
+    first = attend(scalars, facts, values[:2], gains, shifts, w_qkv, w_out)
+    mate_facts, mate_frames = after(mate_facts, first[3]), after(mate_frames, first[3])
+    both = (facts, mate_facts)
+    values += [mate_frames, swap(mate_frames, "role")]
+    own_cot = after(own_cot, mate_frames)
+    mate_cot = swap(own_cot, "group")
+    dys = [own_cot, swap(own_cot, "role"), mate_cot, swap(mate_cot, "role")]
+    second = attend(scalars, mate_facts, values[2:], gains, shifts, w_qkv, w_out)
+    hts, qkvs, atts, parts, lses = zip(first, second)
+    came = [after(swap(parts[0], "role"), parts[1]), swap(parts[1], "role")]
+    hidden, act, dup, residual, grad_up, *wires = own_units(early, scalars, both, values, parts, came, dys, gains, shifts, w_up, w_down)
+    exchange(early, wires)
     dh, out_keep, out_send = rest_units(scalars, hidden, dys, act, dup, residual, w_up, w_down)
     output = (out_keep + swap(out_send, "role").astype(F32)).astype(BF16)
-    dh_came = swap(dh, "role")
-    if early:
-        dh_came = after(dh_came, *totals[early[0]])
-    pieces["q"], pieces["o"], dr1, vec_two, datt, dqa = back(scalars, values, parts, came, dh, dh_came, dys, both_gs, w_out, atts, qkvs, lses, hts)
-    for block in late:
-        exchange(block, halves)
-    if early:
-        climb(early[0], 0)
-        datt = after(datt, *totals[early[0]], *totals[early[1 % len(early)]])
-    dh1_keep, dh1_send = last(scalars, qkvs[0], lses[0], datt, dqa, w_qkv)
+    dh_came = swap(after(dh, chunks[0]["came"]), "role")
+    settle(chunks[0], dh)
+    climb(chunks[0])
+    dr1, vec_two, datt, grad_out, *wires = turn(middle, scalars, both, values, parts, came, dh, dh_came, dys, gains, shifts, w_out, atts, grad_up)
+    exchange(middle, wires)
+    second_chunk = chunks[min(1, len(early) - 1)]
+    if second_chunk is not chunks[0]:
+        settle(second_chunk, datt)
+        climb(second_chunk)
+    dqa, *wires = back(late, scalars, both, after(datt, second_chunk["total"]), qkvs, hts, grad_out, lses)
+    for chunk in chunks[: min(2, len(early))]:
+        settle(chunk, dqa)
+    exchange(late, wires, *(chunk["came"] for chunk in chunks[len(early) :]))
+    dh1_keep, dh1_send = last(scalars, facts, qkvs[0], lses[0], after(datt, *(c["came"] for c in chunks[len(early) : -len(late)])), dqa, w_qkv)
+    dh1_send = after(dh1_send, chunks[-len(late)]["came"])
     dh1 = dh1_keep + swap(dh1_send, "role").astype(F32)
     unit, rstd = norm_stats(own_frames.astype(F32))
-    input_grad = dr1 + norm_back(unit, rstd, gs[0][0:1], dh1)
+    input_grad = dr1 + norm_back(unit, rstd, lax.dynamic_slice(gains, (facts[1], 0, 0), (1, 1, width))[0].astype(F32), dh1)
 
     vectors = jnp.stack([jnp.stack([jnp.sum(dh1 * unit, 0), vec_two[0]]), jnp.stack([jnp.sum(dh1, 0), vec_two[1]])])
-    select = (jnp.arange(sections, dtype=jnp.int32) == section_ids[0]).astype(F32)
+    select = (jnp.arange(sections, dtype=jnp.int32) == facts[1]).astype(F32)
     small = select[None, :, None, None] * vectors[:, None]
     small = jnp.pad(small.reshape(4 * sections, width), ((0, -4 * sections % 8), (0, 0)))
+    small_steps = []
     for axis in ("role", "group", "member"):
         distance = 1
         while distance < lax.axis_size(axis):
             small = small + swap(small, axis, distance)
+            small_steps.append(small)
             distance *= 2
 
-    for block in early + late:
-        for level in range(1 if early and block == early[0] else 0, levels):
-            climb(block, level)
-    finals = None
-    for block in early + late:
-        here = totals[block] if len(totals[block]) == 2 else halves(totals[block][0])
-        finals = here if finals is None else [jnp.where(outer == block, h, f) for h, f in zip(here, finals)]
-    distance = 2
-    while distance < groups:
-        finals = [add(f, swap(f, "group", distance)) for f in finals]
-        distance *= 2
-    mates = [swap(f, "group") for f in finals]
-    own, mate = jnp.concatenate(finals, 0), jnp.concatenate(mates, 0)
-    quad = [own, mate, swap(own, "role"), swap(mate, "role")]
+    for chunk in chunks[min(2, len(early)) :]:
+        settle(chunk, dqa)
+    joined = chunks[: min(2, len(early))]
+    for chunk in chunks[min(2, len(early)) :]:
+        before = joined[-1]
+        mates = [c for c in joined if c["block"] == chunk["block"] and chunk["high"] == c["low"] and c["level"] == 0]
+        mates += [c for c in joined if c["block"] == chunk["block"] and chunk["low"] == c["high"] and c["level"] == 0]
+        if mates and chunk not in chunks[-len(late) :]:
+            mate = mates[0]
+            ends = sorted((mate, chunk), key=lambda c: c["low"])
+            mate["total"] = jnp.concatenate([c["total"] for c in ends], 0)
+            mate["low"], mate["high"] = ends[0]["low"], ends[1]["high"]
+        else:
+            joined.append(chunk)
+    chunks = joined
+    for chunk in chunks:
+        if chunk["level"] == 0:
+            climb(chunk)
+            settle(chunk)
+    for level in range(1, levels):
+        for chunk in chunks:
+            if level == levels - 1 and chunk in chunks[-2:]:
+                chunk["total"] = after(chunk["total"], small_steps[-3 if chunk is chunks[-2] else -2])
+            climb(chunk)
+            settle(chunk)
+    edges = [0, layout.rows // 32 * 16, layout.rows]
+    quads = [[], [], [], []]
+    for low, high in zip(edges, edges[1:]):
+        final = jnp.zeros((high - low, width), BF16)
+        for chunk in chunks:
+            first, past = max(low, chunk["low"]), min(high, chunk["high"])
+            if first >= past:
+                continue
+            here = chunk["total"][first - chunk["low"] : past - chunk["low"]]
+            mine = outer == chunk["block"]
+            part = jnp.where(mine, here, final[first - low : past - low])
+            final = jnp.concatenate([final[: first - low], part, final[past - low :]], 0)
+        distance = 2
+        while distance < groups:
+            final = add(final, swap(final, "group", distance))
+            distance *= 2
+        if high == layout.rows:
+            final = after(final, small)
+        mate = swap(final, "group")
+        for into, value in zip(quads, (final, mate, swap(final, "role"), swap(mate, "role"))):
+            into.append(value)
     table = lax.dynamic_slice(jnp.asarray(layout.table()), (2 * member + role, 0), (1, 24))[0]
     table = jnp.concatenate([table, (role + 2 * x)[None].astype(jnp.int32), jnp.zeros((7,), jnp.int32)])
-    shard = place(layout, table, quad, small).reshape(-1)
+    shard = place(layout, table, quads, small).reshape(-1)
     return output[None, None], input_grad[None, None], shard
 
 

time: 315 us -> 252 us (0.80); the launches traced: 310 us -> 251 us
  waiting for transfers between devices: 102 us -> 51.6 us
  Pallas kernels: 93.6 us -> 105 us
  other arithmetic: 39 us -> 28.4 us
  local copies, waits for them, and re-layouts: 15.4 us -> 7.36 us
    ppermute x12 -> x10, waiting for transfers between devices: 33.4 us -> 8.13 us  [climb(): lax.ppermute(chunk['total'], 'member', tree_pairs(chunk['block'], chunk['...]
    ppermute x28 -> x29, waiting for transfers between devices: 68.1 us -> 43.5 us  [swap(): return lax.ppermute(value, axis, [(i, i ^ distance) for i in range(count)])]
    select_n x9 -> x1, other arithmetic: 18.8 us -> 1.21 us  [local(): part = jnp.where(mine, here, final[first - low:past - low])]
    pallas_call x6 -> x7, Pallas kernels: 89.8 us -> 99.9 us  [the longest x2 26.2 us: attend(): pl.pallas_call(attend_kernel, in_specs=[SMEM, SMEM, HBM, HBM, VMEM, VMEM,...]
    convert_element_type x12 -> x14, other arithmetic: 11.8 us -> 18.4 us  [add(): return (left.astype(F32) + right.astype(F32)).astype(BF16)]
    slice x15 -> x0, local copies, waits for them, and re-layouts: 6.4 us -> none  [the longest x2 2.22 us: wire(): piece = jnp.concatenate([piece[:n1], jnp.concatenate(side, 0)], 1)]
    ppermute x12 -> x10, starting transfers between devices: 26.3 us -> 23.2 us  [climb(): lax.ppermute(chunk['total'], 'member', tree_pairs(chunk['block'], chunk['...]
    ppermute x28 -> x29, starting transfers between devices: 29.6 us -> 32.1 us  [swap(): return lax.ppermute(value, axis, [(i, i ^ distance) for i in range(count)])]
  transfers between devices with their start and end apart: 40 -> 39, of which waited for: 16 -> 12; matrix products, arithmetic and copies ran while one was open for 14% -> 12% of each run, Pallas kernels for 23% -> 31%
where the time goes in v2:
time: 252 us; the launch traced here: 251 us
  Pallas kernels  105 us (42%)
  starting transfers between devices  55.3 us (22%)
  waiting for transfers between devices  51.6 us (20%)
  other arithmetic  28.4 us (11%)
  local copies, waits for them, and re-layouts  7.36 us (3%)
  between operations  2.69 us (1%)
    ppermute x29, waiting for transfers between devices, swap(): return lax.ppermute(value, axis, [(i, i ^ distance) for i in range(count)])  43.5 us
    ppermute x29, starting transfers between devices, swap(): return lax.ppermute(value, axis, [(i, i ^ distance) for i in range(count)])  32.1 us
    pallas_call x2, Pallas kernels, attend(): pl.pallas_call(attend_kernel, in_specs=[SMEM, SMEM, HBM, HBM, VMEM, VMEM,...  26.2 us
    ppermute x10, starting transfers between devices, climb(): lax.ppermute(chunk['total'], 'member', tree_pairs(chunk['block'], chunk['...  23.2 us
    pallas_call x1, Pallas kernels, own_units(): pl.pallas_call(functools.partial(own_kernel, plan), in_specs=[SMEM] * 3 +...  21.4 us
    pallas_call x1, Pallas kernels, rest_units(): pl.pallas_call(rest_kernel, in_specs=[SMEM] + [HBM] * 7 + [VMEM] + [HBM]...  19.5 us
    convert_element_type x14, other arithmetic, add(): return (left.astype(F32) + right.astype(F32)).astype(BF16)  18.4 us
    pallas_call x1, Pallas kernels, back(): pl.pallas_call(functools.partial(back_kernel, plan), in_specs=[SMEM] * 3...  12.9 us
  transfers between devices with their start and end apart: 39, of which 12 were waited for; matrix products, arithmetic and copies ran while one was open for 12% of the time, Pallas kernels for 31%

profile of v2, /device:TPU:1, one launch (start us, length us, event | category | flops | bytes accessed | tf_op | source)
XLA Modules:
  0.0 250.6 jit_solution(2371393114806668143)
XLA Ops:
  0.8 2.7 %collective-permute-start.2 = (bf16[256,1024]{1,0:T(8,128)(2,1)}, bf16[256,1024]{1,0:T(8,128)(2,1)S(1)}, u32[]{:S(2)}, u32[]{:S(2)}) collective-permute-start(bf16[256,1024]{1,0:T(8,128)(2,1)} %bitcast.31), channel_id=1, source_target_pairs={{0,16},{16,0},{1,17},{17,1},{2,18},{18,2},{3,19},{19,3},{4,20},{20... | collective-permute-start | bytes 1572872 | tf_op jit(solution)/shard_map/ppermute | solution.py:36
  6.8 13.1 %attend.2 = (bf16[1024,512]{1,0:T(8,128)(2,1)}, bf16[512,1536]{1,0:T(8,128)(2,1)}, bf16[512,512]{1,0:T(8,128)(2,1)}, bf16[512,1024]{1,0:T(8,128)(2,1)}, f32[8,512]{1,0:T(8,128)}) custom-call(s32[3]{0:T(128)} %pad_add_fusion.scalars, s32[2]{0:T(128)} %pad_add_fusion.1.facts.facts_a, bf16[256,1024]{1,0:T(8,128)(2,1)} %bitcast.32, ...), custom_call_target="tpu_custom_call" | custom-call | flops 12000000000 | bytes 8000000 | tf_op jit(solution)/shard_map/attend/pallas_call | solution.py:187
  20.8 2.0 collective-permute-done.facts.facts_b
  24.0 13.1 %attend.3 = (bf16[1024,512]{1,0:T(8,128)(2,1)}, bf16[512,1536]{1,0:T(8,128)(2,1)}, bf16[512,512]{1,0:T(8,128)(2,1)}, bf16[512,1024]{1,0:T(8,128)(2,1)}, f32[8,512]{1,0:T(8,128)}) custom-call(s32[3]{0:T(128)} %pad_add_fusion.scalars, s32[2]{0:T(128)} %copy-done.27, bf16[256,1024]{1,0:T(8,128)(2,1)} %copy-done.18, bf16[256,1024]{1,0:T(8,128)(2,1)} %copy-done.19, ...), custom_call_target="tpu_custom_call" | custom-call | flops 12000000000 | bytes 8000000 | tf_op jit(solution)/shard_map/attend/pallas_call | solution.py:187
  39.0 3.1 %collective-permute-done.6.dyao = bf16[256,1024]{1,0:T(8,128)(2,1)S(1)} collective-permute-done((bf16[256,1024]{1,0:T(8,128)(2,1)S(1)}, bf16[256,1024]{1,0:T(8,128)(2,1)S(1)}, u32[]{:S(2)}, u32[]{:S(2)}) %collective-permute-start.6) | collective-permute-done | bytes 524320 | tf_op jit(solution)/shard_map/ppermute | solution.py:36
  44.3 21.4 %own_units.1 = (bf16[1024,1024]{1,0:T(8,128)(2,1)}, bf16[512,1024]{1,0:T(8,128)(2,1)}, bf16[1024,1024]{1,0:T(8,128)(2,1)}, f32[256,1024]{1,0:T(8,128)}, bf16[102...) custom-call(s32[3]{0:T(128)} %pad_add_fusion.scalars, ...), custom_call_target="tpu_custom_call" | custom-call | flops 20000000000 | bytes 8000000 | tf_op jit(solution)/shard_map/own_units/pallas_call | solution.py:297
  67.1 19.5 %rest_units.1 = (bf16[1024,1024]{1,0:T(8,128)(2,1)}, f32[256,1024]{1,0:T(8,128)}, bf16[256,1024]{1,0:T(8,128)(2,1)}) custom-call(s32[3]{0:T(128)} %pad_add_fusion.scalars, bf16[1024,1024]{1,0:T(8,128)(2,1)} %get-tuple-element.67.h_any, bf16[256,1024]{1,0:T(8,128)(2,1)} %bitcast.40, bf16[256,1024]{1,0:T(8,128)(2,1)} %copy-done.20, ...), custom_call_target="tpu_custom_call" | custom-call | flops 20000000000 | bytes 8000000 | tf_op jit(solution)/shard_map/rest_units/pallas_call | solution.py:356
  90.5 4.2 %collective-permute-start.26 = (bf16[416,1024]{1,0:T(8,128)(2,1)S(1)}, bf16[416,1024]{1,0:T(8,128)(2,1)}, u32[]{:S(2)}, u32[]{:S(2)}) collective-permute-start(bf16[416,1024]{1,0:T(8,128)(2,1)S(1)} %add_convert_fusion.2), channel_id=1, source_target_pairs={{0,4},{2,6},{8,12},{10,14},{1,5},{3,7},{9,13},{11,15},{16,20},{18,... | collective-permute-start | bytes 2555912 | tf_op jit(solution)/shard_map/ppermute | solution.py:845
  94.8 11.3 %turn.1 = (f32[256,1024]{1,0:T(8,128)}, f32[8,1024]{1,0:T(8,128)}, bf16[1024,512]{1,0:T(8,128)(2,1)}, bf16[256,1024]{1,0:T(8,128)(2,1)}, bf16[256,1024]{1,0:T(8,128)(2,1)}, /*index=5*/bf16[256,1024]{1,0:T(8,128)(2,1)}) custom-call(s32[3]{0:T(128)} %pad_add_fusion.scalars, s32[2]{0:T(128)} %pad_add_fusion.1.facts.facts_a, s32[2]{0:T(128)} %copy-done.27, ...), custom_call_target="tpu_custom_call" | custom-call | flops 12000000000 | bytes 8000000 | tf_op jit(solution)/shard_map/turn/pallas_call | solution.py:467
  106.0 3.6 %collective-permute-done.13 = bf16[416,1024]{1,0:T(8,128)(2,1)} collective-permute-done((bf16[416,1024]{1,0:T(8,128)(2,1)}, bf16[416,1024]{1,0:T(8,128)(2,1)}, u32[]{:S(2)}, u32[]{:S(2)}) %collective-permute-start.13) | collective-permute-done | bytes 852000 | tf_op jit(solution)/shard_map/ppermute | solution.py:36
  112.5 12.9 %back.1 = (bf16[512,768]{1,0:T(8,128)(2,1)}, bf16[208,1024]{1,0:T(8,128)(2,1)}, bf16[208,1024]{1,0:T(8,128)(2,1)}, bf16[208,1024]{1,0:T(8,128)(2,1)}, bf16[208,1024]{1,0:T(8,128)(2,1)}) custom-call(s32[3]{0:T(128)} %pad_add_fusion.scalars, s32[2]{0:T(128)} %pad_add_fusion.1.facts.facts_a, s32[2]{0:T(128)} %copy-done.27, ...), custom_call_target="tpu_custom_call" | custom-call | flops 14000000000 | bytes 8000000 | tf_op jit(solution)/shard_map/back/pallas_call | solution.py:534
  127.0 3.3 %collective-permute-start.24 = (bf16[416,1024]{1,0:T(8,128)(2,1)S(1)}, bf16[416,1024]{1,0:T(8,128)(2,1)S(1)}, u32[]{:S(2)}, u32[]{:S(2)}) collective-permute-start(bf16[416,1024]{1,0:T(8,128)(2,1)S(1)} %add_convert_fusion.7), channel_id=1, source_target_pairs={{0,4},{2,6},{12,8},{14,10},{1,5},{3,7},{13,9},{15,11},{16,20},{18,... | collective-permute-start | bytes 2555912 | tf_op jit(solution)/shard_map/ppermute | solution.py:845
  130.2 1.6 collective-permute-start.27
  136.3 6.6 %collective-permute-start.22 = (bf16[416,1024]{1,0:T(8,128)(2,1)}, bf16[416,1024]{1,0:T(8,128)(2,1)}, u32[]{:S(2)}, u32[]{:S(2)}) collective-permute-start(bf16[416,1024]{1,0:T(8,128)(2,1)} %pad_maximum_fusion), channel_id=1, source_target_pairs={{0,4},{2,6},{12,8},{14,10},{1,5},{3,7},{13,9},{15,11},{16,20},{18,... | collective-permute-start | bytes 2555912 | tf_op jit(solution)/shard_map/ppermute | solution.py:845
  144.1 8.6 %last.1 = (f32[256,1024]{1,0:T(8,128)}, bf16[256,1024]{1,0:T(8,128)(2,1)}) custom-call(s32[3]{0:T(128)} %pad_add_fusion.scalars, s32[2]{0:T(128)} %pad_add_fusion.1.facts.facts_a, bf16[512,1536]{1,0:T(8,128)(2,1)} %get-tuple-element.80.qkv_a.qkv_ref, f32[8,512]{1,0:T(8,128)} %get-tuple-element.81.lse_a.lse_ref, ...), custom_call_target="tpu_custom_call" | custom-call | flops 7000000000 | bytes 8000000 | tf_op jit(solution)/shard_map/last/pallas_call | solution.py:582
  152.8 2.9 %collective-permute-start.15 = (bf16[256,1024]{1,0:T(8,128)(2,1)}, bf16[256,1024]{1,0:T(8,128)(2,1)S(1)}, u32[]{:S(2)}, u32[]{:S(2)}) collective-permute-start(bf16[256,1024]{1,0:T(8,128)(2,1)} %get-tuple-element.99), channel_id=1, source_target_pairs={{0,1},{1,0},{2,3},{3,2},{4,5},{5,4},{6,7},{7,6},{8,9},{9,8},{10,11... | collective-permute-start | bytes 1572872 | tf_op jit(solution)/shard_map/ppermute | solution.py:36
  156.9 1.7 collective-permute-start.25
  158.6 2.0 add_convert_fusion.15
  161.9 1.9 add_convert_fusion.12
  166.1 1.6 collective-permute-start.17
  172.7 2.5 %collective-permute-done.18 = f32[32,1024]{1,0:T(8,128)S(1)} collective-permute-done((f32[32,1024]{1,0:T(8,128)S(1)}, f32[32,1024]{1,0:T(8,128)S(1)}, u32[]{:S(2)}, u32[]{:S(2)}) %collective-permute-start.18) | collective-permute-done | bytes 131104 | tf_op jit(solution)/shard_map/ppermute | solution.py:36
  177.5 3.5 %collective-permute-done.19 = f32[32,1024]{1,0:T(8,128)S(1)} collective-permute-done((f32[32,1024]{1,0:T(8,128)S(1)}, f32[32,1024]{1,0:T(8,128)S(1)}, u32[]{:S(2)}, u32[]{:S(2)}) %collective-permute-start.19) | collective-permute-done | bytes 131104 | tf_op jit(solution)/shard_map/ppermute | solution.py:36
  181.0 3.8 %collective-permute-start.30 = (f32[32,1024]{1,0:T(8,128)S(1)}, f32[32,1024]{1,0:T(8,128)S(1)}, u32[]{:S(2)}, u32[]{:S(2)}) collective-permute-start(f32[32,1024]{1,0:T(8,128)S(1)} %add.121), channel_id=1, source_target_pairs={{0,4},{2,6},{4,0},{6,2},{8,12},{10,14},{12,8},{14,10},{1,5},{3,7},... | collective-permute-start | bytes 393224 | tf_op jit(solution)/shard_map/ppermute | solution.py:36
  188.0 2.9 %collective-permute-start.32 = (f32[32,1024]{1,0:T(8,128)S(1)}, f32[32,1024]{1,0:T(8,128)S(1)}, u32[]{:S(2)}, u32[]{:S(2)}) collective-permute-start(f32[32,1024]{1,0:T(8,128)S(1)} %add.134), channel_id=1, source_target_pairs={{0,8},{2,10},{4,12},{6,14},{8,0},{10,2},{12,4},{14,6},{1,9},{3,11}... | collective-permute-start | bytes 393224 | tf_op jit(solution)/shard_map/ppermute | solution.py:36
  192.1 1.7 add_convert_fusion.3
  193.8 15.9 %collective-permute-done.32 = f32[32,1024]{1,0:T(8,128)S(1)} collective-permute-done((f32[32,1024]{1,0:T(8,128)S(1)}, f32[32,1024]{1,0:T(8,128)S(1)}, u32[]{:S(2)}, u32[]{:S(2)}) %collective-permute-start.32) | collective-permute-done | bytes 131104 | tf_op jit(solution)/shard_map/ppermute | solution.py:36
  210.7 8.1 %collective-permute-done.31 = bf16[208,1024]{1,0:T(8,128)(2,1)S(1)} collective-permute-done((bf16[208,1024]{1,0:T(8,128)(2,1)S(1)}, bf16[208,1024]{1,0:T(8,128)(2,1)S(1)}, u32[]{:S(2)}, u32[]{:S(2)}) %collective-permute-start.31) | collective-permute-done | bytes 426016 | tf_op jit(solution)/shard_map/ppermute | solution.py:845
  222.8 2.0 fusion.12
  225.9 5.2 %collective-permute-done.34.refs_3_ = bf16[208,1024]{1,0:T(8,128)(2,1)} collective-permute-done((bf16[208,1024]{1,0:T(8,128)(2,1)}, bf16[208,1024]{1,0:T(8,128)(2,1)}, u32[]{:S(2)}, u32[]{:S(2)}) %collective-permute-start.34) | collective-permute-done | bytes 426016 | tf_op jit(solution)/shard_map/ppermute | solution.py:36
  231.1 2.5 collective-permute-start.38
  233.6 6.6 %collective-permute-done.33.refs_2_ = bf16[208,1024]{1,0:T(8,128)(2,1)} collective-permute-done((bf16[208,1024]{1,0:T(8,128)(2,1)}, bf16[208,1024]{1,0:T(8,128)(2,1)}, u32[]{:S(2)}, u32[]{:S(2)}) %collective-permute-start.33) | collective-permute-done | bytes 426016 | tf_op jit(solution)/shard_map/ppermute | solution.py:36
  245.0 5.5 %place.1 = f32[6158,128]{1,0:T(8,128)} custom-call(s32[32]{0:T(128)} %pad_add_fusion.2.table, bf16[208,1024]{1,0:T(8,128)(2,1)} %get-tuple-element.124.refs_0_, bf16[208,1024]{1,0:T(8,128)(2,1)} %get-tuple-element.118.refs_1_, bf16[208,1024]{1,0:T(8,128)(2,1)} %collective-permute-done.33.refs_2_, bf16[208,1024]{1,0:T(8,128)(2,1)} %collective-permute-done.34.refs_3_, ...), custom_call_target="tpu_custom_call" | custom-call | flops 4000000000 | bytes 8000000 | tf_op jit(solution)/shard_map/place/pallas_call | solution.py:807
  (155 shorter events, 50.7 us)
Async XLA Ops:
  0.6 5.4 %collective-permute-start.1 = (bf16[256,1024]{1,0:T(8,128)(2,1)}, bf16[256,1024]{1,0:T(8,128)(2,1)S(1)}, u32[]{:S(2)}, u32[]{:S(2)}) collective-permute-start(bf16[256,1024]{1,0:T(8,128)(2,1)} %bitcast.30), channel_id=1, source_target_pairs={{0,1},{1,0},{2,3},{3,2},{4,5},{5,4},{6,7},{7,6},{8,9},{9,8},{10,11... | collective-permute-start | bytes 1572872 | tf_op jit(solution)/shard_map/ppermute | solution.py:36
  0.8 19.1 %collective-permute-start.2 = (bf16[256,1024]{1,0:T(8,128)(2,1)}, bf16[256,1024]{1,0:T(8,128)(2,1)S(1)}, u32[]{:S(2)}, u32[]{:S(2)}) collective-permute-start(bf16[256,1024]{1,0:T(8,128)(2,1)} %bitcast.31), channel_id=1, source_target_pairs={{0,16},{16,0},{1,17},{17,1},{2,18},{18,2},{3,19},{19,3},{4,20},{20... | collective-permute-start | bytes 1572872 | tf_op jit(solution)/shard_map/ppermute | solution.py:36
  20.3 18.7 %collective-permute-start.4 = (bf16[512,1024]{1,0:T(8,128)(2,1)}, bf16[512,1024]{1,0:T(8,128)(2,1)S(1)}, u32[]{:S(2)}, u32[]{:S(2)}) collective-permute-start(bf16[512,1024]{1,0:T(8,128)(2,1)} %get-tuple-element.61.pa), channel_id=1, source_target_pairs={{0,1},{1,0},{2,3},{3,2},{4,5},{5,4},{6,7},{7,6},{8,9},{9,8},{10,11... | collective-permute-start | bytes 3145736 | tf_op jit(solution)/shard_map/ppermute | solution.py:36
  22.7 15.8 %collective-permute-start.7 = (bf16[256,1024]{1,0:T(8,128)(2,1)S(1)}, bf16[256,1024]{1,0:T(8,128)(2,1)}, u32[]{:S(2)}, u32[]{:S(2)}) collective-permute-start(bf16[256,1024]{1,0:T(8,128)(2,1)S(1)} %bitcast.42), channel_id=1, source_target_pairs={{0,16},{16,0},{1,17},{17,1},{2,18},{18,2},{3,19},{19,3},{4,20},{20... | collective-permute-start | bytes 1572872 | tf_op jit(solution)/shard_map/ppermute | solution.py:36
  37.1 5.4 %collective-permute-start.5 = (bf16[512,1024]{1,0:T(8,128)(2,1)}, bf16[512,1024]{1,0:T(8,128)(2,1)S(1)}, u32[]{:S(2)}, u32[]{:S(2)}) collective-permute-start(bf16[512,1024]{1,0:T(8,128)(2,1)} %get-tuple-element.64.pb), channel_id=1, source_target_pairs={{0,1},{1,0},{2,3},{3,2},{4,5},{5,4},{6,7},{7,6},{8,9},{9,8},{10,11... | collective-permute-start | bytes 3145736 | tf_op jit(solution)/shard_map/ppermute | solution.py:36
  65.7 20.8 %collective-permute-start.10 = (bf16[416,1024]{1,0:T(8,128)(2,1)}, bf16[416,1024]{1,0:T(8,128)(2,1)S(1)}, u32[]{:S(2)}, u32[]{:S(2)}) collective-permute-start(bf16[416,1024]{1,0:T(8,128)(2,1)} %get-tuple-element.74), channel_id=1, source_target_pairs={{0,2},{2,0},{4,6},{6,4},{8,10},{10,8},{12,14},{14,12},{1,3},{3,1},... | collective-permute-start | bytes 2555912 | tf_op jit(solution)/shard_map/ppermute | solution.py:36
  86.5 8.2 %collective-permute-start.11 = (bf16[1024,1024]{1,0:T(8,128)(2,1)}, bf16[1024,1024]{1,0:T(8,128)(2,1)}, u32[]{:S(2)}, u32[]{:S(2)}) collective-permute-start(bf16[1024,1024]{1,0:T(8,128)(2,1)} %get-tuple-element.75.dh_any), channel_id=1, source_target_pairs={{0,1},{1,0},{2,3},{3,2},{4,5},{5,4},{6,7},{7,6},{8,9},{9,8},{10,11... | collective-permute-start | bytes 6291464 | tf_op jit(solution)/shard_map/ppermute | solution.py:36
  88.7 21.0 %collective-permute-start.13 = (bf16[416,1024]{1,0:T(8,128)(2,1)}, bf16[416,1024]{1,0:T(8,128)(2,1)}, u32[]{:S(2)}, u32[]{:S(2)}) collective-permute-start(bf16[416,1024]{1,0:T(8,128)(2,1)} %get-tuple-element.87), channel_id=1, source_target_pairs={{0,2},{2,0},{4,6},{6,4},{8,10},{10,8},{12,14},{14,12},{1,3},{3,1},... | collective-permute-start | bytes 2555912 | tf_op jit(solution)/shard_map/ppermute | solution.py:36
  90.0 42.6 %collective-permute-start.21 = (bf16[160,1024]{1,0:T(8,128)(2,1)}, bf16[160,1024]{1,0:T(8,128)(2,1)}, u32[]{:S(2)}, u32[]{:S(2)}) collective-permute-start(bf16[160,1024]{1,0:T(8,128)(2,1)} %get-tuple-element.108), channel_id=1, source_target_pairs={{0,2},{2,0},{4,6},{6,4},{8,10},{10,8},{12,14},{14,12},{1,3},{3,1},... | collective-permute-start | bytes 983048 | tf_op jit(solution)/shard_map/ppermute | solution.py:36
  90.5 34.9 %collective-permute-start.26 = (bf16[416,1024]{1,0:T(8,128)(2,1)S(1)}, bf16[416,1024]{1,0:T(8,128)(2,1)}, u32[]{:S(2)}, u32[]{:S(2)}) collective-permute-start(bf16[416,1024]{1,0:T(8,128)(2,1)S(1)} %add_convert_fusion.2), channel_id=1, source_target_pairs={{0,4},{2,6},{8,12},{10,14},{1,5},{3,7},{9,13},{11,15},{16,20},{18,... | collective-permute-start | bytes 2555912 | tf_op jit(solution)/shard_map/ppermute | solution.py:845
  111.1 22.7 %collective-permute-start.12 = (bf16[256,1024]{1,0:T(8,128)(2,1)}, bf16[256,1024]{1,0:T(8,128)(2,1)}, u32[]{:S(2)}, u32[]{:S(2)}) collective-permute-start(bf16[256,1024]{1,0:T(8,128)(2,1)} %get-tuple-element.83), channel_id=1, source_target_pairs={{0,2},{2,0},{4,6},{6,4},{8,10},{10,8},{12,14},{14,12},{1,3},{3,1},... | collective-permute-start | bytes 1572872 | tf_op jit(solution)/shard_map/ppermute | solution.py:36
  127.0 28.7 %collective-permute-start.24 = (bf16[416,1024]{1,0:T(8,128)(2,1)S(1)}, bf16[416,1024]{1,0:T(8,128)(2,1)S(1)}, u32[]{:S(2)}, u32[]{:S(2)}) collective-permute-start(bf16[416,1024]{1,0:T(8,128)(2,1)S(1)} %add_convert_fusion.7), channel_id=1, source_target_pairs={{0,4},{2,6},{12,8},{14,10},{1,5},{3,7},{13,9},{15,11},{16,20},{18,... | collective-permute-start | bytes 2555912 | tf_op jit(solution)/shard_map/ppermute | solution.py:845
  130.2 39.7 %collective-permute-start.27 = (bf16[416,1024]{1,0:T(8,128)(2,1)S(1)}, bf16[416,1024]{1,0:T(8,128)(2,1)}, u32[]{:S(2)}, u32[]{:S(2)}) collective-permute-start(bf16[416,1024]{1,0:T(8,128)(2,1)S(1)} %add_convert_fusion.1), channel_id=1, source_target_pairs={{4,12},{6,14},{5,13},{7,15},{20,28},{22,30},{21,29},{23,31}} | collective-permute-start | bytes 2555912 | tf_op jit(solution)/shard_map/ppermute | solution.py:845
  133.8 18.9 %collective-permute-start.14 = (bf16[208,1024]{1,0:T(8,128)(2,1)}, bf16[208,1024]{1,0:T(8,128)(2,1)S(1)}, u32[]{:S(2)}, u32[]{:S(2)}) collective-permute-start(bf16[208,1024]{1,0:T(8,128)(2,1)} %get-tuple-element.98), channel_id=1, source_target_pairs={{0,2},{2,0},{4,6},{6,4},{8,10},{10,8},{12,14},{14,12},{1,3},{3,1},... | collective-permute-start | bytes 1277960 | tf_op jit(solution)/shard_map/ppermute | solution.py:36
  136.3 29.8 %collective-permute-start.22 = (bf16[416,1024]{1,0:T(8,128)(2,1)}, bf16[416,1024]{1,0:T(8,128)(2,1)}, u32[]{:S(2)}, u32[]{:S(2)}) collective-permute-start(bf16[416,1024]{1,0:T(8,128)(2,1)} %pad_maximum_fusion), channel_id=1, source_target_pairs={{0,4},{2,6},{12,8},{14,10},{1,5},{3,7},{13,9},{15,11},{16,20},{18,... | collective-permute-start | bytes 2555912 | tf_op jit(solution)/shard_map/ppermute | solution.py:845
  142.8 17.8 %collective-permute-start.28 = (bf16[208,1024]{1,0:T(8,128)(2,1)}, bf16[208,1024]{1,0:T(8,128)(2,1)}, u32[]{:S(2)}, u32[]{:S(2)}) collective-permute-start(bf16[208,1024]{1,0:T(8,128)(2,1)} %get-tuple-element.116), channel_id=1, source_target_pairs={{0,2},{2,0},{4,6},{6,4},{8,10},{10,8},{12,14},{14,12},{1,3},{3,1},... | collective-permute-start | bytes 1277960 | tf_op jit(solution)/shard_map/ppermute | solution.py:36
  152.8 11.1 %collective-permute-start.15 = (bf16[256,1024]{1,0:T(8,128)(2,1)}, bf16[256,1024]{1,0:T(8,128)(2,1)S(1)}, u32[]{:S(2)}, u32[]{:S(2)}) collective-permute-start(bf16[256,1024]{1,0:T(8,128)(2,1)} %get-tuple-element.99), channel_id=1, source_target_pairs={{0,1},{1,0},{2,3},{3,2},{4,5},{5,4},{6,7},{7,6},{8,9},{9,8},{10,11... | collective-permute-start | bytes 1572872 | tf_op jit(solution)/shard_map/ppermute | solution.py:36
  156.9 33.9 %collective-permute-start.25 = (bf16[416,1024]{1,0:T(8,128)(2,1)}, bf16[416,1024]{1,0:T(8,128)(2,1)}, u32[]{:S(2)}, u32[]{:S(2)}) collective-permute-start(bf16[416,1024]{1,0:T(8,128)(2,1)} %add_convert_fusion.4), channel_id=1, source_target_pairs={{4,8},{6,10},{5,9},{7,11},{20,24},{22,26},{21,25},{23,27}} | collective-permute-start | bytes 2555912 | tf_op jit(solution)/shard_map/ppermute | solution.py:845
  160.6 15.3 %collective-permute-start.16 = (bf16[208,1024]{1,0:T(8,128)(2,1)}, bf16[208,1024]{1,0:T(8,128)(2,1)}, u32[]{:S(2)}, u32[]{:S(2)}) collective-permute-start(bf16[208,1024]{1,0:T(8,128)(2,1)} %add_convert_fusion.15), channel_id=1, source_target_pairs={{4,0},{6,2},{12,8},{14,10},{5,1},{7,3},{13,9},{15,11},{20,16},{22,... | collective-permute-start | bytes 1277960 | tf_op jit(solution)/shard_map/ppermute | solution.py:845
  163.9 21.0 %collective-permute-start.29 = (bf16[208,1024]{1,0:T(8,128)(2,1)}, bf16[208,1024]{1,0:T(8,128)(2,1)}, u32[]{:S(2)}, u32[]{:S(2)}) collective-permute-start(bf16[208,1024]{1,0:T(8,128)(2,1)} %add_convert_fusion.12), channel_id=1, source_target_pairs={{4,0},{6,2},{12,8},{14,10},{5,1},{7,3},{13,9},{15,11},{20,16},{22,... | collective-permute-start | bytes 1277960 | tf_op jit(solution)/shard_map/ppermute | solution.py:845
  169.2 41.2 %collective-permute-start.23 = (bf16[416,1024]{1,0:T(8,128)(2,1)S(1)}, bf16[416,1024]{1,0:T(8,128)(2,1)S(1)}, u32[]{:S(2)}, u32[]{:S(2)}) collective-permute-start(bf16[416,1024]{1,0:T(8,128)(2,1)S(1)} %add_convert_fusion.6), channel_id=1, source_target_pairs={{8,4},{10,6},{9,5},{11,7},{24,20},{26,22},{25,21},{27,23}} | collective-permute-start | bytes 2555912 | tf_op jit(solution)/shard_map/ppermute | solution.py:845
  169.9 5.3 %collective-permute-start.18 = (f32[32,1024]{1,0:T(8,128)S(1)}, f32[32,1024]{1,0:T(8,128)S(1)}, u32[]{:S(2)}, u32[]{:S(2)}) collective-permute-start(f32[32,1024]{1,0:T(8,128)S(1)} %pad_add_fusion.3), channel_id=1, source_target_pairs={{0,16},{16,0},{1,17},{17,1},{2,18},{18,2},{3,19},{19,3},{4,20},{20... | collective-permute-start | bytes 393224 | tf_op jit(solution)/shard_map/ppermute | solution.py:36
  175.2 47.6 %collective-permute-start.9 = (bf16[256,1024]{1,0:T(8,128)(2,1)}, bf16[256,1024]{1,0:T(8,128)(2,1)}, u32[]{:S(2)}, u32[]{:S(2)}) collective-permute-start(bf16[256,1024]{1,0:T(8,128)(2,1)} %get-tuple-element.72), channel_id=1, source_target_pairs={{0,1},{1,0},{2,3},{3,2},{4,5},{5,4},{6,7},{7,6},{8,9},{9,8},{10,11... | collective-permute-start | bytes 1572872 | tf_op jit(solution)/shard_map/ppermute | solution.py:36
  181.0 6.9 %collective-permute-start.30 = (f32[32,1024]{1,0:T(8,128)S(1)}, f32[32,1024]{1,0:T(8,128)S(1)}, u32[]{:S(2)}, u32[]{:S(2)}) collective-permute-start(f32[32,1024]{1,0:T(8,128)S(1)} %add.121), channel_id=1, source_target_pairs={{0,4},{2,6},{4,0},{6,2},{8,12},{10,14},{12,8},{14,10},{1,5},{3,7},... | collective-permute-start | bytes 393224 | tf_op jit(solution)/shard_map/ppermute | solution.py:36
  186.1 24.6 %collective-permute-start.20 = (bf16[208,1024]{1,0:T(8,128)(2,1)S(1)}, bf16[208,1024]{1,0:T(8,128)(2,1)S(1)}, u32[]{:S(2)}, u32[]{:S(2)}) collective-permute-start(bf16[208,1024]{1,0:T(8,128)(2,1)S(1)} %add_convert_fusion.14), channel_id=1, source_target_pairs={{8,0},{10,2},{9,1},{11,3},{24,16},{26,18},{25,17},{27,19}} | collective-permute-start | bytes 1277960 | tf_op jit(solution)/shard_map/ppermute | solution.py:845
  188.0 21.7 %collective-permute-start.32 = (f32[32,1024]{1,0:T(8,128)S(1)}, f32[32,1024]{1,0:T(8,128)S(1)}, u32[]{:S(2)}, u32[]{:S(2)}) collective-permute-start(f32[32,1024]{1,0:T(8,128)S(1)} %add.134), channel_id=1, source_target_pairs={{0,8},{2,10},{4,12},{6,14},{8,0},{10,2},{12,4},{14,6},{1,9},{3,11}... | collective-permute-start | bytes 393224 | tf_op jit(solution)/shard_map/ppermute | solution.py:36
  190.8 28.0 %collective-permute-start.31 = (bf16[208,1024]{1,0:T(8,128)(2,1)S(1)}, bf16[208,1024]{1,0:T(8,128)(2,1)S(1)}, u32[]{:S(2)}, u32[]{:S(2)}) collective-permute-start(bf16[208,1024]{1,0:T(8,128)(2,1)S(1)} %add_convert_fusion.11), channel_id=1, source_target_pairs={{8,0},{10,2},{9,1},{11,3},{24,16},{26,18},{25,17},{27,19}} | collective-permute-start | bytes 1277960 | tf_op jit(solution)/shard_map/ppermute | solution.py:845
  220.0 11.1 %collective-permute-start.34 = (bf16[208,1024]{1,0:T(8,128)(2,1)}, bf16[208,1024]{1,0:T(8,128)(2,1)}, u32[]{:S(2)}, u32[]{:S(2)}) collective-permute-start(bf16[208,1024]{1,0:T(8,128)(2,1)} %get-tuple-element.118.refs_1_), channel_id=1, source_target_pairs={{0,16},{16,0},{1,17},{17,1},{2,18},{18,2},{3,19},{19,3},{4,20},{20... | collective-permute-start | bytes 1277960 | tf_op jit(solution)/shard_map/ppermute | solution.py:36
  221.3 19.0 %collective-permute-start.33 = (bf16[208,1024]{1,0:T(8,128)(2,1)}, bf16[208,1024]{1,0:T(8,128)(2,1)}, u32[]{:S(2)}, u32[]{:S(2)}) collective-permute-start(bf16[208,1024]{1,0:T(8,128)(2,1)} %get-tuple-element.124.refs_0_), channel_id=1, source_target_pairs={{0,16},{16,0},{1,17},{17,1},{2,18},{18,2},{3,19},{19,3},{4,20},{20... | collective-permute-start | bytes 1277960 | tf_op jit(solution)/shard_map/ppermute | solution.py:36
  224.8 18.4 %collective-permute-start.36 = (bf16[208,1024]{1,0:T(8,128)(2,1)}, bf16[208,1024]{1,0:T(8,128)(2,1)S(1)}, u32[]{:S(2)}, u32[]{:S(2)}) collective-permute-start(bf16[208,1024]{1,0:T(8,128)(2,1)} %get-tuple-element.118.refs_1_), channel_id=1, source_target_pairs={{0,1},{1,0},{2,3},{3,2},{4,5},{5,4},{6,7},{7,6},{8,9},{9,8},{10,11... | collective-permute-start | bytes 1277960 | tf_op jit(solution)/shard_map/ppermute | solution.py:36
  225.9 17.2 %collective-permute-start.35 = (bf16[208,1024]{1,0:T(8,128)(2,1)}, bf16[208,1024]{1,0:T(8,128)(2,1)S(1)}, u32[]{:S(2)}, u32[]{:S(2)}) collective-permute-start(bf16[208,1024]{1,0:T(8,128)(2,1)} %get-tuple-element.124.refs_0_), channel_id=1, source_target_pairs={{0,1},{1,0},{2,3},{3,2},{4,5},{5,4},{6,7},{7,6},{8,9},{9,8},{10,11... | collective-permute-start | bytes 1277960 | tf_op jit(solution)/shard_map/ppermute | solution.py:36
  231.1 12.0 %collective-permute-start.38 = (bf16[208,1024]{1,0:T(8,128)(2,1)}, bf16[208,1024]{1,0:T(8,128)(2,1)S(1)}, u32[]{:S(2)}, u32[]{:S(2)}) collective-permute-start(bf16[208,1024]{1,0:T(8,128)(2,1)} %collective-permute-done.34.refs_3_), channel_id=1, source_target_pairs={{0,1},{1,0},{2,3},{3,2},{4,5},{5,4},{6,7},{7,6},{8,9},{9,8},{10,11... | collective-permute-start | bytes 1277960 | tf_op jit(solution)/shard_map/ppermute | solution.py:36
  (35 other events, 214.3 us)

commit v3 on v2

--- a/solution.py
+++ b/solution.py
@@ -82,18 +82,17 @@
     return jnp.where(lax.broadcasted_iota(jnp.int32, scores.shape, 0) < length, scores, -1e30)
 
 
-def emit(regions, pieces, target, sems, first):
-    return [
-        pltpu.make_async_copy(
-            pieces[name].at[pl.ds(row, rows), pl.ds(column, columns)],
-            target.at[pl.ds(to_row, rows), pl.ds(to_column, columns)],
-            sems.at[first + i],
-        )
-        for i, (name, row, column, rows, columns, to_row, to_column) in enumerate(regions)
-    ]
-
-
-def wire_copies(plan, inner, pieces, targets, sems, act):
+def span_of(plan, name):
+    rows = [edge for chunk in plan for regions in chunk["regions"] for r in regions if r[0] == name for edge in (r[1], r[1] + r[3])]
+    return (min(rows), max(rows)) if rows else (0, 16)
+
+
+def shifted(plan, name, by):
+    move = lambda r: (r[0], r[1] - by, *r[2:]) if r[0] == name else r
+    return [dict(chunk, regions=[[move(r) for r in regions] for regions in chunk["regions"]]) for chunk in plan]
+
+
+def wire_copies(plan, inner, pieces, targets, sems, act, names="qoud"):
     for parity in range(2):
 
         @pl.when(inner == parity)
@@ -101,8 +100,11 @@
             at = to = 0
             for chunk in plan:
                 for regions in (chunk["regions"][parity], chunk["regions"][1 - parity]):
-                    for each in emit(regions, pieces, targets[to], sems, at):
-                        getattr(each, act)()
+                    for i, (name, row, column, rows, columns, to_row, to_column) in enumerate(regions):
+                        if name in names:
+                            source = pieces[name].at[pl.ds(row, rows), pl.ds(column, columns)]
+                            target = targets[to].at[pl.ds(to_row, rows), pl.ds(to_column, columns)]
+                            getattr(pltpu.make_async_copy(source, target, sems.at[at + i]), act)()
                     at += chunk["most"]
                     to += 1
 
@@ -223,7 +225,7 @@
     return out
 
 
-def own_kernel(plan, scalars, facts_a, facts_b, xa, xao, xb, xbo, pa, ra, pb, rb, dya, dyao, dyb, dybo, gains_ref, shifts_ref, w_up, w_down, *refs):
+def own_kernel(plan, kept, scalars, facts_a, facts_b, xa, xao, xb, xbo, pa, ra, pb, rb, dya, dyao, dyb, dybo, gains_ref, shifts_ref, w_up, w_down, *refs):
     h_any, act_any, dup_any, res_any, gu_any = refs[:5]
     targets = refs[5:-14]
     x_buf, p_buf, r_buf, dy_buf, up_buf, down_buf, ht_buf, h_ref, gd_ref, gu_ref, act_ref, dup_ref, res_ref, sems = refs[-14:]
@@ -260,7 +262,7 @@
             return carry
 
         lax.fori_loop(0, rows // LANE, norm, 0)
-    writes = [pltpu.make_async_copy(s, t, sems.at[count + i]) for i, (s, t) in enumerate(((h_ref, h_any), (res_ref, res_any), (act_ref, act_any), (dup_ref, dup_any), (gu_ref, gu_any)))]
+    writes = [pltpu.make_async_copy(s, t, sems.at[count + i]) for i, (s, t) in enumerate(((h_ref, h_any), (res_ref, res_any), (act_ref, act_any), (dup_ref, dup_any), (gu_ref.at[pl.ds(kept[0], kept[1] - kept[0]), :], gu_any)))]
     writes[0].start()
     writes[1].start()
     for each in copies[8:]:
@@ -271,34 +273,41 @@
         act, slope = gelu_parts(mm(h_ref[...], up_buf[:, cols]))
         act = act.astype(BF16)
         act_ref[:, cols] = act[:rows]
-        dup = (mm_nt(dy_buf[...], down_buf[cols, :]) * slope).astype(BF16)
-        dup_ref[:, cols] = dup
+        dup_ref[:, cols] = (mm_nt(dy_buf[...], down_buf[cols, :]) * slope).astype(BF16)
         gd_ref[cols, :] = mm_tn(act, dy_buf[...]).astype(BF16)
-        gu_ref[:, cols] = mm(ht_buf[...], dup).astype(BF16)
         return carry
 
     lax.fori_loop(0, quarter // 256, block, 0)
     pieces = {"d": gd_ref, "u": gu_ref}
     wire_sems = sems.at[pl.ds(count + 5, plan_sems(plan))]
-    wire_copies(plan, inner, pieces, targets, wire_sems, "start")
-    for each in writes[2:]:
-        each.start()
+    wire_copies(plan, inner, pieces, targets, wire_sems, "start", "d")
+    writes[2].start()
+    writes[3].start()
+
+    def wide(i, carry):
+        cols = pl.ds(pl.multiple_of(i * 256, 256), 256)
+        gu_ref[:, cols] = mm(ht_buf[...], dup_ref[:, cols]).astype(BF16)
+        return carry
+
+    lax.fori_loop(0, quarter // 256, wide, 0)
+    wire_copies(plan, inner, pieces, targets, wire_sems, "start", "u")
+    writes[4].start()
     wire_copies(plan, inner, pieces, targets, wire_sems, "wait")
     for each in writes:
         each.wait()
 
 
-def own_units(plan, scalars, facts, values, parts, came, dys, gains, shifts, w_up, w_down):
+def own_units(plan, kept, scalars, facts, values, parts, came, dys, gains, shifts, w_up, w_down):
     rows, width = 2 * values[0].shape[0], values[0].shape[1]
     quarter = w_up.shape[1] // 4
     count = 8 + 2 * (quarter // LANE) + 4 + 5 + plan_sems(plan)
     big = lambda *s: pltpu.VMEM(s, BF16)
     shapes = plan_shapes(plan, width)
     return pl.pallas_call(
-        functools.partial(own_kernel, plan),
+        functools.partial(own_kernel, plan, kept),
         in_specs=[SMEM] * 3 + [HBM] * 12 + [VMEM] * 2 + [HBM] * 2,
         out_specs=[HBM] * (5 + len(shapes)),
-        out_shape=[full((2 * rows, width), BF16), full((rows, quarter), BF16), full((2 * rows, quarter), BF16), full((rows // 2, width), F32), full((width, quarter), BF16)] + shapes,
+        out_shape=[full((2 * rows, width), BF16), full((rows, quarter), BF16), full((2 * rows, quarter), BF16), full((rows // 2, width), F32), full((kept[1] - kept[0], quarter), BF16)] + shapes,
         scratch_shapes=[big(2 * rows, width)] * 4
         + [big(width, quarter), big(quarter, width), big(width, 2 * rows), big(2 * rows, width), big(quarter, width), big(width, quarter), big(rows, quarter), big(2 * rows, quarter), pltpu.VMEM((rows // 2, width), F32), pltpu.SemaphoreType.DMA((count,))],
         compiler_params=params(60),
@@ -834,6 +843,7 @@
     scalars = jnp.stack([role, x, inner]).astype(jnp.int32)
 
     levels = count.bit_length() - 1
+    kept = span_of(middle, "u")
     chunks = []
 
     def exchange(plan, arrays, *first):
@@ -859,25 +869,37 @@
     second = attend(scalars, mate_facts, values[2:], gains, shifts, w_qkv, w_out)
     hts, qkvs, atts, parts, lses = zip(first, second)
     came = [after(swap(parts[0], "role"), parts[1]), swap(parts[1], "role")]
-    hidden, act, dup, residual, grad_up, *wires = own_units(early, scalars, both, values, parts, came, dys, gains, shifts, w_up, w_down)
+    hidden, act, dup, residual, grad_up, *wires = own_units(early, kept, scalars, both, values, parts, came, dys, gains, shifts, w_up, w_down)
     exchange(early, wires)
     dh, out_keep, out_send = rest_units(scalars, hidden, dys, act, dup, residual, w_up, w_down)
     output = (out_keep + swap(out_send, "role").astype(F32)).astype(BF16)
     dh_came = swap(after(dh, chunks[0]["came"]), "role")
     settle(chunks[0], dh)
     climb(chunks[0])
-    dr1, vec_two, datt, grad_out, *wires = turn(middle, scalars, both, values, parts, came, dh, dh_came, dys, gains, shifts, w_out, atts, grad_up)
+    dr1, vec_two, datt, grad_out, *wires = turn(shifted(middle, "u", kept[0]), scalars, both, values, parts, came, dh, dh_came, dys, gains, shifts, w_out, atts, grad_up)
     exchange(middle, wires)
     second_chunk = chunks[min(1, len(early) - 1)]
     if second_chunk is not chunks[0]:
-        settle(second_chunk, datt)
+        pass
+    dqa, *wires = back(late, scalars, both, datt, qkvs, hts, grad_out, lses)
+    exchange(late, wires, *(c["came"] for c in chunks[len(early) :]))
+    if second_chunk is not chunks[0]:
+        settle(second_chunk, dqa)
         climb(second_chunk)
-    dqa, *wires = back(late, scalars, both, after(datt, second_chunk["total"]), qkvs, hts, grad_out, lses)
     for chunk in chunks[: min(2, len(early))]:
         settle(chunk, dqa)
-    exchange(late, wires, *(chunk["came"] for chunk in chunks[len(early) :]))
-    dh1_keep, dh1_send = last(scalars, facts, qkvs[0], lses[0], after(datt, *(c["came"] for c in chunks[len(early) : -len(late)])), dqa, w_qkv)
-    dh1_send = after(dh1_send, chunks[-len(late)]["came"])
+    joined = chunks[: min(2, len(early))]
+    for chunk in chunks[min(2, len(early)) :]:
+        settle(chunk, dqa)
+        mates = [c for c in joined if c["block"] == chunk["block"] and c["level"] == 0 and (chunk["high"] == c["low"] or chunk["low"] == c["high"])]
+        if mates and not any(chunk is c for c in chunks[-len(late) :]):
+            ends = sorted((mates[0], chunk), key=lambda c: c["low"])
+            mates[0]["total"] = jnp.concatenate([c["total"] for c in ends], 0)
+            mates[0]["low"], mates[0]["high"] = ends[0]["low"], ends[1]["high"]
+        else:
+            joined.append(chunk)
+    chunks = joined
+    dh1_keep, dh1_send = last(scalars, facts, qkvs[0], lses[0], after(datt, chunks[-1]["total"]), dqa, w_qkv)
     dh1 = dh1_keep + swap(dh1_send, "role").astype(F32)
     unit, rstd = norm_stats(own_frames.astype(F32))
     input_grad = dr1 + norm_back(unit, rstd, lax.dynamic_slice(gains, (facts[1], 0, 0), (1, 1, width))[0].astype(F32), dh1)
@@ -894,29 +916,14 @@
             small_steps.append(small)
             distance *= 2
 
-    for chunk in chunks[min(2, len(early)) :]:
-        settle(chunk, dqa)
-    joined = chunks[: min(2, len(early))]
-    for chunk in chunks[min(2, len(early)) :]:
-        before = joined[-1]
-        mates = [c for c in joined if c["block"] == chunk["block"] and chunk["high"] == c["low"] and c["level"] == 0]
-        mates += [c for c in joined if c["block"] == chunk["block"] and chunk["low"] == c["high"] and c["level"] == 0]
-        if mates and chunk not in chunks[-len(late) :]:
-            mate = mates[0]
-            ends = sorted((mate, chunk), key=lambda c: c["low"])
-            mate["total"] = jnp.concatenate([c["total"] for c in ends], 0)
-            mate["low"], mate["high"] = ends[0]["low"], ends[1]["high"]
-        else:
-            joined.append(chunk)
-    chunks = joined
     for chunk in chunks:
         if chunk["level"] == 0:
             climb(chunk)
             settle(chunk)
     for level in range(1, levels):
-        for chunk in chunks:
-            if level == levels - 1 and chunk in chunks[-2:]:
-                chunk["total"] = after(chunk["total"], small_steps[-3 if chunk is chunks[-2] else -2])
+        for i, chunk in enumerate(chunks):
+            if level == levels - 1 and i >= len(chunks) - 2:
+                chunk["total"] = after(chunk["total"], small_steps[-3 if i == len(chunks) - 2 else -2])
             climb(chunk)
             settle(chunk)
     edges = [0, layout.rows // 32 * 16, layout.rows]
@@ -928,15 +935,14 @@
             if first >= past:
                 continue
             here = chunk["total"][first - chunk["low"] : past - chunk["low"]]
-            mine = outer == chunk["block"]
-            part = jnp.where(mine, here, final[first - low : past - low])
+            part = jnp.where(outer == chunk["block"], here, final[first - low : past - low])
             final = jnp.concatenate([final[: first - low], part, final[past - low :]], 0)
         distance = 2
         while distance < groups:
             final = add(final, swap(final, "group", distance))
             distance *= 2
         if high == layout.rows:
-            final = after(final, small)
+            final = after(final, small, quads[1][0])
         mate = swap(final, "group")
         for into, value in zip(quads, (final, mate, swap(final, "role"), swap(mate, "role"))):
             into.append(value)

time: 252 us -> 241 us (0.956)
  starting transfers between devices: 55.3 us -> 48.3 us
    ppermute x10, waiting for transfers between devices: 8.13 us -> 33.3 us  [climb(): lax.ppermute(chunk['total'], 'member', tree_pairs(chunk['block'], chunk['...]
    ppermute x29, waiting for transfers between devices: 43.5 us -> 20.8 us  [swap(): return lax.ppermute(value, axis, [(i, i ^ distance) for i in range(count)])]
    ppermute x29, starting transfers between devices: 32.1 us -> 27.3 us  [swap(): return lax.ppermute(value, axis, [(i, i ^ distance) for i in range(count)])]
    pallas_call x1, Pallas kernels: 21.4 us -> 18.8 us  [own_units(): pl.pallas_call(functools.partial(own_kernel, plan, kept), in_specs=[SMEM]...]
  transfers between devices with their start and end apart: 39 -> 39, of which waited for: 12 -> 13; matrix products, arithmetic and copies ran while one was open for 12% -> 11% of each run, Pallas kernels for 31% -> 33%
where the time goes in v3:
time: 241 us; the launch traced here: 240 us
  Pallas kernels  103 us (43%)
  waiting for transfers between devices  54.1 us (22%)
  starting transfers between devices  48.3 us (20%)
  other arithmetic  26.3 us (11%)
  local copies, waits for them, and re-layouts  6.44 us (3%)
  between operations  2.68 us (1%)
    ppermute x10, waiting for transfers between devices, climb(): lax.ppermute(chunk['total'], 'member', tree_pairs(chunk['block'], chunk['...  33.3 us
    ppermute x29, starting transfers between devices, swap(): return lax.ppermute(value, axis, [(i, i ^ distance) for i in range(count)])  27.3 us
    pallas_call x2, Pallas kernels, attend(): pl.pallas_call(attend_kernel, in_specs=[SMEM, SMEM, HBM, HBM, VMEM, VMEM,...  26.2 us
    ppermute x10, starting transfers between devices, climb(): lax.ppermute(chunk['total'], 'member', tree_pairs(chunk['block'], chunk['...  21.1 us
    ppermute x29, waiting for transfers between devices, swap(): return lax.ppermute(value, axis, [(i, i ^ distance) for i in range(count)])  20.8 us
    pallas_call x1, Pallas kernels, rest_units(): pl.pallas_call(rest_kernel, in_specs=[SMEM] + [HBM] * 7 + [VMEM] + [HBM]...  19.5 us
    pallas_call x1, Pallas kernels, own_units(): pl.pallas_call(functools.partial(own_kernel, plan, kept), in_specs=[SMEM]...  18.8 us
    convert_element_type x14, other arithmetic, add(): return (left.astype(F32) + right.astype(F32)).astype(BF16)  16.2 us
  transfers between devices with their start and end apart: 39, of which 13 were waited for; matrix products, arithmetic and copies ran while one was open for 11% of the time, Pallas kernels for 33%

profile of v3, /device:TPU:1, one launch (start us, length us, event | category | flops | bytes accessed | tf_op | source)
XLA Modules:
  0.0 240.5 jit_solution(10061043137147830345)
XLA Ops:
  0.8 2.7 %collective-permute-start.2 = (bf16[256,1024]{1,0:T(8,128)(2,1)}, bf16[256,1024]{1,0:T(8,128)(2,1)S(1)}, u32[]{:S(2)}, u32[]{:S(2)}) collective-permute-start(bf16[256,1024]{1,0:T(8,128)(2,1)} %bitcast.31), channel_id=1, source_target_pairs={{0,16},{16,0},{1,17},{17,1},{2,18},{18,2},{3,19},{19,3},{4,20},{20... | collective-permute-start | bytes 1572872 | tf_op jit(solution)/shard_map/ppermute | solution.py:36
  6.7 13.1 %attend.2 = (bf16[1024,512]{1,0:T(8,128)(2,1)}, bf16[512,1536]{1,0:T(8,128)(2,1)}, bf16[512,512]{1,0:T(8,128)(2,1)}, bf16[512,1024]{1,0:T(8,128)(2,1)}, f32[8,512]{1,0:T(8,128)}) custom-call(s32[3]{0:T(128)} %pad_add_fusion.scalars, s32[2]{0:T(128)} %pad_add_fusion.1.facts.facts_a, bf16[256,1024]{1,0:T(8,128)(2,1)} %bitcast.32, ...), custom_call_target="tpu_custom_call" | custom-call | flops 12000000000 | bytes 8000000 | tf_op jit(solution)/shard_map/attend/pallas_call | solution.py:189
  20.7 2.0 collective-permute-done.facts.facts_b
  23.9 13.1 %attend.3 = (bf16[1024,512]{1,0:T(8,128)(2,1)}, bf16[512,1536]{1,0:T(8,128)(2,1)}, bf16[512,512]{1,0:T(8,128)(2,1)}, bf16[512,1024]{1,0:T(8,128)(2,1)}, f32[8,512]{1,0:T(8,128)}) custom-call(s32[3]{0:T(128)} %pad_add_fusion.scalars, s32[2]{0:T(128)} %copy-done.27, bf16[256,1024]{1,0:T(8,128)(2,1)} %copy-done.18, bf16[256,1024]{1,0:T(8,128)(2,1)} %copy-done.19, ...), custom_call_target="tpu_custom_call" | custom-call | flops 12000000000 | bytes 8000000 | tf_op jit(solution)/shard_map/attend/pallas_call | solution.py:189
  38.9 3.1 %collective-permute-done.6.dyao = bf16[256,1024]{1,0:T(8,128)(2,1)S(1)} collective-permute-done((bf16[256,1024]{1,0:T(8,128)(2,1)S(1)}, bf16[256,1024]{1,0:T(8,128)(2,1)S(1)}, u32[]{:S(2)}, u32[]{:S(2)}) %collective-permute-start.6) | collective-permute-done | bytes 524320 | tf_op jit(solution)/shard_map/ppermute | solution.py:36
  44.2 18.8 %own_units.1 = (bf16[1024,1024]{1,0:T(8,128)(2,1)}, bf16[512,1024]{1,0:T(8,128)(2,1)}, bf16[1024,1024]{1,0:T(8,128)(2,1)}, f32[256,1024]{1,0:T(8,128)}, bf16[256...) custom-call(s32[3]{0:T(128)} %pad_add_fusion.scalars, ...), custom_call_target="tpu_custom_call" | custom-call | flops 20000000000 | bytes 8000000 | tf_op jit(solution)/shard_map/own_units/pallas_call | solution.py:306
  64.4 19.5 %rest_units.1 = (bf16[1024,1024]{1,0:T(8,128)(2,1)}, f32[256,1024]{1,0:T(8,128)}, bf16[256,1024]{1,0:T(8,128)(2,1)}) custom-call(s32[3]{0:T(128)} %pad_add_fusion.scalars, bf16[1024,1024]{1,0:T(8,128)(2,1)} %get-tuple-element.65.h_any, bf16[256,1024]{1,0:T(8,128)(2,1)} %bitcast.40, bf16[256,1024]{1,0:T(8,128)(2,1)} %copy-done.20, ...), custom_call_target="tpu_custom_call" | custom-call | flops 20000000000 | bytes 8000000 | tf_op jit(solution)/shard_map/rest_units/pallas_call | solution.py:365
  87.8 3.3 %collective-permute-start.27 = (bf16[416,1024]{1,0:T(8,128)(2,1)S(1)}, bf16[416,1024]{1,0:T(8,128)(2,1)S(1)}, u32[]{:S(2)}, u32[]{:S(2)}) collective-permute-start(bf16[416,1024]{1,0:T(8,128)(2,1)S(1)} %add_convert_fusion.2), channel_id=1, source_target_pairs={{0,4},{2,6},{8,12},{10,14},{1,5},{3,7},{9,13},{11,15},{16,20},{18,... | collective-permute-start | bytes 2555912 | tf_op jit(solution)/shard_map/ppermute | solution.py:855
  91.1 11.2 %turn.1 = (f32[256,1024]{1,0:T(8,128)}, f32[8,1024]{1,0:T(8,128)}, bf16[1024,512]{1,0:T(8,128)(2,1)}, bf16[256,1024]{1,0:T(8,128)(2,1)}, bf16[256,1024]{1,0:T(8,128)(2,1)}, /*index=5*/bf16[256,1024]{1,0:T(8,128)(2,1)}) custom-call(s32[3]{0:T(128)} %pad_add_fusion.scalars, s32[2]{0:T(128)} %pad_add_fusion.1.facts.facts_a, s32[2]{0:T(128)} %copy-done.27, ...), custom_call_target="tpu_custom_call" | custom-call | flops 12000000000 | bytes 8000000 | tf_op jit(solution)/shard_map/turn/pallas_call | solution.py:476
  103.6 13.0 %back.1 = (bf16[512,768]{1,0:T(8,128)(2,1)}, bf16[208,1024]{1,0:T(8,128)(2,1)}, bf16[208,1024]{1,0:T(8,128)(2,1)}, bf16[208,1024]{1,0:T(8,128)(2,1)}, bf16[208,1024]{1,0:T(8,128)(2,1)}) custom-call(s32[3]{0:T(128)} %pad_add_fusion.scalars, s32[2]{0:T(128)} %pad_add_fusion.1.facts.facts_a, s32[2]{0:T(128)} %copy-done.27, ...), custom_call_target="tpu_custom_call" | custom-call | flops 14000000000 | bytes 8000000 | tf_op jit(solution)/shard_map/back/pallas_call | solution.py:543
  118.2 2.3 collective-permute-start.25
  120.6 1.6 collective-permute-start.28
  123.0 2.1 collective-permute-done.12
  129.9 6.4 %collective-permute-start.22 = (bf16[416,1024]{1,0:T(8,128)(2,1)}, bf16[416,1024]{1,0:T(8,128)(2,1)}, u32[]{:S(2)}, u32[]{:S(2)}) collective-permute-start(bf16[416,1024]{1,0:T(8,128)(2,1)} %pad_maximum_fusion), channel_id=1, source_target_pairs={{0,4},{2,6},{12,8},{14,10},{1,5},{3,7},{13,9},{15,11},{16,20},{18,... | collective-permute-start | bytes 2555912 | tf_op jit(solution)/shard_map/ppermute | solution.py:855
  137.3 8.6 %last.1 = (f32[256,1024]{1,0:T(8,128)}, bf16[256,1024]{1,0:T(8,128)(2,1)}) custom-call(s32[3]{0:T(128)} %pad_add_fusion.scalars, s32[2]{0:T(128)} %pad_add_fusion.1.facts.facts_a, bf16[512,1536]{1,0:T(8,128)(2,1)} %get-tuple-element.78.qkv_a.qkv_ref, f32[8,512]{1,0:T(8,128)} %get-tuple-element.79.lse_a.lse_ref, ...), custom_call_target="tpu_custom_call" | custom-call | flops 7000000000 | bytes 8000000 | tf_op jit(solution)/shard_map/last/pallas_call | solution.py:591
  145.9 2.6 %collective-permute-start.14 = (bf16[256,1024]{1,0:T(8,128)(2,1)}, bf16[256,1024]{1,0:T(8,128)(2,1)S(1)}, u32[]{:S(2)}, u32[]{:S(2)}) collective-permute-start(bf16[256,1024]{1,0:T(8,128)(2,1)} %get-tuple-element.94), channel_id=1, source_target_pairs={{0,1},{1,0},{2,3},{3,2},{4,5},{5,4},{6,7},{7,6},{8,9},{9,8},{10,11... | collective-permute-start | bytes 1572872 | tf_op jit(solution)/shard_map/ppermute | solution.py:36
  148.5 2.7 %add_convert_fusion.4 = bf16[416,1024]{1,0:T(8,128)(2,1)} fusion(bf16[416,1024]{1,0:T(8,128)(2,1)} %collective-permute-done.25, bf16[416,1024]{1,0:T(8,128)(2,1)} %add_convert_fusion.5), kind=kLoop, calls=%fused_computation.4 | loop fusion | flops 1703936 | bytes 2555904 | tf_op jit(solution)/shard_map/convert_element_type | solution.py:703
  151.2 1.6 collective-permute-start.26
  160.9 1.5 add_convert_fusion
  162.4 2.1 collective-permute-done.18
  165.7 12.7 %collective-permute-done.16 = bf16[208,1024]{1,0:T(8,128)(2,1)} collective-permute-done((bf16[208,1024]{1,0:T(8,128)(2,1)}, bf16[208,1024]{1,0:T(8,128)(2,1)}, u32[]{:S(2)}, u32[]{:S(2)}) %collective-permute-start.16) | collective-permute-done | bytes 426016 | tf_op jit(solution)/shard_map/ppermute | solution.py:855
  182.4 1.7 collective-permute-done.30
  185.4 1.7 add_convert_fusion.3
  187.5 11.5 %collective-permute-done.20 = bf16[208,1024]{1,0:T(8,128)(2,1)S(1)} collective-permute-done((bf16[208,1024]{1,0:T(8,128)(2,1)S(1)}, bf16[208,1024]{1,0:T(8,128)(2,1)S(1)}, u32[]{:S(2)}, u32[]{:S(2)}) %collective-permute-start.20) | collective-permute-done | bytes 426016 | tf_op jit(solution)/shard_map/ppermute | solution.py:855
  199.0 9.1 %collective-permute-done.31 = bf16[208,1024]{1,0:T(8,128)(2,1)S(1)} collective-permute-done((bf16[208,1024]{1,0:T(8,128)(2,1)S(1)}, bf16[208,1024]{1,0:T(8,128)(2,1)S(1)}, u32[]{:S(2)}, u32[]{:S(2)}) %collective-permute-start.31) | collective-permute-done | bytes 426016 | tf_op jit(solution)/shard_map/ppermute | solution.py:855
  210.5 1.5 collective-permute-start.9
  212.0 6.0 %collective-permute-done.32 = f32[32,1024]{1,0:T(8,128)S(1)} collective-permute-done((f32[32,1024]{1,0:T(8,128)S(1)}, f32[32,1024]{1,0:T(8,128)S(1)}, u32[]{:S(2)}, u32[]{:S(2)}) %collective-permute-start.32) | collective-permute-done | bytes 131104 | tf_op jit(solution)/shard_map/ppermute | solution.py:36
  222.3 2.0 fusion.12
  224.3 2.4 collective-permute-start.35
  227.2 2.0 collective-permute-done.34.refs_3_
  229.3 3.0 %collective-permute-start.38 = (bf16[208,1024]{1,0:T(8,128)(2,1)}, bf16[208,1024]{1,0:T(8,128)(2,1)}, u32[]{:S(2)}, u32[]{:S(2)}) collective-permute-start(bf16[208,1024]{1,0:T(8,128)(2,1)} %collective-permute-done.34.refs_3_), channel_id=1, source_target_pairs={{0,1},{1,0},{2,3},{3,2},{4,5},{5,4},{6,7},{7,6},{8,9},{9,8},{10,11... | collective-permute-start | bytes 1277960 | tf_op jit(solution)/shard_map/ppermute | solution.py:36
  234.8 5.5 %place.1 = f32[6158,128]{1,0:T(8,128)} custom-call(s32[32]{0:T(128)} %pad_add_fusion.2.table, bf16[208,1024]{1,0:T(8,128)(2,1)} %get-tuple-element.120.refs_0_, bf16[208,1024]{1,0:T(8,128)(2,1)} %get-tuple-element.114.refs_1_, bf16[208,1024]{1,0:T(8,128)(2,1)} %collective-permute-done.33.refs_2_, bf16[208,1024]{1,0:T(8,128)(2,1)} %collective-permute-done.34.refs_3_, ...), custom_call_target="tpu_custom_call" | custom-call | flops 4000000000 | bytes 8000000 | tf_op jit(solution)/shard_map/place/pallas_call | solution.py:816
  (155 shorter events, 47.5 us)
Async XLA Ops:
  0.6 5.3 %collective-permute-start.1 = (bf16[256,1024]{1,0:T(8,128)(2,1)}, bf16[256,1024]{1,0:T(8,128)(2,1)S(1)}, u32[]{:S(2)}, u32[]{:S(2)}) collective-permute-start(bf16[256,1024]{1,0:T(8,128)(2,1)} %bitcast.30), channel_id=1, source_target_pairs={{0,1},{1,0},{2,3},{3,2},{4,5},{5,4},{6,7},{7,6},{8,9},{9,8},{10,11... | collective-permute-start | bytes 1572872 | tf_op jit(solution)/shard_map/ppermute | solution.py:36
  0.8 19.0 %collective-permute-start.2 = (bf16[256,1024]{1,0:T(8,128)(2,1)}, bf16[256,1024]{1,0:T(8,128)(2,1)S(1)}, u32[]{:S(2)}, u32[]{:S(2)}) collective-permute-start(bf16[256,1024]{1,0:T(8,128)(2,1)} %bitcast.31), channel_id=1, source_target_pairs={{0,16},{16,0},{1,17},{17,1},{2,18},{18,2},{3,19},{19,3},{4,20},{20... | collective-permute-start | bytes 1572872 | tf_op jit(solution)/shard_map/ppermute | solution.py:36
  20.2 18.7 %collective-permute-start.4 = (bf16[512,1024]{1,0:T(8,128)(2,1)}, bf16[512,1024]{1,0:T(8,128)(2,1)S(1)}, u32[]{:S(2)}, u32[]{:S(2)}) collective-permute-start(bf16[512,1024]{1,0:T(8,128)(2,1)} %get-tuple-element.59.pa), channel_id=1, source_target_pairs={{0,1},{1,0},{2,3},{3,2},{4,5},{5,4},{6,7},{7,6},{8,9},{9,8},{10,11... | collective-permute-start | bytes 3145736 | tf_op jit(solution)/shard_map/ppermute | solution.py:36
  22.6 15.9 %collective-permute-start.7 = (bf16[256,1024]{1,0:T(8,128)(2,1)S(1)}, bf16[256,1024]{1,0:T(8,128)(2,1)}, u32[]{:S(2)}, u32[]{:S(2)}) collective-permute-start(bf16[256,1024]{1,0:T(8,128)(2,1)S(1)} %bitcast.42), channel_id=1, source_target_pairs={{0,16},{16,0},{1,17},{17,1},{2,18},{18,2},{3,19},{19,3},{4,20},{20... | collective-permute-start | bytes 1572872 | tf_op jit(solution)/shard_map/ppermute | solution.py:36
  37.0 5.4 %collective-permute-start.5 = (bf16[512,1024]{1,0:T(8,128)(2,1)}, bf16[512,1024]{1,0:T(8,128)(2,1)S(1)}, u32[]{:S(2)}, u32[]{:S(2)}) collective-permute-start(bf16[512,1024]{1,0:T(8,128)(2,1)} %get-tuple-element.62.pb), channel_id=1, source_target_pairs={{0,1},{1,0},{2,3},{3,2},{4,5},{5,4},{6,7},{7,6},{8,9},{9,8},{10,11... | collective-permute-start | bytes 3145736 | tf_op jit(solution)/shard_map/ppermute | solution.py:36
  62.9 20.9 %collective-permute-start.10 = (bf16[416,1024]{1,0:T(8,128)(2,1)}, bf16[416,1024]{1,0:T(8,128)(2,1)S(1)}, u32[]{:S(2)}, u32[]{:S(2)}) collective-permute-start(bf16[416,1024]{1,0:T(8,128)(2,1)} %get-tuple-element.72), channel_id=1, source_target_pairs={{0,2},{2,0},{4,6},{6,4},{8,10},{10,8},{12,14},{14,12},{1,3},{3,1},... | collective-permute-start | bytes 2555912 | tf_op jit(solution)/shard_map/ppermute | solution.py:36
  83.9 7.3 %collective-permute-start.11 = (bf16[1024,1024]{1,0:T(8,128)(2,1)}, bf16[1024,1024]{1,0:T(8,128)(2,1)}, u32[]{:S(2)}, u32[]{:S(2)}) collective-permute-start(bf16[1024,1024]{1,0:T(8,128)(2,1)} %get-tuple-element.73.dh_any), channel_id=1, source_target_pairs={{0,1},{1,0},{2,3},{3,2},{4,5},{5,4},{6,7},{7,6},{8,9},{9,8},{10,11... | collective-permute-start | bytes 6291464 | tf_op jit(solution)/shard_map/ppermute | solution.py:36
  85.9 40.6 %collective-permute-start.21 = (bf16[160,1024]{1,0:T(8,128)(2,1)}, bf16[160,1024]{1,0:T(8,128)(2,1)}, u32[]{:S(2)}, u32[]{:S(2)}) collective-permute-start(bf16[160,1024]{1,0:T(8,128)(2,1)} %get-tuple-element.105), channel_id=1, source_target_pairs={{0,2},{2,0},{4,6},{6,4},{8,10},{10,8},{12,14},{14,12},{1,3},{3,1},... | collective-permute-start | bytes 983048 | tf_op jit(solution)/shard_map/ppermute | solution.py:36
  87.3 29.3 %collective-permute-start.24 = (bf16[416,1024]{1,0:T(8,128)(2,1)}, bf16[416,1024]{1,0:T(8,128)(2,1)S(1)}, u32[]{:S(2)}, u32[]{:S(2)}) collective-permute-start(bf16[416,1024]{1,0:T(8,128)(2,1)} %get-tuple-element.108), channel_id=1, source_target_pairs={{0,2},{2,0},{4,6},{6,4},{8,10},{10,8},{12,14},{14,12},{1,3},{3,1},... | collective-permute-start | bytes 2555912 | tf_op jit(solution)/shard_map/ppermute | solution.py:36
  87.8 30.1 %collective-permute-start.27 = (bf16[416,1024]{1,0:T(8,128)(2,1)S(1)}, bf16[416,1024]{1,0:T(8,128)(2,1)S(1)}, u32[]{:S(2)}, u32[]{:S(2)}) collective-permute-start(bf16[416,1024]{1,0:T(8,128)(2,1)S(1)} %add_convert_fusion.2), channel_id=1, source_target_pairs={{0,4},{2,6},{8,12},{10,14},{1,5},{3,7},{9,13},{11,15},{16,20},{18,... | collective-permute-start | bytes 2555912 | tf_op jit(solution)/shard_map/ppermute | solution.py:855
  102.3 22.8 %collective-permute-start.12 = (bf16[256,1024]{1,0:T(8,128)(2,1)}, bf16[256,1024]{1,0:T(8,128)(2,1)}, u32[]{:S(2)}, u32[]{:S(2)}) collective-permute-start(bf16[256,1024]{1,0:T(8,128)(2,1)} %get-tuple-element.90), channel_id=1, source_target_pairs={{0,2},{2,0},{4,6},{6,4},{8,10},{10,8},{12,14},{14,12},{1,3},{3,1},... | collective-permute-start | bytes 1572872 | tf_op jit(solution)/shard_map/ppermute | solution.py:36
  118.2 30.3 %collective-permute-start.25 = (bf16[416,1024]{1,0:T(8,128)(2,1)}, bf16[416,1024]{1,0:T(8,128)(2,1)}, u32[]{:S(2)}, u32[]{:S(2)}) collective-permute-start(bf16[416,1024]{1,0:T(8,128)(2,1)} %add_convert_fusion.5), channel_id=1, source_target_pairs={{0,4},{2,6},{12,8},{14,10},{1,5},{3,7},{13,9},{15,11},{16,20},{18,... | collective-permute-start | bytes 2555912 | tf_op jit(solution)/shard_map/ppermute | solution.py:855
  120.6 39.1 %collective-permute-start.28 = (bf16[416,1024]{1,0:T(8,128)(2,1)S(1)}, bf16[416,1024]{1,0:T(8,128)(2,1)}, u32[]{:S(2)}, u32[]{:S(2)}) collective-permute-start(bf16[416,1024]{1,0:T(8,128)(2,1)S(1)} %add_convert_fusion.1), channel_id=1, source_target_pairs={{4,12},{6,14},{5,13},{7,15},{20,28},{22,30},{21,29},{23,31}} | collective-permute-start | bytes 2555912 | tf_op jit(solution)/shard_map/ppermute | solution.py:855
  125.1 11.2 %collective-permute-start.13 = (bf16[208,1024]{1,0:T(8,128)(2,1)S(1)}, bf16[208,1024]{1,0:T(8,128)(2,1)S(1)}, u32[]{:S(2)}, u32[]{:S(2)}) collective-permute-start(bf16[208,1024]{1,0:T(8,128)(2,1)S(1)} %copy-done.22), channel_id=1, source_target_pairs={{0,2},{2,0},{4,6},{6,4},{8,10},{10,8},{12,14},{14,12},{1,3},{3,1},... | collective-permute-start | bytes 1277960 | tf_op jit(solution)/shard_map/ppermute | solution.py:36
  127.6 25.2 %collective-permute-start.15 = (bf16[208,1024]{1,0:T(8,128)(2,1)}, bf16[208,1024]{1,0:T(8,128)(2,1)S(1)}, u32[]{:S(2)}, u32[]{:S(2)}) collective-permute-start(bf16[208,1024]{1,0:T(8,128)(2,1)} %get-tuple-element.98), channel_id=1, source_target_pairs={{0,2},{2,0},{4,6},{6,4},{8,10},{10,8},{12,14},{14,12},{1,3},{3,1},... | collective-permute-start | bytes 1277960 | tf_op jit(solution)/shard_map/ppermute | solution.py:36
  129.9 27.2 %collective-permute-start.22 = (bf16[416,1024]{1,0:T(8,128)(2,1)}, bf16[416,1024]{1,0:T(8,128)(2,1)}, u32[]{:S(2)}, u32[]{:S(2)}) collective-permute-start(bf16[416,1024]{1,0:T(8,128)(2,1)} %pad_maximum_fusion), channel_id=1, source_target_pairs={{0,4},{2,6},{12,8},{14,10},{1,5},{3,7},{13,9},{15,11},{16,20},{18,... | collective-permute-start | bytes 2555912 | tf_op jit(solution)/shard_map/ppermute | solution.py:855
  145.9 9.0 %collective-permute-start.14 = (bf16[256,1024]{1,0:T(8,128)(2,1)}, bf16[256,1024]{1,0:T(8,128)(2,1)S(1)}, u32[]{:S(2)}, u32[]{:S(2)}) collective-permute-start(bf16[256,1024]{1,0:T(8,128)(2,1)} %get-tuple-element.94), channel_id=1, source_target_pairs={{0,1},{1,0},{2,3},{3,2},{4,5},{5,4},{6,7},{7,6},{8,9},{9,8},{10,11... | collective-permute-start | bytes 1572872 | tf_op jit(solution)/shard_map/ppermute | solution.py:36
  151.2 34.2 %collective-permute-start.26 = (bf16[416,1024]{1,0:T(8,128)(2,1)}, bf16[416,1024]{1,0:T(8,128)(2,1)}, u32[]{:S(2)}, u32[]{:S(2)}) collective-permute-start(bf16[416,1024]{1,0:T(8,128)(2,1)} %add_convert_fusion.4), channel_id=1, source_target_pairs={{4,8},{6,10},{5,9},{7,11},{20,24},{22,26},{21,25},{23,27}} | collective-permute-start | bytes 2555912 | tf_op jit(solution)/shard_map/ppermute | solution.py:855
  152.8 27.1 %collective-permute-start.29 = (bf16[208,1024]{1,0:T(8,128)(2,1)}, bf16[208,1024]{1,0:T(8,128)(2,1)}, u32[]{:S(2)}, u32[]{:S(2)}) collective-permute-start(bf16[208,1024]{1,0:T(8,128)(2,1)} %add_convert_fusion.15), channel_id=1, source_target_pairs={{4,0},{6,2},{12,8},{14,10},{5,1},{7,3},{13,9},{15,11},{20,16},{22,... | collective-permute-start | bytes 1277960 | tf_op jit(solution)/shard_map/ppermute | solution.py:855
  155.0 23.4 %collective-permute-start.16 = (bf16[208,1024]{1,0:T(8,128)(2,1)}, bf16[208,1024]{1,0:T(8,128)(2,1)}, u32[]{:S(2)}, u32[]{:S(2)}) collective-permute-start(bf16[208,1024]{1,0:T(8,128)(2,1)} %add_convert_fusion.14), channel_id=1, source_target_pairs={{4,0},{6,2},{12,8},{14,10},{5,1},{7,3},{13,9},{15,11},{20,16},{22,... | collective-permute-start | bytes 1277960 | tf_op jit(solution)/shard_map/ppermute | solution.py:855
  158.9 28.3 %collective-permute-start.23 = (bf16[416,1024]{1,0:T(8,128)(2,1)S(1)}, bf16[416,1024]{1,0:T(8,128)(2,1)S(1)}, u32[]{:S(2)}, u32[]{:S(2)}) collective-permute-start(bf16[416,1024]{1,0:T(8,128)(2,1)S(1)} %add_convert_fusion.7), channel_id=1, source_target_pairs={{8,4},{10,6},{9,5},{11,7},{24,20},{26,22},{25,21},{27,23}} | collective-permute-start | bytes 2555912 | tf_op jit(solution)/shard_map/ppermute | solution.py:855
  159.6 4.9 %collective-permute-start.18 = (f32[32,1024]{1,0:T(8,128)S(1)}, f32[32,1024]{1,0:T(8,128)S(1)}, u32[]{:S(2)}, u32[]{:S(2)}) collective-permute-start(f32[32,1024]{1,0:T(8,128)S(1)} %pad_add_fusion.3), channel_id=1, source_target_pairs={{0,16},{16,0},{1,17},{17,1},{2,18},{18,2},{3,19},{19,3},{4,20},{20... | collective-permute-start | bytes 393224 | tf_op jit(solution)/shard_map/ppermute | solution.py:36
  164.5 15.2 %collective-permute-start.19 = (f32[32,1024]{1,0:T(8,128)S(1)}, f32[32,1024]{1,0:T(8,128)S(1)}, u32[]{:S(2)}, u32[]{:S(2)}) collective-permute-start(f32[32,1024]{1,0:T(8,128)S(1)} %add.120), channel_id=1, source_target_pairs={{0,2},{2,0},{4,6},{6,4},{8,10},{10,8},{12,14},{14,12},{1,3},{3,1},... | collective-permute-start | bytes 393224 | tf_op jit(solution)/shard_map/ppermute | solution.py:36
  181.1 17.9 %collective-permute-start.20 = (bf16[208,1024]{1,0:T(8,128)(2,1)S(1)}, bf16[208,1024]{1,0:T(8,128)(2,1)S(1)}, u32[]{:S(2)}, u32[]{:S(2)}) collective-permute-start(bf16[208,1024]{1,0:T(8,128)(2,1)S(1)} %add_convert_fusion.13), channel_id=1, source_target_pairs={{8,0},{10,2},{9,1},{11,3},{24,16},{26,18},{25,17},{27,19}} | collective-permute-start | bytes 1277960 | tf_op jit(solution)/shard_map/ppermute | solution.py:855
  184.1 24.0 %collective-permute-start.31 = (bf16[208,1024]{1,0:T(8,128)(2,1)S(1)}, bf16[208,1024]{1,0:T(8,128)(2,1)S(1)}, u32[]{:S(2)}, u32[]{:S(2)}) collective-permute-start(bf16[208,1024]{1,0:T(8,128)(2,1)S(1)} %add_convert_fusion.11), channel_id=1, source_target_pairs={{8,0},{10,2},{9,1},{11,3},{24,16},{26,18},{25,17},{27,19}} | collective-permute-start | bytes 1277960 | tf_op jit(solution)/shard_map/ppermute | solution.py:855
  209.3 10.4 %collective-permute-start.33 = (bf16[208,1024]{1,0:T(8,128)(2,1)}, bf16[208,1024]{1,0:T(8,128)(2,1)}, u32[]{:S(2)}, u32[]{:S(2)}) collective-permute-start(bf16[208,1024]{1,0:T(8,128)(2,1)} %get-tuple-element.120.refs_0_), channel_id=1, source_target_pairs={{0,16},{16,0},{1,17},{17,1},{2,18},{18,2},{3,19},{19,3},{4,20},{20... | collective-permute-start | bytes 1277960 | tf_op jit(solution)/shard_map/ppermute | solution.py:36
  210.5 11.8 %collective-permute-start.9 = (bf16[256,1024]{1,0:T(8,128)(2,1)}, bf16[256,1024]{1,0:T(8,128)(2,1)}, u32[]{:S(2)}, u32[]{:S(2)}) collective-permute-start(bf16[256,1024]{1,0:T(8,128)(2,1)} %get-tuple-element.70), channel_id=1, source_target_pairs={{0,1},{1,0},{2,3},{3,2},{4,5},{5,4},{6,7},{7,6},{8,9},{9,8},{10,11... | collective-permute-start | bytes 1572872 | tf_op jit(solution)/shard_map/ppermute | solution.py:36
  212.0 6.0 %collective-permute-start.32 = (f32[32,1024]{1,0:T(8,128)S(1)}, f32[32,1024]{1,0:T(8,128)S(1)}, u32[]{:S(2)}, u32[]{:S(2)}) collective-permute-start(f32[32,1024]{1,0:T(8,128)S(1)} %add.134), channel_id=1, source_target_pairs={{0,8},{2,10},{4,12},{6,14},{8,0},{10,2},{12,4},{14,6},{1,9},{3,11}... | collective-permute-start | bytes 393224 | tf_op jit(solution)/shard_map/ppermute | solution.py:36
  219.8 9.5 %collective-permute-start.34 = (bf16[208,1024]{1,0:T(8,128)(2,1)}, bf16[208,1024]{1,0:T(8,128)(2,1)}, u32[]{:S(2)}, u32[]{:S(2)}) collective-permute-start(bf16[208,1024]{1,0:T(8,128)(2,1)} %get-tuple-element.114.refs_1_), channel_id=1, source_target_pairs={{0,16},{16,0},{1,17},{17,1},{2,18},{18,2},{3,19},{19,3},{4,20},{20... | collective-permute-start | bytes 1277960 | tf_op jit(solution)/shard_map/ppermute | solution.py:36
  224.3 9.4 %collective-permute-start.35 = (bf16[208,1024]{1,0:T(8,128)(2,1)}, bf16[208,1024]{1,0:T(8,128)(2,1)S(1)}, u32[]{:S(2)}, u32[]{:S(2)}) collective-permute-start(bf16[208,1024]{1,0:T(8,128)(2,1)} %get-tuple-element.120.refs_0_), channel_id=1, source_target_pairs={{0,1},{1,0},{2,3},{3,2},{4,5},{5,4},{6,7},{7,6},{8,9},{9,8},{10,11... | collective-permute-start | bytes 1277960 | tf_op jit(solution)/shard_map/ppermute | solution.py:36
  226.7 7.0 %collective-permute-start.36 = (bf16[208,1024]{1,0:T(8,128)(2,1)S(1)}, bf16[208,1024]{1,0:T(8,128)(2,1)S(1)}, u32[]{:S(2)}, u32[]{:S(2)}) collective-permute-start(bf16[208,1024]{1,0:T(8,128)(2,1)S(1)} %copy-done.10), channel_id=1, source_target_pairs={{0,1},{1,0},{2,3},{3,2},{4,5},{5,4},{6,7},{7,6},{8,9},{9,8},{10,11... | collective-permute-start | bytes 1277960 | tf_op jit(solution)/shard_map/ppermute | solution.py:36
  226.7 7.0 %collective-permute-start.37 = (bf16[208,1024]{1,0:T(8,128)(2,1)}, bf16[208,1024]{1,0:T(8,128)(2,1)S(1)}, u32[]{:S(2)}, u32[]{:S(2)}) collective-permute-start(bf16[208,1024]{1,0:T(8,128)(2,1)} %collective-permute-done.33.refs_2_), channel_id=1, source_target_pairs={{0,1},{1,0},{2,3},{3,2},{4,5},{5,4},{6,7},{7,6},{8,9},{9,8},{10,11... | collective-permute-start | bytes 1277960 | tf_op jit(solution)/shard_map/ppermute | solution.py:36
  (35 other events, 244.1 us)

commit v4 on v3

--- a/solution.py
+++ b/solution.py
@@ -688,7 +688,7 @@
                 else:
                     runs.append([low, high, stage])
             for low, high, stage in runs:
-                middle = low + (high - low) // 32 * 16
+                middle = low + (high - low) * 5 // 8 // 16 * 16
                 for first, last in [(low, middle), (middle, high)] if stage == 2 else [(low, high)]:
                     regions = [self.regions(2 * block + i, first, last) for i in range(2)]
                     stages[stage].append({"block": block, "low": first, "high": last, "regions": regions, "most": max(map(len, regions))})
@@ -926,7 +926,7 @@
                 chunk["total"] = after(chunk["total"], small_steps[-3 if i == len(chunks) - 2 else -2])
             climb(chunk)
             settle(chunk)
-    edges = [0, layout.rows // 32 * 16, layout.rows]
+    edges = [0, layout.rows * 5 // 8 // 16 * 16, layout.rows]
     quads = [[], [], [], []]
     for low, high in zip(edges, edges[1:]):
         final = jnp.zeros((high - low, width), BF16)

time: 241 us -> 236 us (0.979)
  waiting for transfers between devices: 54.1 us -> 39.6 us
  other arithmetic: 26.3 us -> 30.4 us
  starting transfers between devices: 48.3 us -> 50.8 us
    ppermute x29, waiting for transfers between devices: 20.8 us -> 11.4 us  [swap(): return lax.ppermute(value, axis, [(i, i ^ distance) for i in range(count)])]
    ppermute x10, waiting for transfers between devices: 33.3 us -> 28.2 us  [climb(): lax.ppermute(chunk['total'], 'member', tree_pairs(chunk['block'], chunk['...]
    ppermute x29, starting transfers between devices: 27.3 us -> 30.2 us  [swap(): return lax.ppermute(value, axis, [(i, i ^ distance) for i in range(count)])]
    unnamed x56 -> x66, local copies, waits for them, and re-layouts: 4.63 us -> 5.84 us
  transfers between devices with their start and end apart: 39 -> 39, of which waited for: 13 -> 9; matrix products, arithmetic and copies ran while one was open for 11% -> 14% of each run, Pallas kernels for 33% -> 33%
where the time goes in v4:
time: 236 us; the launch traced here: 234 us
  Pallas kernels  103 us (44%)
  starting transfers between devices  50.8 us (22%)
  waiting for transfers between devices  39.6 us (17%)
  other arithmetic  30.4 us (13%)
  local copies, waits for them, and re-layouts  8.23 us (3%)
  between operations  2.76 us (1%)
    ppermute x29, starting transfers between devices, swap(): return lax.ppermute(value, axis, [(i, i ^ distance) for i in range(count)])  30.2 us
    ppermute x10, waiting for transfers between devices, climb(): lax.ppermute(chunk['total'], 'member', tree_pairs(chunk['block'], chunk['...  28.2 us
    pallas_call x2, Pallas kernels, attend(): pl.pallas_call(attend_kernel, in_specs=[SMEM, SMEM, HBM, HBM, VMEM, VMEM,...  26.2 us
    ppermute x10, starting transfers between devices, climb(): lax.ppermute(chunk['total'], 'member', tree_pairs(chunk['block'], chunk['...  20.6 us
    pallas_call x1, Pallas kernels, rest_units(): pl.pallas_call(rest_kernel, in_specs=[SMEM] + [HBM] * 7 + [VMEM] + [HBM]...  19.5 us
    pallas_call x1, Pallas kernels, own_units(): pl.pallas_call(functools.partial(own_kernel, plan, kept), in_specs=[SMEM]...  18.7 us
    convert_element_type x14, other arithmetic, add(): return (left.astype(F32) + right.astype(F32)).astype(BF16)  17.7 us
    pallas_call x1, Pallas kernels, back(): pl.pallas_call(functools.partial(back_kernel, plan), in_specs=[SMEM] * 3...  13 us
  transfers between devices with their start and end apart: 39, of which 9 were waited for; matrix products, arithmetic and copies ran while one was open for 14% of the time, Pallas kernels for 33%

profile of v4, /device:TPU:1, one launch (start us, length us, event | category | flops | bytes accessed | tf_op | source)
XLA Modules:
  0.0 234.4 jit_solution(13156006508898969187)
XLA Ops:
  0.8 2.7 %collective-permute-start.2 = (bf16[256,1024]{1,0:T(8,128)(2,1)}, bf16[256,1024]{1,0:T(8,128)(2,1)S(1)}, u32[]{:S(2)}, u32[]{:S(2)}) collective-permute-start(bf16[256,1024]{1,0:T(8,128)(2,1)} %bitcast.31), channel_id=1, source_target_pairs={{0,16},{16,0},{1,17},{17,1},{2,18},{18,2},{3,19},{19,3},{4,20},{20... | collective-permute-start | bytes 1572872 | tf_op jit(solution)/shard_map/ppermute | solution.py:36
  6.9 13.1 %attend.2 = (bf16[1024,512]{1,0:T(8,128)(2,1)}, bf16[512,1536]{1,0:T(8,128)(2,1)}, bf16[512,512]{1,0:T(8,128)(2,1)}, bf16[512,1024]{1,0:T(8,128)(2,1)}, f32[8,512]{1,0:T(8,128)}) custom-call(s32[3]{0:T(128)} %pad_add_fusion.scalars, s32[2]{0:T(128)} %pad_add_fusion.1.facts.facts_a, bf16[256,1024]{1,0:T(8,128)(2,1)} %bitcast.32, ...), custom_call_target="tpu_custom_call" | custom-call | flops 12000000000 | bytes 8000000 | tf_op jit(solution)/shard_map/attend/pallas_call | solution.py:189
  20.9 2.0 collective-permute-done.facts.facts_b
  24.2 13.1 %attend.3 = (bf16[1024,512]{1,0:T(8,128)(2,1)}, bf16[512,1536]{1,0:T(8,128)(2,1)}, bf16[512,512]{1,0:T(8,128)(2,1)}, bf16[512,1024]{1,0:T(8,128)(2,1)}, f32[8,512]{1,0:T(8,128)}) custom-call(s32[3]{0:T(128)} %pad_add_fusion.scalars, s32[2]{0:T(128)} %copy-done.32, bf16[256,1024]{1,0:T(8,128)(2,1)} %copy-done.21, bf16[256,1024]{1,0:T(8,128)(2,1)} %copy-done.22, ...), custom_call_target="tpu_custom_call" | custom-call | flops 12000000000 | bytes 8000000 | tf_op jit(solution)/shard_map/attend/pallas_call | solution.py:189
  39.2 3.1 %collective-permute-done.6.dyao = bf16[256,1024]{1,0:T(8,128)(2,1)S(1)} collective-permute-done((bf16[256,1024]{1,0:T(8,128)(2,1)S(1)}, bf16[256,1024]{1,0:T(8,128)(2,1)S(1)}, u32[]{:S(2)}, u32[]{:S(2)}) %collective-permute-start.6) | collective-permute-done | bytes 524320 | tf_op jit(solution)/shard_map/ppermute | solution.py:36
  44.4 18.7 %own_units.1 = (bf16[1024,1024]{1,0:T(8,128)(2,1)}, bf16[512,1024]{1,0:T(8,128)(2,1)}, bf16[1024,1024]{1,0:T(8,128)(2,1)}, f32[256,1024]{1,0:T(8,128)}, bf16[256...) custom-call(s32[3]{0:T(128)} %pad_add_fusion.scalars, ...), custom_call_target="tpu_custom_call" | custom-call | flops 20000000000 | bytes 8000000 | tf_op jit(solution)/shard_map/own_units/pallas_call | solution.py:306
  64.5 19.5 %rest_units.1 = (bf16[1024,1024]{1,0:T(8,128)(2,1)}, f32[256,1024]{1,0:T(8,128)}, bf16[256,1024]{1,0:T(8,128)(2,1)}) custom-call(s32[3]{0:T(128)} %pad_add_fusion.scalars, bf16[1024,1024]{1,0:T(8,128)(2,1)} %get-tuple-element.65.h_any, bf16[256,1024]{1,0:T(8,128)(2,1)} %bitcast.40, bf16[256,1024]{1,0:T(8,128)(2,1)} %copy-done.23, ...), custom_call_target="tpu_custom_call" | custom-call | flops 20000000000 | bytes 8000000 | tf_op jit(solution)/shard_map/rest_units/pallas_call | solution.py:365
  88.0 3.3 %collective-permute-start.27 = (bf16[416,1024]{1,0:T(8,128)(2,1)S(1)}, bf16[416,1024]{1,0:T(8,128)(2,1)S(1)}, u32[]{:S(2)}, u32[]{:S(2)}) collective-permute-start(bf16[416,1024]{1,0:T(8,128)(2,1)S(1)} %add_convert_fusion.2), channel_id=1, source_target_pairs={{0,4},{2,6},{8,12},{10,14},{1,5},{3,7},{9,13},{11,15},{16,20},{18,... | collective-permute-start | bytes 2555912 | tf_op jit(solution)/shard_map/ppermute | solution.py:855
  91.3 11.2 %turn.1 = (f32[256,1024]{1,0:T(8,128)}, f32[8,1024]{1,0:T(8,128)}, bf16[1024,512]{1,0:T(8,128)(2,1)}, bf16[256,1024]{1,0:T(8,128)(2,1)}, bf16[256,1024]{1,0:T(8,128)(2,1)}, /*index=5*/bf16[256,1024]{1,0:T(8,128)(2,1)}) custom-call(s32[3]{0:T(128)} %pad_add_fusion.scalars, s32[2]{0:T(128)} %pad_add_fusion.1.facts.facts_a, s32[2]{0:T(128)} %copy-done.32, ...), custom_call_target="tpu_custom_call" | custom-call | flops 12000000000 | bytes 8000000 | tf_op jit(solution)/shard_map/turn/pallas_call | solution.py:476
  103.8 13.0 %back.1 = (bf16[512,768]{1,0:T(8,128)(2,1)}, bf16[256,1024]{1,0:T(8,128)(2,1)}, bf16[256,1024]{1,0:T(8,128)(2,1)}, bf16[160,1024]{1,0:T(8,128)(2,1)}, bf16[160,1024]{1,0:T(8,128)(2,1)}) custom-call(s32[3]{0:T(128)} %pad_add_fusion.scalars, s32[2]{0:T(128)} %pad_add_fusion.1.facts.facts_a, s32[2]{0:T(128)} %copy-done.32, ...), custom_call_target="tpu_custom_call" | custom-call | flops 14000000000 | bytes 8000000 | tf_op jit(solution)/shard_map/back/pallas_call | solution.py:543
  116.8 1.5 add_convert_fusion.5
  120.8 1.6 collective-permute-start.28
  128.6 6.7 %collective-permute-start.22 = (bf16[416,1024]{1,0:T(8,128)(2,1)}, bf16[416,1024]{1,0:T(8,128)(2,1)}, u32[]{:S(2)}, u32[]{:S(2)}) collective-permute-start(bf16[416,1024]{1,0:T(8,128)(2,1)} %pad_maximum_fusion), channel_id=1, source_target_pairs={{0,4},{2,6},{12,8},{14,10},{1,5},{3,7},{13,9},{15,11},{16,20},{18,... | collective-permute-start | bytes 2555912 | tf_op jit(solution)/shard_map/ppermute | solution.py:855
  138.7 8.6 %last.1 = (f32[256,1024]{1,0:T(8,128)}, bf16[256,1024]{1,0:T(8,128)(2,1)}) custom-call(s32[3]{0:T(128)} %pad_add_fusion.scalars, s32[2]{0:T(128)} %pad_add_fusion.1.facts.facts_a, bf16[512,1536]{1,0:T(8,128)(2,1)} %get-tuple-element.78.qkv_a.qkv_ref, f32[8,512]{1,0:T(8,128)} %get-tuple-element.79.lse_a.lse_ref, ...), custom_call_target="tpu_custom_call" | custom-call | flops 7000000000 | bytes 8000000 | tf_op jit(solution)/shard_map/last/pallas_call | solution.py:591
  147.4 2.6 %collective-permute-start.14 = (bf16[256,1024]{1,0:T(8,128)(2,1)}, bf16[256,1024]{1,0:T(8,128)(2,1)S(1)}, u32[]{:S(2)}, u32[]{:S(2)}) collective-permute-start(bf16[256,1024]{1,0:T(8,128)(2,1)} %get-tuple-element.94), channel_id=1, source_target_pairs={{0,1},{1,0},{2,3},{3,2},{4,5},{5,4},{6,7},{7,6},{8,9},{9,8},{10,11... | collective-permute-start | bytes 1572872 | tf_op jit(solution)/shard_map/ppermute | solution.py:36
  150.3 1.7 collective-permute-start.26
  152.1 2.6 %add_convert_fusion = bf16[416,1024]{1,0:T(8,128)(2,1)} fusion(bf16[416,1024]{1,0:T(8,128)(2,1)} %collective-permute-done.28, bf16[416,1024]{1,0:T(8,128)(2,1)} %add_convert_fusion.1), kind=kLoop, calls=%fused_computation | loop fusion | flops 1703936 | bytes 2555904 | tf_op jit(solution)/shard_map/convert_element_type | solution.py:703
  154.7 2.0 add_convert_fusion.11
  160.4 1.5 add_convert_fusion.7
  163.9 1.9 add_convert_fusion.14
  165.8 1.6 collective-permute-done.18
  167.7 7.6 %collective-permute-done.16 = bf16[256,1024]{1,0:T(8,128)(2,1)} collective-permute-done((bf16[256,1024]{1,0:T(8,128)(2,1)}, bf16[256,1024]{1,0:T(8,128)(2,1)}, u32[]{:S(2)}, u32[]{:S(2)}) %collective-permute-start.16) | collective-permute-done | bytes 524320 | tf_op jit(solution)/shard_map/ppermute | solution.py:855
  178.9 1.5 add_convert_fusion.3
  180.6 1.4 collective-permute-start.31
  182.4 20.7 %collective-permute-done.20 = bf16[256,1024]{1,0:T(8,128)(2,1)S(1)} collective-permute-done((bf16[256,1024]{1,0:T(8,128)(2,1)S(1)}, bf16[256,1024]{1,0:T(8,128)(2,1)S(1)}, u32[]{:S(2)}, u32[]{:S(2)}) %collective-permute-start.20) | collective-permute-done | bytes 524320 | tf_op jit(solution)/shard_map/ppermute | solution.py:855
  205.3 2.5 %collective-permute-start.9 = (bf16[256,1024]{1,0:T(8,128)(2,1)}, bf16[256,1024]{1,0:T(8,128)(2,1)}, u32[]{:S(2)}, u32[]{:S(2)}) collective-permute-start(bf16[256,1024]{1,0:T(8,128)(2,1)} %get-tuple-element.70), channel_id=1, source_target_pairs={{0,1},{1,0},{2,3},{3,2},{4,5},{5,4},{6,7},{7,6},{8,9},{9,8},{10,11... | collective-permute-start | bytes 1572872 | tf_op jit(solution)/shard_map/ppermute | solution.py:36
  210.5 3.4 %collective-permute-done.32 = f32[32,1024]{1,0:T(8,128)S(1)} collective-permute-done((f32[32,1024]{1,0:T(8,128)S(1)}, f32[32,1024]{1,0:T(8,128)S(1)}, u32[]{:S(2)}, u32[]{:S(2)}) %collective-permute-start.32) | collective-permute-done | bytes 131104 | tf_op jit(solution)/shard_map/ppermute | solution.py:36
  216.8 2.0 fusion.12
  218.7 3.5 %collective-permute-start.35 = (bf16[256,1024]{1,0:T(8,128)(2,1)}, bf16[256,1024]{1,0:T(8,128)(2,1)S(1)}, u32[]{:S(2)}, u32[]{:S(2)}) collective-permute-start(bf16[256,1024]{1,0:T(8,128)(2,1)} %fusion.13.refs_0_), channel_id=1, source_target_pairs={{0,1},{1,0},{2,3},{3,2},{4,5},{5,4},{6,7},{7,6},{8,9},{9,8},{10,11... | collective-permute-start | bytes 1572872 | tf_op jit(solution)/shard_map/ppermute | solution.py:36
  222.7 3.4 %collective-permute-start.38 = (bf16[160,1024]{1,0:T(8,128)(2,1)S(1)}, bf16[160,1024]{1,0:T(8,128)(2,1)}, u32[]{:S(2)}, u32[]{:S(2)}) collective-permute-start(bf16[160,1024]{1,0:T(8,128)(2,1)S(1)} %collective-permute-done.34.refs_3_), channel_id=1, source_target_pairs={{0,1},{1,0},{2,3},{3,2},{4,5},{5,4},{6,7},{7,6},{8,9},{9,8},{10,11... | collective-permute-start | bytes 983048 | tf_op jit(solution)/shard_map/ppermute | solution.py:36
  226.2 1.4 fusion.9
  228.7 5.5 %place.1 = f32[6158,128]{1,0:T(8,128)} custom-call(s32[32]{0:T(128)} %pad_add_fusion.2.table, bf16[256,1024]{1,0:T(8,128)(2,1)} %fusion.13.refs_0_, bf16[160,1024]{1,0:T(8,128)(2,1)} %copy-done.14, bf16[256,1024]{1,0:T(8,128)(2,1)} %collective-permute-done.33.refs_2_, bf16[160,1024]{1,0:T(8,128)(2,1)} %copy-done.29, bf16[256,1024]{1,0:T(8,128)(2,1)} %copy-done.25, ...), custom_call_target="tpu_custom_call" | custom-call | flops 4000000000 | bytes 8000000 | tf_op jit(solution)/shard_map/place/pallas_call | solution.py:816
  (166 shorter events, 46.9 us)
Async XLA Ops:
  0.6 5.4 %collective-permute-start.1 = (bf16[256,1024]{1,0:T(8,128)(2,1)}, bf16[256,1024]{1,0:T(8,128)(2,1)S(1)}, u32[]{:S(2)}, u32[]{:S(2)}) collective-permute-start(bf16[256,1024]{1,0:T(8,128)(2,1)} %bitcast.30), channel_id=1, source_target_pairs={{0,1},{1,0},{2,3},{3,2},{4,5},{5,4},{6,7},{7,6},{8,9},{9,8},{10,11... | collective-permute-start | bytes 1572872 | tf_op jit(solution)/shard_map/ppermute | solution.py:36
  0.8 19.2 %collective-permute-start.2 = (bf16[256,1024]{1,0:T(8,128)(2,1)}, bf16[256,1024]{1,0:T(8,128)(2,1)S(1)}, u32[]{:S(2)}, u32[]{:S(2)}) collective-permute-start(bf16[256,1024]{1,0:T(8,128)(2,1)} %bitcast.31), channel_id=1, source_target_pairs={{0,16},{16,0},{1,17},{17,1},{2,18},{18,2},{3,19},{19,3},{4,20},{20... | collective-permute-start | bytes 1572872 | tf_op jit(solution)/shard_map/ppermute | solution.py:36
  20.4 18.7 %collective-permute-start.4 = (bf16[512,1024]{1,0:T(8,128)(2,1)}, bf16[512,1024]{1,0:T(8,128)(2,1)S(1)}, u32[]{:S(2)}, u32[]{:S(2)}) collective-permute-start(bf16[512,1024]{1,0:T(8,128)(2,1)} %get-tuple-element.59.pa), channel_id=1, source_target_pairs={{0,1},{1,0},{2,3},{3,2},{4,5},{5,4},{6,7},{7,6},{8,9},{9,8},{10,11... | collective-permute-start | bytes 3145736 | tf_op jit(solution)/shard_map/ppermute | solution.py:36
  22.8 15.9 %collective-permute-start.7 = (bf16[256,1024]{1,0:T(8,128)(2,1)S(1)}, bf16[256,1024]{1,0:T(8,128)(2,1)}, u32[]{:S(2)}, u32[]{:S(2)}) collective-permute-start(bf16[256,1024]{1,0:T(8,128)(2,1)S(1)} %bitcast.42), channel_id=1, source_target_pairs={{0,16},{16,0},{1,17},{17,1},{2,18},{18,2},{3,19},{19,3},{4,20},{20... | collective-permute-start | bytes 1572872 | tf_op jit(solution)/shard_map/ppermute | solution.py:36
  37.3 5.4 %collective-permute-start.5 = (bf16[512,1024]{1,0:T(8,128)(2,1)}, bf16[512,1024]{1,0:T(8,128)(2,1)S(1)}, u32[]{:S(2)}, u32[]{:S(2)}) collective-permute-start(bf16[512,1024]{1,0:T(8,128)(2,1)} %get-tuple-element.62.pb), channel_id=1, source_target_pairs={{0,1},{1,0},{2,3},{3,2},{4,5},{5,4},{6,7},{7,6},{8,9},{9,8},{10,11... | collective-permute-start | bytes 3145736 | tf_op jit(solution)/shard_map/ppermute | solution.py:36
  63.1 20.9 %collective-permute-start.10 = (bf16[416,1024]{1,0:T(8,128)(2,1)}, bf16[416,1024]{1,0:T(8,128)(2,1)S(1)}, u32[]{:S(2)}, u32[]{:S(2)}) collective-permute-start(bf16[416,1024]{1,0:T(8,128)(2,1)} %get-tuple-element.72), channel_id=1, source_target_pairs={{0,2},{2,0},{4,6},{6,4},{8,10},{10,8},{12,14},{14,12},{1,3},{3,1},... | collective-permute-start | bytes 2555912 | tf_op jit(solution)/shard_map/ppermute | solution.py:36
  84.0 7.3 %collective-permute-start.11 = (bf16[1024,1024]{1,0:T(8,128)(2,1)}, bf16[1024,1024]{1,0:T(8,128)(2,1)}, u32[]{:S(2)}, u32[]{:S(2)}) collective-permute-start(bf16[1024,1024]{1,0:T(8,128)(2,1)} %get-tuple-element.73.dh_any), channel_id=1, source_target_pairs={{0,1},{1,0},{2,3},{3,2},{4,5},{5,4},{6,7},{7,6},{8,9},{9,8},{10,11... | collective-permute-start | bytes 6291464 | tf_op jit(solution)/shard_map/ppermute | solution.py:36
  86.1 37.1 %collective-permute-start.21 = (bf16[160,1024]{1,0:T(8,128)(2,1)S(1)}, bf16[160,1024]{1,0:T(8,128)(2,1)}, u32[]{:S(2)}, u32[]{:S(2)}) collective-permute-start(bf16[160,1024]{1,0:T(8,128)(2,1)S(1)} %copy-done.27), channel_id=1, source_target_pairs={{0,2},{2,0},{4,6},{6,4},{8,10},{10,8},{12,14},{14,12},{1,3},{3,1},... | collective-permute-start | bytes 983048 | tf_op jit(solution)/shard_map/ppermute | solution.py:36
  87.5 29.3 %collective-permute-start.24 = (bf16[416,1024]{1,0:T(8,128)(2,1)}, bf16[416,1024]{1,0:T(8,128)(2,1)}, u32[]{:S(2)}, u32[]{:S(2)}) collective-permute-start(bf16[416,1024]{1,0:T(8,128)(2,1)} %get-tuple-element.108), channel_id=1, source_target_pairs={{0,2},{2,0},{4,6},{6,4},{8,10},{10,8},{12,14},{14,12},{1,3},{3,1},... | collective-permute-start | bytes 2555912 | tf_op jit(solution)/shard_map/ppermute | solution.py:36
  88.0 30.3 %collective-permute-start.27 = (bf16[416,1024]{1,0:T(8,128)(2,1)S(1)}, bf16[416,1024]{1,0:T(8,128)(2,1)S(1)}, u32[]{:S(2)}, u32[]{:S(2)}) collective-permute-start(bf16[416,1024]{1,0:T(8,128)(2,1)S(1)} %add_convert_fusion.2), channel_id=1, source_target_pairs={{0,4},{2,6},{8,12},{10,14},{1,5},{3,7},{9,13},{11,15},{16,20},{18,... | collective-permute-start | bytes 2555912 | tf_op jit(solution)/shard_map/ppermute | solution.py:855
  102.5 22.7 %collective-permute-start.12 = (bf16[256,1024]{1,0:T(8,128)(2,1)}, bf16[256,1024]{1,0:T(8,128)(2,1)}, u32[]{:S(2)}, u32[]{:S(2)}) collective-permute-start(bf16[256,1024]{1,0:T(8,128)(2,1)} %get-tuple-element.90), channel_id=1, source_target_pairs={{0,2},{2,0},{4,6},{6,4},{8,10},{10,8},{12,14},{14,12},{1,3},{3,1},... | collective-permute-start | bytes 1572872 | tf_op jit(solution)/shard_map/ppermute | solution.py:36
  119.5 27.9 %collective-permute-start.25 = (bf16[416,1024]{1,0:T(8,128)(2,1)S(1)}, bf16[416,1024]{1,0:T(8,128)(2,1)S(1)}, u32[]{:S(2)}, u32[]{:S(2)}) collective-permute-start(bf16[416,1024]{1,0:T(8,128)(2,1)S(1)} %add_convert_fusion.5), channel_id=1, source_target_pairs={{0,4},{2,6},{12,8},{14,10},{1,5},{3,7},{13,9},{15,11},{16,20},{18,... | collective-permute-start | bytes 2555912 | tf_op jit(solution)/shard_map/ppermute | solution.py:855
  120.8 29.5 %collective-permute-start.28 = (bf16[416,1024]{1,0:T(8,128)(2,1)}, bf16[416,1024]{1,0:T(8,128)(2,1)}, u32[]{:S(2)}, u32[]{:S(2)}) collective-permute-start(bf16[416,1024]{1,0:T(8,128)(2,1)} %add_convert_fusion.1), channel_id=1, source_target_pairs={{4,12},{6,14},{5,13},{7,15},{20,28},{22,30},{21,29},{23,31}} | collective-permute-start | bytes 2555912 | tf_op jit(solution)/shard_map/ppermute | solution.py:855
  125.1 11.5 %collective-permute-start.13 = (bf16[160,1024]{1,0:T(8,128)(2,1)S(1)}, bf16[160,1024]{1,0:T(8,128)(2,1)S(1)}, u32[]{:S(2)}, u32[]{:S(2)}) collective-permute-start(bf16[160,1024]{1,0:T(8,128)(2,1)S(1)} %copy-done.28), channel_id=1, source_target_pairs={{0,2},{2,0},{4,6},{6,4},{8,10},{10,8},{12,14},{14,12},{1,3},{3,1},... | collective-permute-start | bytes 983048 | tf_op jit(solution)/shard_map/ppermute | solution.py:36
  128.6 31.8 %collective-permute-start.22 = (bf16[416,1024]{1,0:T(8,128)(2,1)}, bf16[416,1024]{1,0:T(8,128)(2,1)}, u32[]{:S(2)}, u32[]{:S(2)}) collective-permute-start(bf16[416,1024]{1,0:T(8,128)(2,1)} %pad_maximum_fusion), channel_id=1, source_target_pairs={{0,4},{2,6},{12,8},{14,10},{1,5},{3,7},{13,9},{15,11},{16,20},{18,... | collective-permute-start | bytes 2555912 | tf_op jit(solution)/shard_map/ppermute | solution.py:855
  135.3 19.3 %collective-permute-start.15 = (bf16[256,1024]{1,0:T(8,128)(2,1)}, bf16[256,1024]{1,0:T(8,128)(2,1)}, u32[]{:S(2)}, u32[]{:S(2)}) collective-permute-start(bf16[256,1024]{1,0:T(8,128)(2,1)} %get-tuple-element.98), channel_id=1, source_target_pairs={{0,2},{2,0},{4,6},{6,4},{8,10},{10,8},{12,14},{14,12},{1,3},{3,1},... | collective-permute-start | bytes 1572872 | tf_op jit(solution)/shard_map/ppermute | solution.py:36
  137.4 26.5 %collective-permute-start.29 = (bf16[160,1024]{1,0:T(8,128)(2,1)}, bf16[160,1024]{1,0:T(8,128)(2,1)}, u32[]{:S(2)}, u32[]{:S(2)}) collective-permute-start(bf16[160,1024]{1,0:T(8,128)(2,1)} %add_convert_fusion.16), channel_id=1, source_target_pairs={{4,0},{6,2},{12,8},{14,10},{5,1},{7,3},{13,9},{15,11},{20,16},{22,... | collective-permute-start | bytes 983048 | tf_op jit(solution)/shard_map/ppermute | solution.py:855
  147.4 10.6 %collective-permute-start.14 = (bf16[256,1024]{1,0:T(8,128)(2,1)}, bf16[256,1024]{1,0:T(8,128)(2,1)S(1)}, u32[]{:S(2)}, u32[]{:S(2)}) collective-permute-start(bf16[256,1024]{1,0:T(8,128)(2,1)} %get-tuple-element.94), channel_id=1, source_target_pairs={{0,1},{1,0},{2,3},{3,2},{4,5},{5,4},{6,7},{7,6},{8,9},{9,8},{10,11... | collective-permute-start | bytes 1572872 | tf_op jit(solution)/shard_map/ppermute | solution.py:36
  150.3 28.6 %collective-permute-start.26 = (bf16[416,1024]{1,0:T(8,128)(2,1)S(1)}, bf16[416,1024]{1,0:T(8,128)(2,1)}, u32[]{:S(2)}, u32[]{:S(2)}) collective-permute-start(bf16[416,1024]{1,0:T(8,128)(2,1)S(1)} %add_convert_fusion.4), channel_id=1, source_target_pairs={{4,8},{6,10},{5,9},{7,11},{20,24},{22,26},{21,25},{23,27}} | collective-permute-start | bytes 2555912 | tf_op jit(solution)/shard_map/ppermute | solution.py:855
  156.7 18.5 %collective-permute-start.16 = (bf16[256,1024]{1,0:T(8,128)(2,1)}, bf16[256,1024]{1,0:T(8,128)(2,1)}, u32[]{:S(2)}, u32[]{:S(2)}) collective-permute-start(bf16[256,1024]{1,0:T(8,128)(2,1)} %add_convert_fusion.11), channel_id=1, source_target_pairs={{4,0},{6,2},{12,8},{14,10},{5,1},{7,3},{13,9},{15,11},{20,16},{22,... | collective-permute-start | bytes 1572872 | tf_op jit(solution)/shard_map/ppermute | solution.py:855
  161.9 20.1 %collective-permute-start.23 = (bf16[416,1024]{1,0:T(8,128)(2,1)S(1)}, bf16[416,1024]{1,0:T(8,128)(2,1)S(1)}, u32[]{:S(2)}, u32[]{:S(2)}) collective-permute-start(bf16[416,1024]{1,0:T(8,128)(2,1)S(1)} %add_convert_fusion.7), channel_id=1, source_target_pairs={{8,4},{10,6},{9,5},{11,7},{24,20},{26,22},{25,21},{27,23}} | collective-permute-start | bytes 2555912 | tf_op jit(solution)/shard_map/ppermute | solution.py:855
  167.4 9.2 %collective-permute-start.19 = (f32[32,1024]{1,0:T(8,128)S(1)}, f32[32,1024]{1,0:T(8,128)S(1)}, u32[]{:S(2)}, u32[]{:S(2)}) collective-permute-start(f32[32,1024]{1,0:T(8,128)S(1)} %add.120), channel_id=1, source_target_pairs={{0,2},{2,0},{4,6},{6,4},{8,10},{10,8},{12,14},{14,12},{1,3},{3,1},... | collective-permute-start | bytes 393224 | tf_op jit(solution)/shard_map/ppermute | solution.py:36
  177.6 25.4 %collective-permute-start.20 = (bf16[256,1024]{1,0:T(8,128)(2,1)S(1)}, bf16[256,1024]{1,0:T(8,128)(2,1)S(1)}, u32[]{:S(2)}, u32[]{:S(2)}) collective-permute-start(bf16[256,1024]{1,0:T(8,128)(2,1)S(1)} %add_convert_fusion.10), channel_id=1, source_target_pairs={{8,0},{10,2},{9,1},{11,3},{24,16},{26,18},{25,17},{27,19}} | collective-permute-start | bytes 1572872 | tf_op jit(solution)/shard_map/ppermute | solution.py:855
  180.6 33.9 %collective-permute-start.31 = (bf16[160,1024]{1,0:T(8,128)(2,1)}, bf16[160,1024]{1,0:T(8,128)(2,1)}, u32[]{:S(2)}, u32[]{:S(2)}) collective-permute-start(bf16[160,1024]{1,0:T(8,128)(2,1)} %add_convert_fusion.14), channel_id=1, source_target_pairs={{8,0},{10,2},{9,1},{11,3},{24,16},{26,18},{25,17},{27,19}} | collective-permute-start | bytes 983048 | tf_op jit(solution)/shard_map/ppermute | solution.py:855
  204.1 11.9 %collective-permute-start.33 = (bf16[256,1024]{1,0:T(8,128)(2,1)}, bf16[256,1024]{1,0:T(8,128)(2,1)}, u32[]{:S(2)}, u32[]{:S(2)}) collective-permute-start(bf16[256,1024]{1,0:T(8,128)(2,1)} %fusion.13.refs_0_), channel_id=1, source_target_pairs={{0,16},{16,0},{1,17},{17,1},{2,18},{18,2},{3,19},{19,3},{4,20},{20... | collective-permute-start | bytes 1572872 | tf_op jit(solution)/shard_map/ppermute | solution.py:36
  205.3 11.5 %collective-permute-start.9 = (bf16[256,1024]{1,0:T(8,128)(2,1)}, bf16[256,1024]{1,0:T(8,128)(2,1)}, u32[]{:S(2)}, u32[]{:S(2)}) collective-permute-start(bf16[256,1024]{1,0:T(8,128)(2,1)} %get-tuple-element.70), channel_id=1, source_target_pairs={{0,1},{1,0},{2,3},{3,2},{4,5},{5,4},{6,7},{7,6},{8,9},{9,8},{10,11... | collective-permute-start | bytes 1572872 | tf_op jit(solution)/shard_map/ppermute | solution.py:36
  207.8 6.0 %collective-permute-start.32 = (f32[32,1024]{1,0:T(8,128)S(1)}, f32[32,1024]{1,0:T(8,128)S(1)}, u32[]{:S(2)}, u32[]{:S(2)}) collective-permute-start(f32[32,1024]{1,0:T(8,128)S(1)} %add.134), channel_id=1, source_target_pairs={{0,8},{2,10},{4,12},{6,14},{8,0},{10,2},{12,4},{14,6},{1,9},{3,11}... | collective-permute-start | bytes 393224 | tf_op jit(solution)/shard_map/ppermute | solution.py:36
  216.0 6.8 %collective-permute-start.34 = (bf16[160,1024]{1,0:T(8,128)(2,1)S(1)}, bf16[160,1024]{1,0:T(8,128)(2,1)S(1)}, u32[]{:S(2)}, u32[]{:S(2)}) collective-permute-start(bf16[160,1024]{1,0:T(8,128)(2,1)S(1)} %fusion.16.refs_1_), channel_id=1, source_target_pairs={{0,16},{16,0},{1,17},{17,1},{2,18},{18,2},{3,19},{19,3},{4,20},{20... | collective-permute-start | bytes 983048 | tf_op jit(solution)/shard_map/ppermute | solution.py:36
  218.7 8.8 %collective-permute-start.35 = (bf16[256,1024]{1,0:T(8,128)(2,1)}, bf16[256,1024]{1,0:T(8,128)(2,1)S(1)}, u32[]{:S(2)}, u32[]{:S(2)}) collective-permute-start(bf16[256,1024]{1,0:T(8,128)(2,1)} %fusion.13.refs_0_), channel_id=1, source_target_pairs={{0,1},{1,0},{2,3},{3,2},{4,5},{5,4},{6,7},{7,6},{8,9},{9,8},{10,11... | collective-permute-start | bytes 1572872 | tf_op jit(solution)/shard_map/ppermute | solution.py:36
  222.2 5.4 %collective-permute-start.37 = (bf16[256,1024]{1,0:T(8,128)(2,1)}, bf16[256,1024]{1,0:T(8,128)(2,1)S(1)}, u32[]{:S(2)}, u32[]{:S(2)}) collective-permute-start(bf16[256,1024]{1,0:T(8,128)(2,1)} %collective-permute-done.33.refs_2_), channel_id=1, source_target_pairs={{0,1},{1,0},{2,3},{3,2},{4,5},{5,4},{6,7},{7,6},{8,9},{9,8},{10,11... | collective-permute-start | bytes 1572872 | tf_op jit(solution)/shard_map/ppermute | solution.py:36
  222.2 5.4 %collective-permute-start.36 = (bf16[160,1024]{1,0:T(8,128)(2,1)S(1)}, bf16[160,1024]{1,0:T(8,128)(2,1)S(1)}, u32[]{:S(2)}, u32[]{:S(2)}) collective-permute-start(bf16[160,1024]{1,0:T(8,128)(2,1)S(1)} %fusion.16.refs_1_), channel_id=1, source_target_pairs={{0,1},{1,0},{2,3},{3,2},{4,5},{5,4},{6,7},{7,6},{8,9},{9,8},{10,11... | collective-permute-start | bytes 983048 | tf_op jit(solution)/shard_map/ppermute | solution.py:36
  222.7 4.9 %collective-permute-start.38 = (bf16[160,1024]{1,0:T(8,128)(2,1)S(1)}, bf16[160,1024]{1,0:T(8,128)(2,1)}, u32[]{:S(2)}, u32[]{:S(2)}) collective-permute-start(bf16[160,1024]{1,0:T(8,128)(2,1)S(1)} %collective-permute-done.34.refs_3_), channel_id=1, source_target_pairs={{0,1},{1,0},{2,3},{3,2},{4,5},{5,4},{6,7},{7,6},{8,9},{9,8},{10,11... | collective-permute-start | bytes 983048 | tf_op jit(solution)/shard_map/ppermute | solution.py:36
  (40 other events, 281.1 us)

commit v5 on v4

--- a/solution.py
+++ b/solution.py
@@ -688,7 +688,7 @@
                 else:
                     runs.append([low, high, stage])
             for low, high, stage in runs:
-                middle = low + (high - low) * 5 // 8 // 16 * 16
+                middle = low + (high - low) * 21 // 32 // 16 * 16
                 for first, last in [(low, middle), (middle, high)] if stage == 2 else [(low, high)]:
                     regions = [self.regions(2 * block + i, first, last) for i in range(2)]
                     stages[stage].append({"block": block, "low": first, "high": last, "regions": regions, "most": max(map(len, regions))})
@@ -926,7 +926,7 @@
                 chunk["total"] = after(chunk["total"], small_steps[-3 if i == len(chunks) - 2 else -2])
             climb(chunk)
             settle(chunk)
-    edges = [0, layout.rows * 5 // 8 // 16 * 16, layout.rows]
+    edges = [0, layout.rows * 21 // 32 // 16 * 16, layout.rows]
     quads = [[], [], [], []]
     for low, high in zip(edges, edges[1:]):
         final = jnp.zeros((high - low, width), BF16)

time: 236 us -> 235 us (level)
  no operation moved by 1% of the time
where the time goes in v5:
time: 235 us; the launch traced here: 234 us
  Pallas kernels  103 us (44%)
  starting transfers between devices  49.8 us (21%)
  waiting for transfers between devices  40.5 us (17%)
  other arithmetic  30.3 us (13%)
  local copies, waits for them, and re-layouts  8.23 us (4%)
  between operations  2.77 us (1%)
    ppermute x29, starting transfers between devices, swap(): return lax.ppermute(value, axis, [(i, i ^ distance) for i in range(count)])  29.4 us
    ppermute x10, waiting for transfers between devices, climb(): lax.ppermute(chunk['total'], 'member', tree_pairs(chunk['block'], chunk['...  27.6 us
    pallas_call x2, Pallas kernels, attend(): pl.pallas_call(attend_kernel, in_specs=[SMEM, SMEM, HBM, HBM, VMEM, VMEM,...  26.1 us
    ppermute x10, starting transfers between devices, climb(): lax.ppermute(chunk['total'], 'member', tree_pairs(chunk['block'], chunk['...  20.4 us
    pallas_call x1, Pallas kernels, rest_units(): pl.pallas_call(rest_kernel, in_specs=[SMEM] + [HBM] * 7 + [VMEM] + [HBM]...  19.5 us
    pallas_call x1, Pallas kernels, own_units(): pl.pallas_call(functools.partial(own_kernel, plan, kept), in_specs=[SMEM]...  18.8 us
    convert_element_type x14, other arithmetic, add(): return (left.astype(F32) + right.astype(F32)).astype(BF16)  17.7 us
    pallas_call x1, Pallas kernels, back(): pl.pallas_call(functools.partial(back_kernel, plan), in_specs=[SMEM] * 3...  13 us
  transfers between devices with their start and end apart: 39, of which 9 were waited for; matrix products, arithmetic and copies ran while one was open for 14% of the time, Pallas kernels for 33%

profile of v5, /device:TPU:1, one launch (start us, length us, event | category | flops | bytes accessed | tf_op | source)
XLA Modules:
  0.0 234.2 jit_solution(8138733598956360093)
XLA Ops:
  0.8 2.7 %collective-permute-start.2 = (bf16[256,1024]{1,0:T(8,128)(2,1)}, bf16[256,1024]{1,0:T(8,128)(2,1)S(1)}, u32[]{:S(2)}, u32[]{:S(2)}) collective-permute-start(bf16[256,1024]{1,0:T(8,128)(2,1)} %bitcast.31), channel_id=1, source_target_pairs={{0,16},{16,0},{1,17},{17,1},{2,18},{18,2},{3,19},{19,3},{4,20},{20... | collective-permute-start | bytes 1572872 | tf_op jit(solution)/shard_map/ppermute | solution.py:36
  6.8 13.0 %attend.2 = (bf16[1024,512]{1,0:T(8,128)(2,1)}, bf16[512,1536]{1,0:T(8,128)(2,1)}, bf16[512,512]{1,0:T(8,128)(2,1)}, bf16[512,1024]{1,0:T(8,128)(2,1)}, f32[8,512]{1,0:T(8,128)}) custom-call(s32[3]{0:T(128)} %pad_add_fusion.scalars, s32[2]{0:T(128)} %pad_add_fusion.1.facts.facts_a, bf16[256,1024]{1,0:T(8,128)(2,1)} %bitcast.32, ...), custom_call_target="tpu_custom_call" | custom-call | flops 12000000000 | bytes 8000000 | tf_op jit(solution)/shard_map/attend/pallas_call | solution.py:189
  20.7 2.0 collective-permute-done.facts.facts_b
  24.0 13.1 %attend.3 = (bf16[1024,512]{1,0:T(8,128)(2,1)}, bf16[512,1536]{1,0:T(8,128)(2,1)}, bf16[512,512]{1,0:T(8,128)(2,1)}, bf16[512,1024]{1,0:T(8,128)(2,1)}, f32[8,512]{1,0:T(8,128)}) custom-call(s32[3]{0:T(128)} %pad_add_fusion.scalars, s32[2]{0:T(128)} %copy-done.32, bf16[256,1024]{1,0:T(8,128)(2,1)} %copy-done.23, bf16[256,1024]{1,0:T(8,128)(2,1)} %copy-done.24, ...), custom_call_target="tpu_custom_call" | custom-call | flops 12000000000 | bytes 8000000 | tf_op jit(solution)/shard_map/attend/pallas_call | solution.py:189
  39.0 3.1 %collective-permute-done.6.dyao = bf16[256,1024]{1,0:T(8,128)(2,1)S(1)} collective-permute-done((bf16[256,1024]{1,0:T(8,128)(2,1)S(1)}, bf16[256,1024]{1,0:T(8,128)(2,1)S(1)}, u32[]{:S(2)}, u32[]{:S(2)}) %collective-permute-start.6) | collective-permute-done | bytes 524320 | tf_op jit(solution)/shard_map/ppermute | solution.py:36
  44.3 18.8 %own_units.1 = (bf16[1024,1024]{1,0:T(8,128)(2,1)}, bf16[512,1024]{1,0:T(8,128)(2,1)}, bf16[1024,1024]{1,0:T(8,128)(2,1)}, f32[256,1024]{1,0:T(8,128)}, bf16[256...) custom-call(s32[3]{0:T(128)} %pad_add_fusion.scalars, ...), custom_call_target="tpu_custom_call" | custom-call | flops 20000000000 | bytes 8000000 | tf_op jit(solution)/shard_map/own_units/pallas_call | solution.py:306
  64.4 19.5 %rest_units.1 = (bf16[1024,1024]{1,0:T(8,128)(2,1)}, f32[256,1024]{1,0:T(8,128)}, bf16[256,1024]{1,0:T(8,128)(2,1)}) custom-call(s32[3]{0:T(128)} %pad_add_fusion.scalars, bf16[1024,1024]{1,0:T(8,128)(2,1)} %get-tuple-element.65.h_any, bf16[256,1024]{1,0:T(8,128)(2,1)} %bitcast.40, bf16[256,1024]{1,0:T(8,128)(2,1)} %copy-done.25, ...), custom_call_target="tpu_custom_call" | custom-call | flops 20000000000 | bytes 8000000 | tf_op jit(solution)/shard_map/rest_units/pallas_call | solution.py:365
  87.9 3.3 %collective-permute-start.27 = (bf16[416,1024]{1,0:T(8,128)(2,1)S(1)}, bf16[416,1024]{1,0:T(8,128)(2,1)S(1)}, u32[]{:S(2)}, u32[]{:S(2)}) collective-permute-start(bf16[416,1024]{1,0:T(8,128)(2,1)S(1)} %add_convert_fusion.2), channel_id=1, source_target_pairs={{0,4},{2,6},{8,12},{10,14},{1,5},{3,7},{9,13},{11,15},{16,20},{18,... | collective-permute-start | bytes 2555912 | tf_op jit(solution)/shard_map/ppermute | solution.py:855
  91.1 11.2 %turn.1 = (f32[256,1024]{1,0:T(8,128)}, f32[8,1024]{1,0:T(8,128)}, bf16[1024,512]{1,0:T(8,128)(2,1)}, bf16[256,1024]{1,0:T(8,128)(2,1)}, bf16[256,1024]{1,0:T(8,128)(2,1)}, /*index=5*/bf16[256,1024]{1,0:T(8,128)(2,1)}) custom-call(s32[3]{0:T(128)} %pad_add_fusion.scalars, s32[2]{0:T(128)} %pad_add_fusion.1.facts.facts_a, s32[2]{0:T(128)} %copy-done.32, ...), custom_call_target="tpu_custom_call" | custom-call | flops 12000000000 | bytes 8000000 | tf_op jit(solution)/shard_map/turn/pallas_call | solution.py:476
  103.6 13.0 %back.1 = (bf16[512,768]{1,0:T(8,128)(2,1)}, bf16[272,1024]{1,0:T(8,128)(2,1)}, bf16[272,1024]{1,0:T(8,128)(2,1)}, bf16[144,1024]{1,0:T(8,128)(2,1)}, bf16[144,1024]{1,0:T(8,128)(2,1)}) custom-call(s32[3]{0:T(128)} %pad_add_fusion.scalars, s32[2]{0:T(128)} %pad_add_fusion.1.facts.facts_a, s32[2]{0:T(128)} %copy-done.32, ...), custom_call_target="tpu_custom_call" | custom-call | flops 14000000000 | bytes 8000000 | tf_op jit(solution)/shard_map/back/pallas_call | solution.py:543
  116.6 1.5 add_convert_fusion.5
  120.7 1.6 collective-permute-start.28
  128.5 6.7 %collective-permute-start.22 = (bf16[416,1024]{1,0:T(8,128)(2,1)}, bf16[416,1024]{1,0:T(8,128)(2,1)}, u32[]{:S(2)}, u32[]{:S(2)}) collective-permute-start(bf16[416,1024]{1,0:T(8,128)(2,1)} %pad_maximum_fusion), channel_id=1, source_target_pairs={{0,4},{2,6},{12,8},{14,10},{1,5},{3,7},{13,9},{15,11},{16,20},{18,... | collective-permute-start | bytes 2555912 | tf_op jit(solution)/shard_map/ppermute | solution.py:855
  138.5 8.6 %last.1 = (f32[256,1024]{1,0:T(8,128)}, bf16[256,1024]{1,0:T(8,128)(2,1)}) custom-call(s32[3]{0:T(128)} %pad_add_fusion.scalars, s32[2]{0:T(128)} %pad_add_fusion.1.facts.facts_a, bf16[512,1536]{1,0:T(8,128)(2,1)} %get-tuple-element.78.qkv_a.qkv_ref, f32[8,512]{1,0:T(8,128)} %get-tuple-element.79.lse_a.lse_ref, ...), custom_call_target="tpu_custom_call" | custom-call | flops 7000000000 | bytes 8000000 | tf_op jit(solution)/shard_map/last/pallas_call | solution.py:591
  147.2 2.6 %collective-permute-start.14 = (bf16[256,1024]{1,0:T(8,128)(2,1)}, bf16[256,1024]{1,0:T(8,128)(2,1)S(1)}, u32[]{:S(2)}, u32[]{:S(2)}) collective-permute-start(bf16[256,1024]{1,0:T(8,128)(2,1)} %get-tuple-element.94), channel_id=1, source_target_pairs={{0,1},{1,0},{2,3},{3,2},{4,5},{5,4},{6,7},{7,6},{8,9},{9,8},{10,11... | collective-permute-start | bytes 1572872 | tf_op jit(solution)/shard_map/ppermute | solution.py:36
  150.1 1.7 collective-permute-start.26
  151.8 2.6 %add_convert_fusion = bf16[416,1024]{1,0:T(8,128)(2,1)} fusion(bf16[416,1024]{1,0:T(8,128)(2,1)} %collective-permute-done.28, bf16[416,1024]{1,0:T(8,128)(2,1)} %add_convert_fusion.1), kind=kLoop, calls=%fused_computation | loop fusion | flops 1703936 | bytes 2555904 | tf_op jit(solution)/shard_map/convert_element_type | solution.py:703
  154.5 2.1 add_convert_fusion.10
  160.2 1.5 add_convert_fusion.7
  163.7 1.8 add_convert_fusion.15
  165.6 1.6 collective-permute-done.18
  167.5 7.5 %collective-permute-done.16 = bf16[272,1024]{1,0:T(8,128)(2,1)} collective-permute-done((bf16[272,1024]{1,0:T(8,128)(2,1)}, bf16[272,1024]{1,0:T(8,128)(2,1)}, u32[]{:S(2)}, u32[]{:S(2)}) %collective-permute-start.16) | collective-permute-done | bytes 557088 | tf_op jit(solution)/shard_map/ppermute | solution.py:855
  175.1 1.4 add_convert_fusion.9
  178.0 1.5 add_convert_fusion.3
  179.5 1.6 collective-permute-done.30
  182.7 20.1 %collective-permute-done.20 = bf16[272,1024]{1,0:T(8,128)(2,1)S(1)} collective-permute-done((bf16[272,1024]{1,0:T(8,128)(2,1)S(1)}, bf16[272,1024]{1,0:T(8,128)(2,1)S(1)}, u32[]{:S(2)}, u32[]{:S(2)}) %collective-permute-start.20) | collective-permute-done | bytes 557088 | tf_op jit(solution)/shard_map/ppermute | solution.py:855
  205.1 2.5 %collective-permute-start.9 = (bf16[256,1024]{1,0:T(8,128)(2,1)}, bf16[256,1024]{1,0:T(8,128)(2,1)}, u32[]{:S(2)}, u32[]{:S(2)}) collective-permute-start(bf16[256,1024]{1,0:T(8,128)(2,1)} %get-tuple-element.70), channel_id=1, source_target_pairs={{0,1},{1,0},{2,3},{3,2},{4,5},{5,4},{6,7},{7,6},{8,9},{9,8},{10,11... | collective-permute-start | bytes 1572872 | tf_op jit(solution)/shard_map/ppermute | solution.py:36
  210.3 3.3 %collective-permute-done.32 = f32[32,1024]{1,0:T(8,128)S(1)} collective-permute-done((f32[32,1024]{1,0:T(8,128)S(1)}, f32[32,1024]{1,0:T(8,128)S(1)}, u32[]{:S(2)}, u32[]{:S(2)}) %collective-permute-start.32) | collective-permute-done | bytes 131104 | tf_op jit(solution)/shard_map/ppermute | solution.py:36
  217.3 3.5 %collective-permute-start.37 = (bf16[272,1024]{1,0:T(8,128)(2,1)}, bf16[272,1024]{1,0:T(8,128)(2,1)S(1)}, u32[]{:S(2)}, u32[]{:S(2)}) collective-permute-start(bf16[272,1024]{1,0:T(8,128)(2,1)} %collective-permute-done.33.refs_2_), channel_id=1, source_target_pairs={{0,1},{1,0},{2,3},{3,2},{4,5},{5,4},{6,7},{7,6},{8,9},{9,8},{10,11... | collective-permute-start | bytes 1671176 | tf_op jit(solution)/shard_map/ppermute | solution.py:36
  220.7 2.0 fusion.15
  222.7 3.3 %collective-permute-start.38 = (bf16[144,1024]{1,0:T(8,128)(2,1)S(1)}, bf16[144,1024]{1,0:T(8,128)(2,1)}, u32[]{:S(2)}, u32[]{:S(2)}) collective-permute-start(bf16[144,1024]{1,0:T(8,128)(2,1)S(1)} %collective-permute-done.34.refs_3_), channel_id=1, source_target_pairs={{0,1},{1,0},{2,3},{3,2},{4,5},{5,4},{6,7},{7,6},{8,9},{9,8},{10,11... | collective-permute-start | bytes 884744 | tf_op jit(solution)/shard_map/ppermute | solution.py:36
  228.5 5.5 %place.1 = f32[6158,128]{1,0:T(8,128)} custom-call(s32[32]{0:T(128)} %pad_add_fusion.2.table, bf16[272,1024]{1,0:T(8,128)(2,1)} %fusion.12.refs_0_, bf16[144,1024]{1,0:T(8,128)(2,1)} %copy-done.15, bf16[272,1024]{1,0:T(8,128)(2,1)} %collective-permute-done.33.refs_2_, bf16[144,1024]{1,0:T(8,128)(2,1)} %copy-done.29, bf16[272,1024]{1,0:T(8,128)(2,1)} %copy-done.19, ...), custom_call_target="tpu_custom_call" | custom-call | flops 4000000000 | bytes 8000000 | tf_op jit(solution)/shard_map/place/pallas_call | solution.py:816
  (166 shorter events, 47.4 us)
Async XLA Ops:
  0.6 5.3 %collective-permute-start.1 = (bf16[256,1024]{1,0:T(8,128)(2,1)}, bf16[256,1024]{1,0:T(8,128)(2,1)S(1)}, u32[]{:S(2)}, u32[]{:S(2)}) collective-permute-start(bf16[256,1024]{1,0:T(8,128)(2,1)} %bitcast.30), channel_id=1, source_target_pairs={{0,1},{1,0},{2,3},{3,2},{4,5},{5,4},{6,7},{7,6},{8,9},{9,8},{10,11... | collective-permute-start | bytes 1572872 | tf_op jit(solution)/shard_map/ppermute | solution.py:36
  0.8 19.1 %collective-permute-start.2 = (bf16[256,1024]{1,0:T(8,128)(2,1)}, bf16[256,1024]{1,0:T(8,128)(2,1)S(1)}, u32[]{:S(2)}, u32[]{:S(2)}) collective-permute-start(bf16[256,1024]{1,0:T(8,128)(2,1)} %bitcast.31), channel_id=1, source_target_pairs={{0,16},{16,0},{1,17},{17,1},{2,18},{18,2},{3,19},{19,3},{4,20},{20... | collective-permute-start | bytes 1572872 | tf_op jit(solution)/shard_map/ppermute | solution.py:36
  20.2 18.8 %collective-permute-start.4 = (bf16[512,1024]{1,0:T(8,128)(2,1)}, bf16[512,1024]{1,0:T(8,128)(2,1)S(1)}, u32[]{:S(2)}, u32[]{:S(2)}) collective-permute-start(bf16[512,1024]{1,0:T(8,128)(2,1)} %get-tuple-element.59.pa), channel_id=1, source_target_pairs={{0,1},{1,0},{2,3},{3,2},{4,5},{5,4},{6,7},{7,6},{8,9},{9,8},{10,11... | collective-permute-start | bytes 3145736 | tf_op jit(solution)/shard_map/ppermute | solution.py:36
  22.6 15.9 %collective-permute-start.7 = (bf16[256,1024]{1,0:T(8,128)(2,1)S(1)}, bf16[256,1024]{1,0:T(8,128)(2,1)}, u32[]{:S(2)}, u32[]{:S(2)}) collective-permute-start(bf16[256,1024]{1,0:T(8,128)(2,1)S(1)} %bitcast.42), channel_id=1, source_target_pairs={{0,16},{16,0},{1,17},{17,1},{2,18},{18,2},{3,19},{19,3},{4,20},{20... | collective-permute-start | bytes 1572872 | tf_op jit(solution)/shard_map/ppermute | solution.py:36
  37.1 5.4 %collective-permute-start.5 = (bf16[512,1024]{1,0:T(8,128)(2,1)}, bf16[512,1024]{1,0:T(8,128)(2,1)S(1)}, u32[]{:S(2)}, u32[]{:S(2)}) collective-permute-start(bf16[512,1024]{1,0:T(8,128)(2,1)} %get-tuple-element.62.pb), channel_id=1, source_target_pairs={{0,1},{1,0},{2,3},{3,2},{4,5},{5,4},{6,7},{7,6},{8,9},{9,8},{10,11... | collective-permute-start | bytes 3145736 | tf_op jit(solution)/shard_map/ppermute | solution.py:36
  63.0 20.8 %collective-permute-start.10 = (bf16[416,1024]{1,0:T(8,128)(2,1)}, bf16[416,1024]{1,0:T(8,128)(2,1)S(1)}, u32[]{:S(2)}, u32[]{:S(2)}) collective-permute-start(bf16[416,1024]{1,0:T(8,128)(2,1)} %get-tuple-element.72), channel_id=1, source_target_pairs={{0,2},{2,0},{4,6},{6,4},{8,10},{10,8},{12,14},{14,12},{1,3},{3,1},... | collective-permute-start | bytes 2555912 | tf_op jit(solution)/shard_map/ppermute | solution.py:36
  83.9 7.3 %collective-permute-start.11 = (bf16[1024,1024]{1,0:T(8,128)(2,1)}, bf16[1024,1024]{1,0:T(8,128)(2,1)}, u32[]{:S(2)}, u32[]{:S(2)}) collective-permute-start(bf16[1024,1024]{1,0:T(8,128)(2,1)} %get-tuple-element.73.dh_any), channel_id=1, source_target_pairs={{0,1},{1,0},{2,3},{3,2},{4,5},{5,4},{6,7},{7,6},{8,9},{9,8},{10,11... | collective-permute-start | bytes 6291464 | tf_op jit(solution)/shard_map/ppermute | solution.py:36
  86.0 37.1 %collective-permute-start.21 = (bf16[160,1024]{1,0:T(8,128)(2,1)S(1)}, bf16[160,1024]{1,0:T(8,128)(2,1)}, u32[]{:S(2)}, u32[]{:S(2)}) collective-permute-start(bf16[160,1024]{1,0:T(8,128)(2,1)S(1)} %copy-done.27), channel_id=1, source_target_pairs={{0,2},{2,0},{4,6},{6,4},{8,10},{10,8},{12,14},{14,12},{1,3},{3,1},... | collective-permute-start | bytes 983048 | tf_op jit(solution)/shard_map/ppermute | solution.py:36
  87.3 29.3 %collective-permute-start.24 = (bf16[416,1024]{1,0:T(8,128)(2,1)}, bf16[416,1024]{1,0:T(8,128)(2,1)}, u32[]{:S(2)}, u32[]{:S(2)}) collective-permute-start(bf16[416,1024]{1,0:T(8,128)(2,1)} %get-tuple-element.108), channel_id=1, source_target_pairs={{0,2},{2,0},{4,6},{6,4},{8,10},{10,8},{12,14},{14,12},{1,3},{3,1},... | collective-permute-start | bytes 2555912 | tf_op jit(solution)/shard_map/ppermute | solution.py:36
  87.9 30.2 %collective-permute-start.27 = (bf16[416,1024]{1,0:T(8,128)(2,1)S(1)}, bf16[416,1024]{1,0:T(8,128)(2,1)S(1)}, u32[]{:S(2)}, u32[]{:S(2)}) collective-permute-start(bf16[416,1024]{1,0:T(8,128)(2,1)S(1)} %add_convert_fusion.2), channel_id=1, source_target_pairs={{0,4},{2,6},{8,12},{10,14},{1,5},{3,7},{9,13},{11,15},{16,20},{18,... | collective-permute-start | bytes 2555912 | tf_op jit(solution)/shard_map/ppermute | solution.py:855
  102.3 22.7 %collective-permute-start.12 = (bf16[256,1024]{1,0:T(8,128)(2,1)}, bf16[256,1024]{1,0:T(8,128)(2,1)}, u32[]{:S(2)}, u32[]{:S(2)}) collective-permute-start(bf16[256,1024]{1,0:T(8,128)(2,1)} %get-tuple-element.90), channel_id=1, source_target_pairs={{0,2},{2,0},{4,6},{6,4},{8,10},{10,8},{12,14},{14,12},{1,3},{3,1},... | collective-permute-start | bytes 1572872 | tf_op jit(solution)/shard_map/ppermute | solution.py:36
  119.4 27.8 %collective-permute-start.25 = (bf16[416,1024]{1,0:T(8,128)(2,1)S(1)}, bf16[416,1024]{1,0:T(8,128)(2,1)S(1)}, u32[]{:S(2)}, u32[]{:S(2)}) collective-permute-start(bf16[416,1024]{1,0:T(8,128)(2,1)S(1)} %add_convert_fusion.5), channel_id=1, source_target_pairs={{0,4},{2,6},{12,8},{14,10},{1,5},{3,7},{13,9},{15,11},{16,20},{18,... | collective-permute-start | bytes 2555912 | tf_op jit(solution)/shard_map/ppermute | solution.py:855
  120.7 29.4 %collective-permute-start.28 = (bf16[416,1024]{1,0:T(8,128)(2,1)}, bf16[416,1024]{1,0:T(8,128)(2,1)}, u32[]{:S(2)}, u32[]{:S(2)}) collective-permute-start(bf16[416,1024]{1,0:T(8,128)(2,1)} %add_convert_fusion.1), channel_id=1, source_target_pairs={{4,12},{6,14},{5,13},{7,15},{20,28},{22,30},{21,29},{23,31}} | collective-permute-start | bytes 2555912 | tf_op jit(solution)/shard_map/ppermute | solution.py:855
  125.0 11.4 %collective-permute-start.13 = (bf16[144,1024]{1,0:T(8,128)(2,1)S(1)}, bf16[144,1024]{1,0:T(8,128)(2,1)S(1)}, u32[]{:S(2)}, u32[]{:S(2)}) collective-permute-start(bf16[144,1024]{1,0:T(8,128)(2,1)S(1)} %copy-done.28), channel_id=1, source_target_pairs={{0,2},{2,0},{4,6},{6,4},{8,10},{10,8},{12,14},{14,12},{1,3},{3,1},... | collective-permute-start | bytes 884744 | tf_op jit(solution)/shard_map/ppermute | solution.py:36
  128.5 31.8 %collective-permute-start.22 = (bf16[416,1024]{1,0:T(8,128)(2,1)}, bf16[416,1024]{1,0:T(8,128)(2,1)}, u32[]{:S(2)}, u32[]{:S(2)}) collective-permute-start(bf16[416,1024]{1,0:T(8,128)(2,1)} %pad_maximum_fusion), channel_id=1, source_target_pairs={{0,4},{2,6},{12,8},{14,10},{1,5},{3,7},{13,9},{15,11},{16,20},{18,... | collective-permute-start | bytes 2555912 | tf_op jit(solution)/shard_map/ppermute | solution.py:855
  135.2 19.3 %collective-permute-start.15 = (bf16[272,1024]{1,0:T(8,128)(2,1)}, bf16[272,1024]{1,0:T(8,128)(2,1)}, u32[]{:S(2)}, u32[]{:S(2)}) collective-permute-start(bf16[272,1024]{1,0:T(8,128)(2,1)} %get-tuple-element.98), channel_id=1, source_target_pairs={{0,2},{2,0},{4,6},{6,4},{8,10},{10,8},{12,14},{14,12},{1,3},{3,1},... | collective-permute-start | bytes 1671176 | tf_op jit(solution)/shard_map/ppermute | solution.py:36
  137.2 26.5 %collective-permute-start.29 = (bf16[144,1024]{1,0:T(8,128)(2,1)}, bf16[144,1024]{1,0:T(8,128)(2,1)}, u32[]{:S(2)}, u32[]{:S(2)}) collective-permute-start(bf16[144,1024]{1,0:T(8,128)(2,1)} %add_convert_fusion.16), channel_id=1, source_target_pairs={{4,0},{6,2},{12,8},{14,10},{5,1},{7,3},{13,9},{15,11},{20,16},{22,... | collective-permute-start | bytes 884744 | tf_op jit(solution)/shard_map/ppermute | solution.py:855
  147.2 10.7 %collective-permute-start.14 = (bf16[256,1024]{1,0:T(8,128)(2,1)}, bf16[256,1024]{1,0:T(8,128)(2,1)S(1)}, u32[]{:S(2)}, u32[]{:S(2)}) collective-permute-start(bf16[256,1024]{1,0:T(8,128)(2,1)} %get-tuple-element.94), channel_id=1, source_target_pairs={{0,1},{1,0},{2,3},{3,2},{4,5},{5,4},{6,7},{7,6},{8,9},{9,8},{10,11... | collective-permute-start | bytes 1572872 | tf_op jit(solution)/shard_map/ppermute | solution.py:36
  150.1 27.8 %collective-permute-start.26 = (bf16[416,1024]{1,0:T(8,128)(2,1)S(1)}, bf16[416,1024]{1,0:T(8,128)(2,1)}, u32[]{:S(2)}, u32[]{:S(2)}) collective-permute-start(bf16[416,1024]{1,0:T(8,128)(2,1)S(1)} %add_convert_fusion.4), channel_id=1, source_target_pairs={{4,8},{6,10},{5,9},{7,11},{20,24},{22,26},{21,25},{23,27}} | collective-permute-start | bytes 2555912 | tf_op jit(solution)/shard_map/ppermute | solution.py:855
  156.6 18.5 %collective-permute-start.16 = (bf16[272,1024]{1,0:T(8,128)(2,1)}, bf16[272,1024]{1,0:T(8,128)(2,1)}, u32[]{:S(2)}, u32[]{:S(2)}) collective-permute-start(bf16[272,1024]{1,0:T(8,128)(2,1)} %add_convert_fusion.10), channel_id=1, source_target_pairs={{4,0},{6,2},{12,8},{14,10},{5,1},{7,3},{13,9},{15,11},{20,16},{22,... | collective-permute-start | bytes 1671176 | tf_op jit(solution)/shard_map/ppermute | solution.py:855
  161.7 20.7 %collective-permute-start.23 = (bf16[416,1024]{1,0:T(8,128)(2,1)S(1)}, bf16[416,1024]{1,0:T(8,128)(2,1)S(1)}, u32[]{:S(2)}, u32[]{:S(2)}) collective-permute-start(bf16[416,1024]{1,0:T(8,128)(2,1)S(1)} %add_convert_fusion.7), channel_id=1, source_target_pairs={{8,4},{10,6},{9,5},{11,7},{24,20},{26,22},{25,21},{27,23}} | collective-permute-start | bytes 2555912 | tf_op jit(solution)/shard_map/ppermute | solution.py:855
  162.5 4.8 %collective-permute-start.18 = (f32[32,1024]{1,0:T(8,128)S(1)}, f32[32,1024]{1,0:T(8,128)S(1)}, u32[]{:S(2)}, u32[]{:S(2)}) collective-permute-start(f32[32,1024]{1,0:T(8,128)S(1)} %pad_add_fusion.3), channel_id=1, source_target_pairs={{0,16},{16,0},{1,17},{17,1},{2,18},{18,2},{3,19},{19,3},{4,20},{20... | collective-permute-start | bytes 393224 | tf_op jit(solution)/shard_map/ppermute | solution.py:36
  167.2 9.3 %collective-permute-start.19 = (f32[32,1024]{1,0:T(8,128)S(1)}, f32[32,1024]{1,0:T(8,128)S(1)}, u32[]{:S(2)}, u32[]{:S(2)}) collective-permute-start(f32[32,1024]{1,0:T(8,128)S(1)} %add.120), channel_id=1, source_target_pairs={{0,2},{2,0},{4,6},{6,4},{8,10},{10,8},{12,14},{14,12},{1,3},{3,1},... | collective-permute-start | bytes 393224 | tf_op jit(solution)/shard_map/ppermute | solution.py:36
  176.7 26.1 %collective-permute-start.20 = (bf16[272,1024]{1,0:T(8,128)(2,1)S(1)}, bf16[272,1024]{1,0:T(8,128)(2,1)S(1)}, u32[]{:S(2)}, u32[]{:S(2)}) collective-permute-start(bf16[272,1024]{1,0:T(8,128)(2,1)S(1)} %add_convert_fusion.9), channel_id=1, source_target_pairs={{8,0},{10,2},{9,1},{11,3},{24,16},{26,18},{25,17},{27,19}} | collective-permute-start | bytes 1671176 | tf_op jit(solution)/shard_map/ppermute | solution.py:855
  181.1 33.2 %collective-permute-start.31 = (bf16[144,1024]{1,0:T(8,128)(2,1)}, bf16[144,1024]{1,0:T(8,128)(2,1)}, u32[]{:S(2)}, u32[]{:S(2)}) collective-permute-start(bf16[144,1024]{1,0:T(8,128)(2,1)} %add_convert_fusion.15), channel_id=1, source_target_pairs={{8,0},{10,2},{9,1},{11,3},{24,16},{26,18},{25,17},{27,19}} | collective-permute-start | bytes 884744 | tf_op jit(solution)/shard_map/ppermute | solution.py:855
  203.9 12.7 %collective-permute-start.33 = (bf16[272,1024]{1,0:T(8,128)(2,1)}, bf16[272,1024]{1,0:T(8,128)(2,1)}, u32[]{:S(2)}, u32[]{:S(2)}) collective-permute-start(bf16[272,1024]{1,0:T(8,128)(2,1)} %fusion.12.refs_0_), channel_id=1, source_target_pairs={{0,16},{16,0},{1,17},{17,1},{2,18},{18,2},{3,19},{19,3},{4,20},{20... | collective-permute-start | bytes 1671176 | tf_op jit(solution)/shard_map/ppermute | solution.py:36
  205.1 15.6 %collective-permute-start.9 = (bf16[256,1024]{1,0:T(8,128)(2,1)}, bf16[256,1024]{1,0:T(8,128)(2,1)}, u32[]{:S(2)}, u32[]{:S(2)}) collective-permute-start(bf16[256,1024]{1,0:T(8,128)(2,1)} %get-tuple-element.70), channel_id=1, source_target_pairs={{0,1},{1,0},{2,3},{3,2},{4,5},{5,4},{6,7},{7,6},{8,9},{9,8},{10,11... | collective-permute-start | bytes 1572872 | tf_op jit(solution)/shard_map/ppermute | solution.py:36
  207.6 6.0 %collective-permute-start.32 = (f32[32,1024]{1,0:T(8,128)S(1)}, f32[32,1024]{1,0:T(8,128)S(1)}, u32[]{:S(2)}, u32[]{:S(2)}) collective-permute-start(f32[32,1024]{1,0:T(8,128)S(1)} %add.134), channel_id=1, source_target_pairs={{0,8},{2,10},{4,12},{6,14},{8,0},{10,2},{12,4},{14,6},{1,9},{3,11}... | collective-permute-start | bytes 393224 | tf_op jit(solution)/shard_map/ppermute | solution.py:36
  215.7 11.7 %collective-permute-start.35 = (bf16[272,1024]{1,0:T(8,128)(2,1)}, bf16[272,1024]{1,0:T(8,128)(2,1)S(1)}, u32[]{:S(2)}, u32[]{:S(2)}) collective-permute-start(bf16[272,1024]{1,0:T(8,128)(2,1)} %fusion.12.refs_0_), channel_id=1, source_target_pairs={{0,1},{1,0},{2,3},{3,2},{4,5},{5,4},{6,7},{7,6},{8,9},{9,8},{10,11... | collective-permute-start | bytes 1671176 | tf_op jit(solution)/shard_map/ppermute | solution.py:36
  216.6 6.2 %collective-permute-start.34 = (bf16[144,1024]{1,0:T(8,128)(2,1)S(1)}, bf16[144,1024]{1,0:T(8,128)(2,1)S(1)}, u32[]{:S(2)}, u32[]{:S(2)}) collective-permute-start(bf16[144,1024]{1,0:T(8,128)(2,1)S(1)} %fusion.16.refs_1_), channel_id=1, source_target_pairs={{0,16},{16,0},{1,17},{17,1},{2,18},{18,2},{3,19},{19,3},{4,20},{20... | collective-permute-start | bytes 884744 | tf_op jit(solution)/shard_map/ppermute | solution.py:36
  217.3 10.2 %collective-permute-start.37 = (bf16[272,1024]{1,0:T(8,128)(2,1)}, bf16[272,1024]{1,0:T(8,128)(2,1)S(1)}, u32[]{:S(2)}, u32[]{:S(2)}) collective-permute-start(bf16[272,1024]{1,0:T(8,128)(2,1)} %collective-permute-done.33.refs_2_), channel_id=1, source_target_pairs={{0,1},{1,0},{2,3},{3,2},{4,5},{5,4},{6,7},{7,6},{8,9},{9,8},{10,11... | collective-permute-start | bytes 1671176 | tf_op jit(solution)/shard_map/ppermute | solution.py:36
  222.7 4.7 %collective-permute-start.38 = (bf16[144,1024]{1,0:T(8,128)(2,1)S(1)}, bf16[144,1024]{1,0:T(8,128)(2,1)}, u32[]{:S(2)}, u32[]{:S(2)}) collective-permute-start(bf16[144,1024]{1,0:T(8,128)(2,1)S(1)} %collective-permute-done.34.refs_3_), channel_id=1, source_target_pairs={{0,1},{1,0},{2,3},{3,2},{4,5},{5,4},{6,7},{7,6},{8,9},{9,8},{10,11... | collective-permute-start | bytes 884744 | tf_op jit(solution)/shard_map/ppermute | solution.py:36
  (40 other events, 286.8 us)
